TPU v7x, 32 devices: a whole 2x2x4 slice. The times are simulated.
32 devices in a mesh: groups: 2 (over x), dp: 4 (over y, core), tensor: 4 (over z).
Axes of the slice: x: 2, y: 2, z: 4, core: 2. Of those that a mesh axis runs over, the one named last changes fastest.
Arguments:
- input_rows: bfloat16 [8192, 8192], P(('groups', 'dp'), 'tensor'), parts along dimension 0, may hold values from -6 to 6
- key_value_weight: bfloat16 [8192, 2, 1024], P(None, None, 'tensor'), may hold values from -0.0625 to 0.0625
- adapter_down_weight: bfloat16 [64, 8192, 128], P('dp', 'tensor'), may hold values from -0.0625 to 0.0625
- adapter_up_weight: bfloat16 [64, 2, 64, 1024], P('dp', None, None, 'tensor'), may hold values from -0.75 to 0.75
- tile_page_index: int32 [64], P('groups'), parts along dimension 0, may hold values from 0 to 63, as said below
- tile_live_rows: int32 [64], P(('groups', 'dp')), parts along dimension 0, may hold values from 1 to 128, as said below
Outputs:
- kv_out: bfloat16 [8192, 2, 1024], P(('groups', 'dp'), None, 'tensor'), parts along dimension 0
There are 2 independent parts, one for each index of `groups`. A program takes and returns all parts, laid end to end along the dimension named above; an argument that names none is the same for every part. Nothing has to cross between parts.
Inputs may be any that keep to these rules, and one draw needn't show every extreme that they name: `tile_page_index`: page p belongs to index p // 16 of dp. Among the tiles of one index of dp, at most 4 name pages of one owner, and one owner is named by exactly 4 tiles of every index of dp. `tile_live_rows`: every index of dp has a tile with 128 live rows.
All inputs are finite; a program needn't handle non-finite values.
Results may differ from a plain program's by a relative error of at most 0.0042.
Values may be sent and summed in bfloat16 or wider, within the bound.
No kernel may reach another device: no remote copies, remote signals or barrier semaphores. Data moves between devices by JAX's collectives and lax.ppermute only.
A program may use at most 192 MiB of HBM per device.

v0:
```python
import jax
import jax.numpy as jnp
from jax import lax
from jax.sharding import PartitionSpec as P


def on_device(
    input_rows,
    key_value_weight,
    adapter_down_weight,
    adapter_up_weight,
    tile_page_index,
    tile_live_rows,
):
    data_rank_count = lax.axis_size("dp")
    own_index = lax.axis_index("dp")
    tiles_here = tile_live_rows.shape[0]
    local_pages = adapter_down_weight.shape[0]
    page_capacity = max(2, (2 * tiles_here + data_rank_count - 1) // data_rank_count)
    row_count = input_rows.shape[0]
    tile_rows = row_count // tiles_here
    local_features = input_rows.shape[1]
    column_width = key_value_weight.shape[2]
    adapter_columns = adapter_down_weight.shape[2]
    adapter_rank_size = adapter_columns // 2
    page_table = tile_page_index.reshape(data_rank_count, tiles_here)
    owners = page_table // local_pages
    slot_ids = page_table % local_pages
    is_mine = owners == own_index
    slot_order = jnp.cumsum(is_mine.astype(jnp.int32), axis=1) - 1
    slot_range = jnp.arange(page_capacity, dtype=jnp.int32)
    chosen = is_mine[:, None, :] & (slot_order[:, None, :] == slot_range[None, :, None])
    outgoing_slot = jnp.sum(jnp.where(chosen, slot_ids[:, None, :], 0), axis=2)
    outgoing_down = adapter_down_weight[outgoing_slot]
    outgoing_up = adapter_up_weight[outgoing_slot]
    incoming_down, incoming_up = (
        lax.all_to_all(outgoing_down, "dp", split_axis=0, concat_axis=0, tiled=True),
        lax.all_to_all(outgoing_up, "dp", split_axis=0, concat_axis=0, tiled=True),
    )
    own_owners = lax.dynamic_index_in_dim(owners, own_index, 0, keepdims=False)
    tile_range = jnp.arange(tiles_here, dtype=jnp.int32)
    same_owner = own_owners[:, None] == own_owners[None, :]
    earlier = tile_range[None, :] < tile_range[:, None]
    own_order = jnp.sum((same_owner & earlier).astype(jnp.int32), axis=1)
    arrival_order = own_owners * page_capacity + own_order
    received_down_maps = incoming_down.reshape(
        data_rank_count * page_capacity, local_features, adapter_columns
    )[arrival_order]
    received_up_maps = incoming_up.reshape(
        data_rank_count * page_capacity, 2, adapter_rank_size, column_width
    )[arrival_order]
    weight_flat = key_value_weight.reshape(key_value_weight.shape[0], 2 * column_width)
    tiled = input_rows.reshape(tiles_here, tile_rows, local_features)
    partial_value = jnp.einsum(
        "trd,tdc->trc", tiled, received_down_maps, preferred_element_type=jnp.float32
    )
    shrink_part = lax.psum(partial_value, "tensor")
    base_part = jnp.dot(
        lax.all_gather(input_rows, "tensor", axis=1, tiled=True),
        weight_flat,
        preferred_element_type=jnp.float32,
    )
    reduced_projection = shrink_part.astype(jnp.bfloat16)
    key_part = jnp.einsum(
        "trk,tkc->trc",
        reduced_projection[..., :adapter_rank_size],
        received_up_maps[:, 0],
        preferred_element_type=jnp.float32,
    )
    value_part = jnp.einsum(
        "trk,tkc->trc",
        reduced_projection[..., adapter_rank_size:],
        received_up_maps[:, 1],
        preferred_element_type=jnp.float32,
    )
    expand = jnp.stack([key_part, value_part], axis=2).reshape(row_count, 2, column_width)
    live_mask = (jnp.arange(tile_rows, dtype=jnp.int32)[None, :] < tile_live_rows[:, None]).reshape(
        row_count
    )
    summed = base_part.reshape(row_count, 2, column_width) + expand
    return jnp.where(live_mask[:, None, None], summed, jnp.zeros_like(summed)).astype(jnp.bfloat16)


def solution(mesh):
    return jax.shard_map(
        on_device,
        mesh=mesh,
        in_specs=(
            P(("groups", "dp"), "tensor"),
            P(None, None, "tensor"),
            P("dp", "tensor", None),
            P("dp", None, None, "tensor"),
            P("groups"),
            P(("groups", "dp")),
        ),
        out_specs=P(("groups", "dp"), None, "tensor"),
        check_vma=False,
    )
```

profile of v0, /device:TPU:3, one launch (start us, length us, event | category | flops | bytes accessed | tf_op | source)
XLA Modules:
  0.0 340.4 jit_solution(4979147903798385848)
XLA Ops:
  6.5 0.7 all-gather.2.cloned.1.call-update
  7.3 0.7 reshape.167
  8.0 0.2 reduce_window_sum.11
  8.2 0.1 select_reduce_fusion
  8.4 0.1 reshape.173
  8.5 1.6 gather_fusion.2
  10.1 4.2 %all-to-all-start.1 = ((bf16[4,4,2,64,256]{4,3,2,1,0:T(8,128)(2,1)}), bf16[4,4,2,64,256]{4,3,2,1,0:T(8,128)(2,1)S(1)}, u32[]{:S(2)}, u32[]{:S(2)}) async-start(bf16[4,4,2,64,256]{4,3,2,1,0:T(8,128)(2,1)} %bitcast.13), calls=%async_computation.1 | async-start | bytes 2097152 | tf_op jit(solution)/shard_map/all_to_all | solution.py:38
  14.2 9.0 %gather_fusion = bf16[16,2048,128]{2,1,0:T(8,128)(2,1)} fusion(bf16[16,2048,128]{2,1,0:T(8,128)(2,1)} %param.8, s32[1024]{0:T(1024)S(1)} %pad_clamp_fusion.1), kind=kCustom, calls=%fused_computation | custom fusion | bytes 16777280 | tf_op jit(solution)/shard_map/gather | solution.py:34
  23.2 4.7 %all-to-all-done.1 = bf16[4,4,2,64,256]{4,3,2,1,0:T(8,128)(2,1)S(1)} async-done(((bf16[4,4,2,64,256]{4,3,2,1,0:T(8,128)(2,1)}), bf16[4,4,2,64,256]{4,3,2,1,0:T(8,128)(2,1)S(1)}, u32[]{:S(2)}, u32[]{:S(2)}) %all-to-all-start.1) | async-done | bytes 1048608 | tf_op jit(solution)/shard_map/all_to_all | solution.py:38
  27.9 6.5 %all-to-all-start = ((bf16[4,4,2048,128]{3,2,1,0:T(8,128)(2,1)}), bf16[4,4,2048,128]{3,2,1,0:T(8,128)(2,1)}, u32[]{:S(2)}, u32[]{:S(2)}) async-start(bf16[4,4,2048,128]{3,2,1,0:T(8,128)(2,1)} %bitcast.48), calls=%async_computation | async-start | bytes 16777216 | tf_op jit(solution)/shard_map/all_to_all | solution.py:37
  34.4 8.0 %copy.22 = bf16[1024,8,2,256]{3,1,2,0:T(8,128)(2,1)} copy(bf16[1024,8,2,256]{3,2,1,0:T(2,128)(2,1)} %bitcast.51) | data formatting | bytes 16777216
  42.4 11.4 %copy.14 = bf16[512,8192]{1,0:T(8,128)(2,1)} copy(bf16[512,8192]{0,1:T(8,128)(2,1)} %bitcast.49) | data formatting | bytes 16777216 | tf_op jit(solution)/shard_map/dot_general | solution.py:58
  53.9 0.2 convert_reduce_fusion
  54.1 0.1 fusion.11
  54.2 0.6 gather_fusion.3
  54.7 72.0 %all-to-all-done = bf16[4,4,2048,128]{3,2,1,0:T(8,128)(2,1)} async-done(((bf16[4,4,2048,128]{3,2,1,0:T(8,128)(2,1)}), bf16[4,4,2048,128]{3,2,1,0:T(8,128)(2,1)}, u32[]{:S(2)}, u32[]{:S(2)}) %all-to-all-start) | async-done | bytes 8388640 | tf_op jit(solution)/shard_map/all_to_all | solution.py:37
  126.8 6.6 %gather_fusion.1 = bf16[8,2048,128]{2,1,0:T(8,128)(2,1)} fusion(bf16[16,2048,128]{2,1,0:T(8,128)(2,1)} %bitcast.6, s32[1024]{0:T(1024)S(1)} %pad_clamp_fusion), kind=kCustom, calls=%fused_computation.1 | custom fusion | bytes 8388640 | tf_op jit(solution)/shard_map/gather | solution.py:46
  133.3 4.9 %convolution_bitcast_fusion = f32[8,128,128]{1,2,0:T(8,128)S(1)} fusion(bf16[8,2048,128]{2,1,0:T(8,128)(2,1)} %gather_fusion.1, bf16[8,128,2048]{2,1,0:T(8,128)(2,1)} %bitcast.50), kind=kOutput, calls=%fused_computation.9 | convolution fusion | flops 536870912 | bytes 8912896 | tf_op jit(solution)/shard_map/trd,tdc->trc/dot_general | solution.py:54
  138.2 64.4 %all-reduce.1 = bf16[8,128,128]{1,2,0:T(8,128)(2,1)S(1)} all-reduce(f32[8,128,128]{1,2,0:T(8,128)S(1)} %convolution_bitcast_fusion), channel_id=1, replica_groups=mesh['groups'=2,'dp'=4,'tensor'=4] {'tensor'}, use_global_device_ids=true, to_apply=%region_3.4 | all-reduce | flops 131072 | bytes 786432 | tf_op jit(solution)/shard_map/psum | solution.py:57
  202.6 0.3 fusion.7
  202.9 1.3 fusion.6
  204.2 109.7 %all-gather.2.cloned.1.call-done = bf16[1024,8192]{1,0:T(8,128)(2,1)} async-done(((bf16[1024,2048]{1,0:T(8,128)(2,1)}), bf16[1024,8192]{1,0:T(8,128)(2,1)}) %all-gather.2.cloned.1.call-update) | async-done | bytes 16777232 | tf_op jit(solution)/shard_map/all_gather | solution.py:59
  314.0 17.6 %fusion.3 = bf16[1024,2,256]{2,0,1:T(8,128)(2,1)S(1)} fusion(f32[1024,1,256]{2,0,1:T(8,128)} %bitcast.55, f32[1024,1,256]{2,0,1:T(8,128)S(1)} %bitcast.54, bf16[2,256,8192]{2,1,0:T(8,128)(2,1)} %bitcast.52, bf16[1024,8192]{1,0:T(8,128)(2,1)} %all-gather.2.cloned.1.call-done, pred[1024]{0:T(1024)(128)(4,1)S(1)} %fusion.11), kind=kOutput, calls=%fused_computation.8 | convolution fusion | flops 8592031744 | bytes 28312576 | tf_op jit(solution)/shard_map/dot_general | solution.py:58
  331.5 2.0 copy.18
  (14 shorter events, 0.1 us)
Async XLA Ops:
  6.5 1.9 copy-start
  6.5 307.4 %all-gather.2.cloned.1.call-start = ((), (), s32[]{:S(2)}) async-start(), calls=%async_computation.2 | async-start | bytes 20971520 | tf_op jit(solution)/shard_map/all_gather | solution.py:59
  10.1 17.9 %all-to-all-start.1 = ((bf16[4,4,2,64,256]{4,3,2,1,0:T(8,128)(2,1)}), bf16[4,4,2,64,256]{4,3,2,1,0:T(8,128)(2,1)S(1)}, u32[]{:S(2)}, u32[]{:S(2)}) async-start(bf16[4,4,2,64,256]{4,3,2,1,0:T(8,128)(2,1)} %bitcast.13), calls=%async_computation.1 | async-start | bytes 2097152 | tf_op jit(solution)/shard_map/all_to_all | solution.py:38
  27.9 98.8 %all-to-all-start = ((bf16[4,4,2048,128]{3,2,1,0:T(8,128)(2,1)}), bf16[4,4,2048,128]{3,2,1,0:T(8,128)(2,1)}, u32[]{:S(2)}, u32[]{:S(2)}) async-start(bf16[4,4,2048,128]{3,2,1,0:T(8,128)(2,1)} %bitcast.48), calls=%async_computation | async-start | bytes 16777216 | tf_op jit(solution)/shard_map/all_to_all | solution.py:37
  42.4 11.7 %copy-start.2 = (s32[8]{0:T(128)S(1)}, s32[8]{0:T(128)}, u32[]{:S(2)}) copy-start(s32[8]{0:T(128)} %param.11) | copy-start | bytes 100
  313.9 19.6 %copy-start.1 = (bf16[16,2,64,256]{3,2,1,0:T(8,128)(2,1)S(1)}, bf16[16,2,64,256]{3,2,1,0:T(8,128)(2,1)}, u32[]{:S(2)}) copy-start(bf16[16,2,64,256]{3,2,1,0:T(8,128)(2,1)} %param.9) | copy-start | bytes 3145732
Sparse Core Ops, SparseCore 0:
  8.9 304.9 all-gather.1
where the time goes:
time: 342 us; the launch traced here: 340 us
  waiting for transfers between devices  187 us (55%)
  blocking collectives  64.4 us (19%)
  local copies, waits for them, and re-layouts  40.1 us (12%)
  matrix products  24.1 us (7%)
  between operations  13.5 us (4%)
  starting transfers between devices  10.7 us (3%)
    all_gather x1, waiting for transfers between devices, on_device(): lax.all_gather(input_rows, 'tensor', axis=1, tiled=True)  110 us
    all_to_all x1, waiting for transfers between devices, on_device(): lax.all_to_all(outgoing_down, 'dp', split_axis=0, concat_axis=0, tiled=True)  72 us
    psum x1, blocking collectives, on_device(): shrink_part = lax.psum(partial_value, 'tensor')  64.4 us
    dot_general x1, matrix products, on_device(): jnp.dot(lax.all_gather(input_rows, 'tensor', axis=1, tiled=True), weight_...  17.6 us
    dot_general x1, local copies, waits for them, and re-layouts, on_device(): jnp.dot(lax.all_gather(input_rows, 'tensor', axis=1, tiled=True), weight_...  11.4 us
    gather x1, local copies, waits for them, and re-layouts, on_device(): outgoing_down = adapter_down_weight[outgoing_slot]  9 us
    unnamed x7, local copies, waits for them, and re-layouts  8.02 us
  transfers between devices with their start and end apart: 3, of which 3 were waited for; matrix products, arithmetic and copies ran while one was open for 13% of the time, Pallas kernels for 0%

commit v1 on v0

v1 whole, which is shorter than its diff:
```python
import functools

import jax
import jax.numpy as jnp
from jax import lax
from jax.experimental import pallas as pl
from jax.experimental.pallas import tpu as pltpu
from jax.sharding import PartitionSpec as P


def flip(x, axis, size, mask):
    return lax.ppermute(x, axis, [(i, i ^ mask) for i in range(size)])


def bits(size, first=1):
    out = []
    while first < size:
        out.append(first)
        first *= 2
    return out


def shrink_kernel(kind, own_at, mate_at, near_at, far_at, x, own, mate, near, far, out):
    t = pl.program_id(0)
    for which, pages in enumerate((own, mate, near, far)):

        @pl.when(kind[t] == which)
        def _(pages=pages):
            out[...] = jnp.dot(
                x[...], pages[0], preferred_element_type=jnp.float32
            ).astype(out.dtype)


def tile_shrink(kind, places, rows, pools, tiles):
    tile_rows = rows.shape[0] // tiles
    features = rows.shape[1]
    columns = pools[0].shape[2]
    held = []
    for which in range(4):
        used = kind == which
        last = lax.cummax(jnp.where(used, jnp.arange(tiles, dtype=jnp.int32), 0))
        held.append(jnp.where(used, places, 0)[last])

    def pool_spec(which):
        return pl.BlockSpec((1, features, columns), lambda t, *s: (s[1 + which][t], 0, 0))

    return pl.pallas_call(
        shrink_kernel,
        out_shape=jax.ShapeDtypeStruct((rows.shape[0], columns), jnp.bfloat16),
        grid_spec=pltpu.PrefetchScalarGridSpec(
            num_scalar_prefetch=5,
            grid=(tiles,),
            in_specs=[pl.BlockSpec((tile_rows, features), lambda t, *s: (t, 0))]
            + [pool_spec(which) for which in range(4)],
            out_specs=pl.BlockSpec((tile_rows, columns), lambda t, *s: (t, 0)),
        ),
        compiler_params=pltpu.CompilerParams(vmem_limit_bytes=32 << 20),
    )(kind, *held, rows, *pools)


def on_device(
    input_rows,
    key_value_weight,
    adapter_down_weight,
    adapter_up_weight,
    tile_page_index,
    tile_live_rows,
):
    groups = lax.axis_size("groups")
    ranks = lax.axis_size("dp")
    shares = lax.axis_size("tensor")
    group = lax.axis_index("groups")
    rank = lax.axis_index("dp")
    share = lax.axis_index("tensor")
    chips = ranks // 2
    chip, core = rank // 2, rank % 2
    tiles = tile_live_rows.shape[0]
    local_pages = adapter_down_weight.shape[0]
    chip_pages = 2 * local_pages
    capacity = max(2, (2 * tiles + ranks - 1) // ranks)
    slots = 2 * capacity
    rows, features = input_rows.shape
    tile_rows = rows // tiles
    column_width = key_value_weight.shape[2]
    columns = 2 * column_width
    half = adapter_down_weight.shape[2] // 2

    table = tile_page_index.reshape(chips, 2 * tiles)
    page_range = jnp.arange(ranks * local_pages, dtype=jnp.int32)
    need = jnp.any(table[:, :, None] == page_range[None, None, :], axis=1)
    need = need.reshape(chips, chips, chip_pages)
    position = jnp.cumsum(need.astype(jnp.int32), axis=2) - 1
    chip_range = jnp.arange(chip_pages, dtype=jnp.int32)
    slot_range = jnp.arange(2 * slots, dtype=jnp.int32)
    near_down, near_up, far_down, far_up = [], [], [], []
    for offset in range(1, chips):
        wanted = need[chip ^ offset, chip]
        place = position[chip ^ offset, chip]
        listed = jnp.sum(
            jnp.where(wanted[None, :] & (place[None, :] == slot_range[:, None]), chip_range[None, :], 0),
            axis=1,
        ).reshape(2, slots)
        here = listed[core]
        there = listed[1 - core]
        mine = (here // local_pages) == core
        down = adapter_down_weight[here % local_pages]
        up = adapter_up_weight[here % local_pages]
        other_down = flip(adapter_down_weight[there % local_pages], "dp", ranks, 1)
        other_up = flip(adapter_up_weight[there % local_pages], "dp", ranks, 1)
        down = jnp.where(mine[:, None, None], down, other_down)
        up = jnp.where(mine[:, None, None, None], up, other_up)
        down = flip(down, "dp", ranks, 2 * offset)
        up = flip(up, "dp", ranks, 2 * offset)
        near_down.append(down)
        near_up.append(up)
        far_down.append(flip(down, "dp", ranks, 1))
        far_up.append(flip(up, "dp", ranks, 1))
    near_down, far_down = jnp.concatenate(near_down), jnp.concatenate(far_down)
    near_up, far_up = jnp.concatenate(near_up), jnp.concatenate(far_up)

    rank_table = tile_page_index.reshape(ranks, tiles)
    mate_pages = rank_table[rank ^ 1]
    asked = (mate_pages // local_pages) == rank
    order = jnp.cumsum(asked.astype(jnp.int32)) - 1
    outgoing = jnp.sum(
        jnp.where(
            asked[None, :] & (order[None, :] == jnp.arange(capacity, dtype=jnp.int32)[:, None]),
            (mate_pages % local_pages)[None, :],
            0,
        ),
        axis=1,
    )
    mate_down = flip(adapter_down_weight[outgoing], "dp", ranks, 1)
    mate_up = flip(adapter_up_weight[outgoing], "dp", ranks, 1)

    pages = rank_table[rank]
    owner = pages // local_pages
    from_mate = owner == (rank ^ 1)
    mate_order = jnp.cumsum(from_mate.astype(jnp.int32)) - 1
    owner_chip = owner // 2
    slot = position[chip, owner_chip, pages % chip_pages]
    sender = slot // slots
    cross_at = ((owner_chip ^ chip) - 1) * slots + slot % slots
    kind = jnp.where(
        owner == rank, 0, jnp.where(from_mate, 1, jnp.where(sender == core, 2, 3))
    ).astype(jnp.int32)
    places = jnp.where(
        owner == rank, pages % local_pages, jnp.where(from_mate, mate_order, cross_at)
    ).astype(jnp.int32)

    plane = groups * ranks
    spot = group * ranks + rank
    part = features // plane
    masks = [0]
    steps = [("dp", ranks, m, m) for m in bits(ranks, 2)]
    steps += [("groups", groups, m, m * ranks) for m in bits(groups)]
    steps += [("dp", ranks, 1, 1)]
    for _, _, _, m in steps:
        masks = masks + [m ^ other for other in masks]
    weights = {}
    for k in range(1, shares):
        start = (share ^ k) * features + spot * part
        piece = lax.dynamic_slice_in_dim(key_value_weight, start, part, 0).reshape(part, columns)
        weights[k] = flip(piece, "tensor", shares, k)
    for k in range(1, shares):
        for axis, size, m, _ in steps:
            weights[k] = jnp.concatenate([weights[k], flip(weights[k], axis, size, m)])
    own_weight = lax.dynamic_slice_in_dim(key_value_weight, share * features, features, 0)
    own_weight = own_weight.reshape(features, columns)
    turned = jnp.concatenate(
        [lax.dynamic_slice_in_dim(input_rows, (spot ^ m) * part, part, 1) for m in masks], axis=1
    )

    chunks = 2
    chunk_rows = rows // chunks
    totals = []
    for i in range(chunks):
        cut = lax.slice_in_dim(turned, i * chunk_rows, (i + 1) * chunk_rows, axis=0)
        straight = lax.slice_in_dim(input_rows, i * chunk_rows, (i + 1) * chunk_rows, axis=0)
        sums = {
            k: jnp.dot(cut, weights[k], preferred_element_type=jnp.float32) for k in range(1, shares)
        }
        sums[0] = jnp.dot(straight, own_weight, preferred_element_type=jnp.float32)
        for m in bits(shares):
            leaving = [k for k in sums if k & m]
            arrived = {k: flip(sums.pop(k).astype(jnp.bfloat16), "tensor", shares, m) for k in leaving}
            for k, value in arrived.items():
                sums[k ^ m] = sums[k ^ m] + value.astype(jnp.float32)
        totals.append(sums[0])
    base = jnp.concatenate(totals)

    shrink = tile_shrink(
        kind, places, input_rows, (adapter_down_weight, mate_down, near_down, far_down), tiles
    )
    shrink_sum = shrink.astype(jnp.float32)
    for m in bits(shares):
        sent = shrink_sum.astype(jnp.bfloat16)
        shrink_sum = shrink_sum + flip(sent, "tensor", shares, m).astype(jnp.float32)
    reduced = shrink_sum.astype(jnp.bfloat16).reshape(tiles, tile_rows, 2 * half)
    sizes = (local_pages, capacity, near_up.shape[0], far_up.shape[0])
    firsts = jnp.array([sum(sizes[:i]) for i in range(4)], jnp.int32)
    up_pool = jnp.concatenate([adapter_up_weight, mate_up, near_up, far_up])
    tile_up = up_pool[firsts[kind] + places]
    expand = [
        jnp.einsum(
            "trk,tkc->trc",
            reduced[..., which * half : (which + 1) * half],
            tile_up[:, which],
            preferred_element_type=jnp.float32,
        )
        for which in range(2)
    ]
    expand = jnp.stack(expand, axis=2).reshape(rows, 2, column_width)
    live = (jnp.arange(tile_rows, dtype=jnp.int32)[None, :] < tile_live_rows[:, None]).reshape(rows)
    summed = base.reshape(rows, 2, column_width) + expand
    return jnp.where(live[:, None, None], summed, jnp.zeros_like(summed)).astype(jnp.bfloat16)


def solution(mesh):
    return jax.shard_map(
        on_device,
        mesh=mesh,
        in_specs=(
            P(("groups", "dp"), "tensor"),
            P(None, None, "tensor"),
            P("dp", "tensor", None),
            P("dp", None, None, "tensor"),
            P("groups"),
            P(("groups", "dp")),
        ),
        out_specs=P(("groups", "dp"), None, "tensor"),
        check_vma=False,
    )
```

time: 342 us -> 288 us (0.84)
  blocking collectives: 64.4 us -> 0 us
  waiting for transfers between devices: 187 us -> 149 us
  other arithmetic: 0.65 us -> 25.5 us
  local copies, waits for them, and re-layouts: 40.1 us -> 59.9 us
  starting transfers between devices: 10.7 us -> 26.9 us
  between operations: 13.5 us -> 0.66 us
  matrix products: 24.1 us -> 15.9 us
  Pallas kernels: 0 us -> 7.02 us
    ppermute x0 -> x28, waiting for transfers between devices: none -> 149 us  [flip(): return lax.ppermute(x, axis, [(i, i ^ mask) for i in range(size)])]
    all_gather x1 -> x0, waiting for transfers between devices: 110 us -> none  [on_device(): lax.all_gather(input_rows, 'tensor', axis=1, tiled=True)]
    all_to_all x2 -> x0, waiting for transfers between devices: 76.7 us -> none  [the longest x1 72 us: on_device(): lax.all_to_all(outgoing_down, 'dp', split_axis=0, concat_axis=0, tiled=True)]
    psum x1 -> x0, blocking collectives: 64.4 us -> none  [on_device(): shrink_part = lax.psum(partial_value, 'tensor')]
    ppermute x0 -> x28, starting transfers between devices: none -> 26.9 us  [flip(): return lax.ppermute(x, axis, [(i, i ^ mask) for i in range(size)])]
    dot_general x1 -> x0, local copies, waits for them, and re-layouts: 11.4 us -> none  [on_device(): jnp.dot(lax.all_gather(input_rows, 'tensor', axis=1, tiled=True), weight_...]
    all_to_all x2 -> x0, starting transfers between devices: 10.7 us -> none  [the longest x1 6.5 us: on_device(): lax.all_to_all(outgoing_down, 'dp', split_axis=0, concat_axis=0, tiled=True)]
    concatenate x0 -> x9, other arithmetic: none -> 10.4 us  [the longest x6 7.16 us: on_device(): weights[k] = jnp.concatenate([weights[k], flip(weights[k], axis, size, m)])]
  transfers between devices with their start and end apart: 3 -> 28, of which waited for: 3 -> 8; matrix products, arithmetic and copies ran while one was open for 13% -> 28% of each run, Pallas kernels for 0% -> 2%
where the time goes in v1:
time: 288 us; the launch traced here: 285 us
  waiting for transfers between devices  149 us (52%)
  local copies, waits for them, and re-layouts  59.9 us (21%)
  starting transfers between devices  26.9 us (9%)
  other arithmetic  25.5 us (9%)
  matrix products  15.9 us (6%)
  Pallas kernels  7.02 us (2%)
    ppermute x28, waiting for transfers between devices, flip(): return lax.ppermute(x, axis, [(i, i ^ mask) for i in range(size)])  149 us
    ppermute x28, starting transfers between devices, flip(): return lax.ppermute(x, axis, [(i, i ^ mask) for i in range(size)])  26.9 us
    unnamed x58, local copies, waits for them, and re-layouts  13.5 us
    dot_general x6, matrix products, on_device(): jnp.dot(cut, weights[k], preferred_element_type=jnp.float32)  9.84 us
    concatenate x6, other arithmetic, on_device(): weights[k] = jnp.concatenate([weights[k], flip(weights[k], axis, size, m)])  7.16 us
    pallas_call x1, Pallas kernels, tile_shrink(): pl.pallas_call(shrink_kernel, out_shape=jax.ShapeDtypeStruct((rows.shape[...  7.02 us
    gather x1, local copies, waits for them, and re-layouts, on_device(): other_down = flip(adapter_down_weight[there % local_pages], 'dp', ranks, 1)  6.49 us
    gather x1, local copies, waits for them, and re-layouts, on_device(): down = adapter_down_weight[here % local_pages]  6.46 us
  transfers between devices with their start and end apart: 28, of which 8 were waited for; matrix products, arithmetic and copies ran while one was open for 28% of the time, Pallas kernels for 2%

profile of v1, /device:TPU:3, one launch (start us, length us, event | category | flops | bytes accessed | tf_op | source)
XLA Modules:
  0.0 285.2 jit_solution(8913962558744730910)
XLA Ops:
  3.1 6.5 %gather_fusion.7 = bf16[8,2048,128]{2,1,0:T(8,128)(2,1)} fusion(bf16[16,2048,128]{2,1,0:T(8,128)(2,1)} %own.1, s32[1024]{0:T(1024)S(1)} %get-tuple-element.33), kind=kCustom, calls=%fused_computation.7 | custom fusion | bytes 8388640 | tf_op jit(solution)/shard_map/gather | solution.py:108
  12.7 2.3 collective-permute-start.5
  20.6 6.5 %gather_fusion.6 = bf16[8,2048,128]{2,1,0:T(8,128)(2,1)} fusion(bf16[16,2048,128]{2,1,0:T(8,128)(2,1)} %own.1, s32[1024]{0:T(1024)S(1)} %pad_clamp_fusion.3), kind=kCustom, calls=%fused_computation.6 | custom fusion | bytes 8388640 | tf_op jit(solution)/shard_map/gather | solution.py:106
  27.9 3.6 %constant_dynamic-slice_fusion.9 = bf16[2048,2,256]{2,1,0:T(2,128)(2,1)S(1)} fusion(bf16[8192,2,256]{2,1,0:T(2,128)(2,1)} %param.8, s32[]{:T(128)S(6)} %select_n.530), kind=kLoop, calls=%fused_computation.97 | loop fusion | bytes 4194308 | tf_op jit(solution)/shard_map/dynamic_slice | solution.py:168
  31.5 4.8 %broadcast_select_fusion = bf16[8,2048,128]{2,1,0:T(8,128)(2,1)} fusion(bf16[8,2048,128]{2,1,0:T(8,128)(2,1)S(1)} %copy-done.3, bf16[8,2048,128]{2,1,0:T(8,128)(2,1)} %collective-permute-done.19, pred[8]{0:T(512)(128)(4,1)S(1)} %fusion.82), kind=kLoop, calls=%fused_computation.13 | loop fusion | flops 2097152 | bytes 12582920 | tf_op jit(solution)/shard_map/jit(_where)/select_n | solution.py:110
  46.9 2.3 fusion.21
  49.2 2.2 fusion.18
  53.3 5.5 %gather_fusion.5 = bf16[4,2048,128]{2,1,0:T(8,128)(2,1)} fusion(bf16[16,2048,128]{2,1,0:T(8,128)(2,1)} %own.1, s32[1024]{0:T(1024)S(1)} %pad_clamp_fusion.4), kind=kCustom, calls=%fused_computation.5 | custom fusion | bytes 4194320 | tf_op jit(solution)/shard_map/gather | solution.py:133
  67.0 67.3 %collective-permute-done.10 = bf16[256,512]{1,0:T(8,128)(2,1)S(1)} collective-permute-done((bf16[256,512]{1,0:T(8,128)(2,1)}, bf16[256,512]{1,0:T(8,128)(2,1)S(1)}, u32[]{:S(2)}, u32[]{:S(2)}) %collective-permute-start.10) | collective-permute-done | bytes 262176 | tf_op jit(solution)/shard_map/ppermute | solution.py:12
  135.7 9.9 %collective-permute-done.1 = bf16[256,512]{1,0:T(8,128)(2,1)S(1)} collective-permute-done((bf16[256,512]{1,0:T(8,128)(2,1)}, bf16[256,512]{1,0:T(8,128)(2,1)S(1)}, u32[]{:S(2)}, u32[]{:S(2)}) %collective-permute-start.1) | collective-permute-done | bytes 262176 | tf_op jit(solution)/shard_map/ppermute | solution.py:12
  154.5 6.0 %collective-permute-done.26 = bf16[8,2,64,256]{3,2,1,0:T(8,128)(2,1)S(1)} collective-permute-done((bf16[8,2,64,256]{3,2,1,0:T(8,128)(2,1)S(1)}, bf16[8,2,64,256]{3,2,1,0:T(8,128)(2,1)S(1)}, u32[]{:S(2)}, u32[]{:S(2)}) %collective-permute-start.26) | collective-permute-done | bytes 524320 | tf_op jit(solution)/shard_map/ppermute | solution.py:12
  164.6 6.0 %collective-permute-done.7 = bf16[512,512]{1,0:T(8,128)(2,1)S(1)} collective-permute-done((bf16[512,512]{1,0:T(8,128)(2,1)S(1)}, bf16[512,512]{1,0:T(8,128)(2,1)S(1)}, u32[]{:S(2)}, u32[]{:S(2)}) %collective-permute-start.7) | collective-permute-done | bytes 524320 | tf_op jit(solution)/shard_map/ppermute | solution.py:12
  175.7 2.2 gather_fusion.12
  178.0 2.5 constant_dynamic-update-slice_fusion.8
  180.4 3.6 %fusion.39 = bf16[512,512]{1,0:T(8,128)(2,1)S(1)} fusion(bf16[2048,512]{1,0:T(8,128)(2,1)} %constant_dynamic-update-slice_fusion.8, bf16[1024,2048]{1,0:T(8,128)(2,1)} %dynamic-slice_dynamic-update-slice_fusion), kind=kOutput, calls=%fused_computation.42 | convolution fusion | flops 1074003968 | bytes 4718592 | tf_op jit(solution)/shard_map/dot_general | solution.py:181
  192.4 4.9 %collective-permute-done.16 = bf16[512,512]{1,0:T(8,128)(2,1)S(1)} collective-permute-done((bf16[512,512]{1,0:T(8,128)(2,1)S(1)}, bf16[512,512]{1,0:T(8,128)(2,1)S(1)}, u32[]{:S(2)}, u32[]{:S(2)}) %collective-permute-start.16) | collective-permute-done | bytes 524320 | tf_op jit(solution)/shard_map/ppermute | solution.py:12
  198.5 2.5 collective-permute-start.17
  202.3 28.7 %collective-permute-done.13 = bf16[512,512]{1,0:T(8,128)(2,1)S(1)} collective-permute-done((bf16[512,512]{1,0:T(8,128)(2,1)S(1)}, bf16[512,512]{1,0:T(8,128)(2,1)S(1)}, u32[]{:S(2)}, u32[]{:S(2)}) %collective-permute-start.13) | collective-permute-done | bytes 524320 | tf_op jit(solution)/shard_map/ppermute | solution.py:12
  232.3 2.9 %collective-permute-start.14 = (bf16[512,512]{1,0:T(8,128)(2,1)S(1)}, bf16[512,512]{1,0:T(8,128)(2,1)S(1)}, u32[]{:S(2)}, u32[]{:S(2)}) collective-permute-start(bf16[512,512]{1,0:T(8,128)(2,1)S(1)} %fusion.45), channel_id=1, source_target_pairs={{0,2},{1,3},{2,0},{3,1},{4,6},{5,7},{6,4},{7,5},{8,10},{9,11},{10,... | collective-permute-start | bytes 1572872 | tf_op jit(solution)/shard_map/ppermute | solution.py:12
  235.1 7.0 %shard_map.73 = bf16[1024,128]{1,0:T(8,128)(2,1)S(1)} custom-call(s32[8]{0:T(128)S(1)} %get-tuple-element.9.kind, s32[8]{0:T(128)S(1)} %gather_fusion.1, s32[8]{0:T(128)S(1)} %gather_fusion.2, s32[8]{0:T(128)S(1)} %gather_fusion.3, s32[8]{0:T(128)S(1)} %gather_fusion.4, bf16[1024,2048]{1,0:T(8,128)(2,1)S(1)} %copy-done.1, bf16[16,2048,128]{2,1,0:T(8,128)(2,1)} %own.1, ...), custom_call_target="tpu_custom_call" | custom-call | tf_op jit(solution)/shard_map/pallas_call | solution.py:47
  242.5 17.5 %collective-permute-done.22 = bf16[1024,128]{1,0:T(8,128)(2,1)S(1)} collective-permute-done((bf16[1024,128]{1,0:T(8,128)(2,1)S(1)}, bf16[1024,128]{1,0:T(8,128)(2,1)S(1)}, u32[]{:S(2)}, u32[]{:S(2)}) %collective-permute-start.22) | collective-permute-done | bytes 262176 | tf_op jit(solution)/shard_map/ppermute | solution.py:12
  263.5 2.6 reshape.861
  266.1 8.8 %collective-permute-done.23 = bf16[1024,128]{1,0:T(8,128)(2,1)} collective-permute-done((bf16[1024,128]{1,0:T(8,128)(2,1)S(1)}, bf16[1024,128]{1,0:T(8,128)(2,1)}, u32[]{:S(2)}, u32[]{:S(2)}) %collective-permute-start.23) | collective-permute-done | bytes 262176 | tf_op jit(solution)/shard_map/ppermute | solution.py:12
  279.8 5.5 %fusion.1 = bf16[1024,2,256]{2,1,0:T(2,128)(2,1)} fusion(f32[1024,2,256]{2,1,0:T(2,128)S(1)} %reshape.861, f32[1024,1,256]{2,1,0:T(1,128)S(1)} %copy.23, f32[1024,1,256]{2,1,0:T(1,128)S(1)} %copy.22, pred[1024]{0:T(1024)(128)(4,1)S(1)} %fusion.55), kind=kLoop, calls=%fused_computation.18 | loop fusion | flops 2097152 | bytes 5243904 | tf_op jit(solution)/shard_map/convert_element_type | solution.py:216
  (182 shorter events, 72.9 us)
Async XLA Ops:
  9.6 21.9 %collective-permute-start.19 = (bf16[8,2048,128]{2,1,0:T(8,128)(2,1)}, bf16[8,2048,128]{2,1,0:T(8,128)(2,1)}, u32[]{:S(2)}, u32[]{:S(2)}) collective-permute-start(bf16[8,2048,128]{2,1,0:T(8,128)(2,1)} %gather_fusion.7), channel_id=1, source_target_pairs={{0,4},{4,0},{8,12},{12,8},{1,5},{5,1},{9,13},{13,9},{2,6},{6,2},{1... | collective-permute-start | bytes 12582920 | tf_op jit(solution)/shard_map/ppermute | solution.py:12
  12.7 50.9 %collective-permute-start.5 = (bf16[256,512]{1,0:T(8,128)(2,1)}, bf16[256,512]{1,0:T(8,128)(2,1)S(1)}, u32[]{:S(2)}, u32[]{:S(2)}) collective-permute-start(bf16[256,512]{1,0:T(8,128)(2,1)} %bitcast.42), channel_id=1, source_target_pairs={{0,2},{1,3},{2,0},{3,1},{4,6},{5,7},{6,4},{7,5},{8,10},{9,11},{10,... | collective-permute-start | bytes 786440 | tf_op jit(solution)/shard_map/ppermute | solution.py:12
  15.7 47.6 %collective-permute-start.9 = (bf16[256,512]{1,0:T(8,128)(2,1)}, bf16[256,512]{1,0:T(8,128)(2,1)}, u32[]{:S(2)}, u32[]{:S(2)}) collective-permute-start(bf16[256,512]{1,0:T(8,128)(2,1)} %bitcast.44), channel_id=1, source_target_pairs={{0,3},{1,2},{2,1},{3,0},{4,7},{5,6},{6,5},{7,4},{8,11},{9,10},{10,... | collective-permute-start | bytes 786440 | tf_op jit(solution)/shard_map/ppermute | solution.py:12
  17.5 47.3 %collective-permute-start = (bf16[256,512]{1,0:T(8,128)(2,1)}, bf16[256,512]{1,0:T(8,128)(2,1)}, u32[]{:S(2)}, u32[]{:S(2)}) collective-permute-start(bf16[256,512]{1,0:T(8,128)(2,1)} %bitcast.40), channel_id=1, source_target_pairs={{0,1},{1,0},{2,3},{3,2},{4,5},{5,4},{6,7},{7,6},{8,9},{9,8},{10,11... | collective-permute-start | bytes 786440 | tf_op jit(solution)/shard_map/ppermute | solution.py:12
  19.1 127.8 %collective-permute-start.25 = (bf16[8,2,64,256]{3,2,1,0:T(8,128)(2,1)}, bf16[8,2,64,256]{3,2,1,0:T(8,128)(2,1)}, u32[]{:S(2)}, u32[]{:S(2)}) collective-permute-start(bf16[8,2,64,256]{3,2,1,0:T(8,128)(2,1)} %gather_fusion.10), channel_id=1, source_target_pairs={{0,4},{4,0},{8,12},{12,8},{1,5},{5,1},{9,13},{13,9},{2,6},{6,2},{1... | collective-permute-start | bytes 1572872 | tf_op jit(solution)/shard_map/ppermute | solution.py:12
  36.3 114.4 %collective-permute-start.20 = (bf16[8,2048,128]{2,1,0:T(8,128)(2,1)}, bf16[8,2048,128]{2,1,0:T(8,128)(2,1)}, u32[]{:S(2)}, u32[]{:S(2)}) collective-permute-start(bf16[8,2048,128]{2,1,0:T(8,128)(2,1)} %broadcast_select_fusion), channel_id=1, source_target_pairs={{0,8},{4,12},{8,0},{12,4},{1,9},{5,13},{9,1},{13,5},{2,10},{6,14},... | collective-permute-start | bytes 12582920 | tf_op jit(solution)/shard_map/ppermute | solution.py:12
  63.3 71.1 %collective-permute-start.10 = (bf16[256,512]{1,0:T(8,128)(2,1)}, bf16[256,512]{1,0:T(8,128)(2,1)S(1)}, u32[]{:S(2)}, u32[]{:S(2)}) collective-permute-start(bf16[256,512]{1,0:T(8,128)(2,1)} %collective-permute-done.9), channel_id=1, source_target_pairs={{0,8},{4,12},{8,0},{12,4},{1,9},{5,13},{9,1},{13,5},{2,10},{6,14},... | collective-permute-start | bytes 786440 | tf_op jit(solution)/shard_map/ppermute | solution.py:12
  63.5 85.8 %collective-permute-start.6 = (bf16[256,512]{1,0:T(8,128)(2,1)S(1)}, bf16[256,512]{1,0:T(8,128)(2,1)S(1)}, u32[]{:S(2)}, u32[]{:S(2)}) collective-permute-start(bf16[256,512]{1,0:T(8,128)(2,1)S(1)} %collective-permute-done.5), channel_id=1, source_target_pairs={{0,8},{4,12},{8,0},{12,4},{1,9},{5,13},{9,1},{13,5},{2,10},{6,14},... | collective-permute-start | bytes 786440 | tf_op jit(solution)/shard_map/ppermute | solution.py:12
  64.9 80.7 %collective-permute-start.1 = (bf16[256,512]{1,0:T(8,128)(2,1)}, bf16[256,512]{1,0:T(8,128)(2,1)S(1)}, u32[]{:S(2)}, u32[]{:S(2)}) collective-permute-start(bf16[256,512]{1,0:T(8,128)(2,1)} %collective-permute-done), channel_id=1, source_target_pairs={{0,8},{4,12},{8,0},{12,4},{1,9},{5,13},{9,1},{13,5},{2,10},{6,14},... | collective-permute-start | bytes 786440 | tf_op jit(solution)/shard_map/ppermute | solution.py:12
  135.3 17.0 %collective-permute-start.11 = (bf16[512,512]{1,0:T(8,128)(2,1)S(1)}, bf16[512,512]{1,0:T(8,128)(2,1)S(1)}, u32[]{:S(2)}, u32[]{:S(2)}) collective-permute-start(bf16[512,512]{1,0:T(8,128)(2,1)S(1)} %pad_maximum_fusion.7), channel_id=1, source_target_pairs={{0,16},{16,0},{1,17},{17,1},{2,18},{18,2},{3,19},{19,3},{4,20},{20... | collective-permute-start | bytes 1572872 | tf_op jit(solution)/shard_map/ppermute | solution.py:12
  146.6 15.9 %collective-permute-start.2 = (bf16[512,512]{1,0:T(8,128)(2,1)S(1)}, bf16[512,512]{1,0:T(8,128)(2,1)S(1)}, u32[]{:S(2)}, u32[]{:S(2)}) collective-permute-start(bf16[512,512]{1,0:T(8,128)(2,1)S(1)} %pad_maximum_fusion.5), channel_id=1, source_target_pairs={{0,16},{16,0},{1,17},{17,1},{2,18},{18,2},{3,19},{19,3},{4,20},{20... | collective-permute-start | bytes 1572872 | tf_op jit(solution)/shard_map/ppermute | solution.py:12
  149.4 21.1 %collective-permute-start.7 = (bf16[512,512]{1,0:T(8,128)(2,1)S(1)}, bf16[512,512]{1,0:T(8,128)(2,1)S(1)}, u32[]{:S(2)}, u32[]{:S(2)}) collective-permute-start(bf16[512,512]{1,0:T(8,128)(2,1)S(1)} %pad_maximum_fusion.6), channel_id=1, source_target_pairs={{0,16},{16,0},{1,17},{17,1},{2,18},{18,2},{3,19},{19,3},{4,20},{20... | collective-permute-start | bytes 1572872 | tf_op jit(solution)/shard_map/ppermute | solution.py:12
  150.7 84.4 %collective-permute-start.21 = (bf16[8,2048,128]{2,1,0:T(8,128)(2,1)}, bf16[8,2048,128]{2,1,0:T(8,128)(2,1)}, u32[]{:S(2)}, u32[]{:S(2)}) collective-permute-start(bf16[8,2048,128]{2,1,0:T(8,128)(2,1)} %collective-permute-done.20.near), channel_id=1, source_target_pairs={{0,4},{4,0},{8,12},{12,8},{1,5},{5,1},{9,13},{13,9},{2,6},{6,2},{1... | collective-permute-start | bytes 12582920 | tf_op jit(solution)/shard_map/ppermute | solution.py:12
  154.4 23.6 %collective-permute-start.12 = (bf16[1024,512]{1,0:T(8,128)(2,1)}, bf16[1024,512]{1,0:T(8,128)(2,1)}, u32[]{:S(2)}, u32[]{:S(2)}) collective-permute-start(bf16[1024,512]{1,0:T(8,128)(2,1)} %pad_maximum_fusion.4), channel_id=1, source_target_pairs={{0,4},{4,0},{8,12},{12,8},{1,5},{5,1},{9,13},{13,9},{2,6},{6,2},{1... | collective-permute-start | bytes 3145736 | tf_op jit(solution)/shard_map/ppermute | solution.py:12
  164.5 21.2 %collective-permute-start.3 = (bf16[1024,512]{1,0:T(8,128)(2,1)}, bf16[1024,512]{1,0:T(8,128)(2,1)}, u32[]{:S(2)}, u32[]{:S(2)}) collective-permute-start(bf16[1024,512]{1,0:T(8,128)(2,1)} %pad_maximum_fusion.2), channel_id=1, source_target_pairs={{0,4},{4,0},{8,12},{12,8},{1,5},{5,1},{9,13},{13,9},{2,6},{6,2},{1... | collective-permute-start | bytes 3145736 | tf_op jit(solution)/shard_map/ppermute | solution.py:12
  173.4 58.9 %collective-permute-start.18 = (bf16[4,2048,128]{2,1,0:T(8,128)(2,1)}, bf16[4,2048,128]{2,1,0:T(8,128)(2,1)S(1)}, u32[]{:S(2)}, u32[]{:S(2)}) collective-permute-start(bf16[4,2048,128]{2,1,0:T(8,128)(2,1)} %gather_fusion.5), channel_id=1, source_target_pairs={{0,4},{4,0},{8,12},{12,8},{1,5},{5,1},{9,13},{13,9},{2,6},{6,2},{1... | collective-permute-start | bytes 6291464 | tf_op jit(solution)/shard_map/ppermute | solution.py:12
  173.9 15.9 %collective-permute-start.8 = (bf16[1024,512]{1,0:T(8,128)(2,1)}, bf16[1024,512]{1,0:T(8,128)(2,1)}, u32[]{:S(2)}, u32[]{:S(2)}) collective-permute-start(bf16[1024,512]{1,0:T(8,128)(2,1)} %pad_maximum_fusion.3), channel_id=1, source_target_pairs={{0,4},{4,0},{8,12},{12,8},{1,5},{5,1},{9,13},{13,9},{2,6},{6,2},{1... | collective-permute-start | bytes 3145736 | tf_op jit(solution)/shard_map/ppermute | solution.py:12
  188.2 54.0 %collective-permute-start.15 = (bf16[512,512]{1,0:T(8,128)(2,1)S(1)}, bf16[512,512]{1,0:T(8,128)(2,1)S(1)}, u32[]{:S(2)}, u32[]{:S(2)}) collective-permute-start(bf16[512,512]{1,0:T(8,128)(2,1)S(1)} %fusion.36), channel_id=1, source_target_pairs={{0,1},{1,0},{2,3},{3,2},{4,5},{5,4},{6,7},{7,6},{8,9},{9,8},{10,11... | collective-permute-start | bytes 1572872 | tf_op jit(solution)/shard_map/ppermute | solution.py:12
  189.8 41.2 %collective-permute-start.13 = (bf16[512,512]{1,0:T(8,128)(2,1)S(1)}, bf16[512,512]{1,0:T(8,128)(2,1)S(1)}, u32[]{:S(2)}, u32[]{:S(2)}) collective-permute-start(bf16[512,512]{1,0:T(8,128)(2,1)S(1)} %fusion.33), channel_id=1, source_target_pairs={{0,1},{1,0},{2,3},{3,2},{4,5},{5,4},{6,7},{7,6},{8,9},{9,8},{10,11... | collective-permute-start | bytes 1572872 | tf_op jit(solution)/shard_map/ppermute | solution.py:12
  198.5 43.7 %collective-permute-start.17 = (bf16[512,512]{1,0:T(8,128)(2,1)S(1)}, bf16[512,512]{1,0:T(8,128)(2,1)S(1)}, u32[]{:S(2)}, u32[]{:S(2)}) collective-permute-start(bf16[512,512]{1,0:T(8,128)(2,1)S(1)} %fusion.42), channel_id=1, source_target_pairs={{0,2},{1,3},{2,0},{3,1},{4,6},{5,7},{6,4},{7,5},{8,10},{9,11},{10,... | collective-permute-start | bytes 1572872 | tf_op jit(solution)/shard_map/ppermute | solution.py:12
  231.0 30.8 %collective-permute-start.4 = (bf16[512,512]{1,0:T(8,128)(2,1)S(1)}, bf16[512,512]{1,0:T(8,128)(2,1)S(1)}, u32[]{:S(2)}, u32[]{:S(2)}) collective-permute-start(bf16[512,512]{1,0:T(8,128)(2,1)S(1)} %fusion.30), channel_id=1, source_target_pairs={{0,1},{1,0},{2,3},{3,2},{4,5},{5,4},{6,7},{7,6},{8,9},{9,8},{10,11... | collective-permute-start | bytes 1572872 | tf_op jit(solution)/shard_map/ppermute | solution.py:12
  232.3 29.5 %collective-permute-start.14 = (bf16[512,512]{1,0:T(8,128)(2,1)S(1)}, bf16[512,512]{1,0:T(8,128)(2,1)S(1)}, u32[]{:S(2)}, u32[]{:S(2)}) collective-permute-start(bf16[512,512]{1,0:T(8,128)(2,1)S(1)} %fusion.45), channel_id=1, source_target_pairs={{0,2},{1,3},{2,0},{3,1},{4,6},{5,7},{6,4},{7,5},{8,10},{9,11},{10,... | collective-permute-start | bytes 1572872 | tf_op jit(solution)/shard_map/ppermute | solution.py:12
  242.2 17.9 %collective-permute-start.22 = (bf16[1024,128]{1,0:T(8,128)(2,1)S(1)}, bf16[1024,128]{1,0:T(8,128)(2,1)S(1)}, u32[]{:S(2)}, u32[]{:S(2)}) collective-permute-start(bf16[1024,128]{1,0:T(8,128)(2,1)S(1)} %shard_map.73), channel_id=1, source_target_pairs={{0,1},{1,0},{2,3},{3,2},{4,5},{5,4},{6,7},{7,6},{8,9},{9,8},{10,11... | collective-permute-start | bytes 786440 | tf_op jit(solution)/shard_map/ppermute | solution.py:12
  260.1 14.8 %collective-permute-start.23 = (bf16[1024,128]{1,0:T(8,128)(2,1)S(1)}, bf16[1024,128]{1,0:T(8,128)(2,1)}, u32[]{:S(2)}, u32[]{:S(2)}) collective-permute-start(bf16[1024,128]{1,0:T(8,128)(2,1)S(1)} %fusion.48), channel_id=1, source_target_pairs={{0,2},{1,3},{2,0},{3,1},{4,6},{5,7},{6,4},{7,5},{8,10},{9,11},{10,... | collective-permute-start | bytes 786440 | tf_op jit(solution)/shard_map/ppermute | solution.py:12
  (23 other events, 285.0 us)

commit v2 on v0

v2 whole, which is shorter than its diff:
```python
import functools

import jax
import jax.numpy as jnp
from jax import lax
from jax.experimental import pallas as pl
from jax.experimental.pallas import tpu as pltpu
from jax.sharding import PartitionSpec as P


def flip(x, axis, size, mask):
    return lax.ppermute(x, axis, [(i, i ^ mask) for i in range(size)])


def bits(size, first=1):
    out = []
    while first < size:
        out.append(first)
        first *= 2
    return out


def after(value, *others):
    return lax.optimization_barrier((value,) + others)[0]


def pick_kernel(low, own_at, mate_at, mine, own, mate, out):
    j = low + pl.program_id(0)

    @pl.when(mine[j] == 1)
    def _():
        out[...] = own[...]

    @pl.when(mine[j] != 1)
    def _():
        out[...] = mate[...]


def pick_pages(lists, low, count, own, mate):
    block = (1,) + own.shape[1:]
    return pl.pallas_call(
        functools.partial(pick_kernel, low),
        out_shape=jax.ShapeDtypeStruct((count,) + block[1:], own.dtype),
        grid_spec=pltpu.PrefetchScalarGridSpec(
            num_scalar_prefetch=3,
            grid=(count,),
            in_specs=[
                pl.BlockSpec(block, lambda j, own_at, mate_at, mine: (own_at[low + j], 0, 0)),
                pl.BlockSpec(block, lambda j, own_at, mate_at, mine: (mate_at[low + j], 0, 0)),
            ],
            out_specs=pl.BlockSpec(block, lambda j, own_at, mate_at, mine: (j, 0, 0)),
        ),
    )(*lists, own, mate)


def side_kernel(at, weight, out):
    width = weight.shape[2]
    for which in range(2):
        out[0, :, which * width : (which + 1) * width] = weight[:, which, :]


def side_by_side(at, weight, part, low, count):
    _, two, width = weight.shape
    return pl.pallas_call(
        side_kernel,
        out_shape=jax.ShapeDtypeStruct((count, part, two * width), weight.dtype),
        grid_spec=pltpu.PrefetchScalarGridSpec(
            num_scalar_prefetch=1,
            grid=(count,),
            in_specs=[pl.BlockSpec((part, two, width), lambda j, at: (at[low + j], 0, 0))],
            out_specs=pl.BlockSpec((1, part, two * width), lambda j, at: (j, 0, 0)),
        ),
    )(at, weight)


def shrink_kernel(pools, kind, *refs):
    x, out = refs[pools], refs[-1]
    t = pl.program_id(0)
    for number, pages in enumerate(refs[pools + 1 : -1]):

        @pl.when(kind[t] == number)
        def _(pages=pages):
            out[...] = jnp.dot(x[...], pages[0], preferred_element_type=jnp.float32).astype(out.dtype)


def tile_shrink(kind, places, rows, pools, tiles):
    tile_rows = rows.shape[0] // tiles
    features = rows.shape[1]
    columns = pools[0].shape[2]
    numbers = jnp.arange(len(pools), dtype=jnp.int32)
    used = kind[None, :] == numbers[:, None]
    last = lax.cummax(jnp.where(used, jnp.arange(tiles, dtype=jnp.int32)[None, :], 0), axis=1)
    same = last[:, :, None] == jnp.arange(tiles, dtype=jnp.int32)[None, None, :]
    held = jnp.sum(jnp.where(same & used[:, None, :], places[None, None, :], 0), axis=2)

    def pool_spec(number):
        return pl.BlockSpec((1, features, columns), lambda t, *s: (s[1 + number][t], 0, 0))

    return pl.pallas_call(
        functools.partial(shrink_kernel, len(pools)),
        out_shape=jax.ShapeDtypeStruct((rows.shape[0], columns), jnp.bfloat16),
        grid_spec=pltpu.PrefetchScalarGridSpec(
            num_scalar_prefetch=1 + len(pools),
            grid=(tiles,),
            in_specs=[pl.BlockSpec((tile_rows, features), lambda t, *s: (t, 0))]
            + [pool_spec(number) for number in range(len(pools))],
            out_specs=pl.BlockSpec((tile_rows, columns), lambda t, *s: (t, 0)),
        ),
        compiler_params=pltpu.CompilerParams(vmem_limit_bytes=48 << 20),
    )(kind, *[held[number] for number in range(len(pools))], rows, *pools)


def finish_kernel(offsets, live, up_at, *refs):
    keys, values, more_keys, more_values, reduced, up, out, held = refs
    t = pl.program_id(0)
    tile_rows, two, width = out.shape
    half = up.shape[2]
    room, rest = keys.shape[0], more_keys.shape[0]

    @pl.when(t == 0)
    def _():
        for which, (first, second) in enumerate(((keys, more_keys), (values, more_values))):
            held[which, :room] = first[...]
            held[which, room : room + rest] = second[...]
            held[which, room + rest :] = jnp.zeros((tile_rows, width), jnp.float32)

    low = pl.multiple_of((offsets[t] // 8) * 8, 8)
    shift = offsets[t] % 8
    alive = lax.broadcasted_iota(jnp.int32, (tile_rows, width), 0) < live[t]
    for which in range(2):
        expand = jnp.dot(
            reduced[:, which * half : (which + 1) * half],
            up[0, which],
            preferred_element_type=jnp.float32,
        )
        wide = held[which, pl.ds(low, tile_rows + 8), :]
        base = pltpu.roll(wide, tile_rows + 8 - shift, 0)[:tile_rows]
        out[:, which, :] = jnp.where(alive, base + expand, 0.0).astype(out.dtype)


def finish(offsets, live, up_at, totals, rest, reduced, ups):
    tiles = offsets.shape[0]
    rows, columns = reduced.shape
    tile_rows = rows // tiles
    width = totals[0].shape[1]

    def whole(array):
        return pl.BlockSpec(array.shape, lambda t, *s: (0, 0))

    return pl.pallas_call(
        finish_kernel,
        out_shape=jax.ShapeDtypeStruct((rows, 2, width), jnp.bfloat16),
        grid_spec=pltpu.PrefetchScalarGridSpec(
            num_scalar_prefetch=3,
            grid=(tiles,),
            in_specs=[whole(array) for array in (*totals, *rest)]
            + [
                pl.BlockSpec((tile_rows, columns), lambda t, *s: (t, 0)),
                pl.BlockSpec((1,) + ups.shape[1:], lambda t, *s: (s[2][t], 0, 0, 0)),
            ],
            out_specs=pl.BlockSpec((tile_rows, 2, width), lambda t, *s: (t, 0, 0)),
            scratch_shapes=[pltpu.VMEM((2, rows + tile_rows, width), jnp.float32)],
        ),
        compiler_params=pltpu.CompilerParams(vmem_limit_bytes=48 << 20),
    )(offsets, live, up_at, *totals, *rest, reduced, ups)


def on_device(
    input_rows,
    key_value_weight,
    adapter_down_weight,
    adapter_up_weight,
    tile_page_index,
    tile_live_rows,
):
    groups = lax.axis_size("groups")
    ranks = lax.axis_size("dp")
    shares = lax.axis_size("tensor")
    group = lax.axis_index("groups")
    rank = lax.axis_index("dp")
    share = lax.axis_index("tensor")
    chips = ranks // 2
    chip, core = rank // 2, rank % 2
    tiles = tile_live_rows.shape[0]
    local_pages = adapter_down_weight.shape[0]
    chip_pages = 2 * local_pages
    capacity = max(2, (2 * tiles + ranks - 1) // ranks)
    most_slots = 2 * capacity
    rows, features = input_rows.shape
    tile_rows = rows // tiles
    column_width = key_value_weight.shape[2]
    half = adapter_down_weight.shape[2] // 2

    columns = 2 * column_width
    plane = groups * ranks
    part = features // plane

    mate_down = flip(adapter_down_weight, "dp", ranks, 1)
    mate_up = flip(adapter_up_weight, "dp", ranks, 1)

    steps = [("dp", ranks, m, (rank // m) % 2) for m in bits(ranks, 2)]
    steps += [("groups", groups, m, (group // m) % 2) for m in bits(groups)]
    steps += [("dp", ranks, 1, core)]
    over_chips = len(bits(ranks, 2))
    spot = sum(bit << i for i, (_, _, _, bit) in enumerate(steps))
    turns = list(range(shares - 1, 0, -1))
    starts = (share ^ jnp.array(turns, jnp.int32)) * plane + spot
    piece = side_by_side(starts, key_value_weight, part, 0, 1)[0]
    weights = {}
    for which in range(2):
        cut = piece[:, which * column_width : (which + 1) * column_width]
        weights[turns[0], which] = flip(cut, "tensor", shares, turns[0])
    for i, k in enumerate(turns[1:]):
        piece = side_by_side(starts, key_value_weight, part, 1 + i, 1)[0]
        weights[k, 2] = flip(piece, "tensor", shares, k)

    table = tile_page_index.reshape(chips, 2 * tiles)
    page_range = jnp.arange(ranks * local_pages, dtype=jnp.int32)
    need = jnp.any(table[:, :, None] == page_range[None, None, :], axis=1)
    need = need.reshape(chips, chips, chip_pages)
    position = jnp.cumsum(need.astype(jnp.int32), axis=2) - 1
    usual = -(-5 * most_slots // 8)
    more = -(-6 * most_slots // 8)
    cuts = [0, max(1, usual // 5), max(2, 3 * usual // 5), usual]
    firsts = [0, 2 * usual, 2 * more, 2 * most_slots]
    most_pages = jnp.max(
        jnp.where(jnp.eye(chips, dtype=jnp.bool_), 0, position[:, :, -1] + 1)
    )
    slot_range = jnp.arange(2 * most_slots, dtype=jnp.int32)
    chip_range = jnp.arange(chip_pages, dtype=jnp.int32)

    offsets = jnp.cumsum(tile_live_rows) - tile_live_rows
    live_total = jnp.sum(tile_live_rows)
    live = jnp.arange(tile_rows, dtype=jnp.int32)[None, :] < tile_live_rows[:, None]
    packed_place = offsets[:, None] + jnp.arange(tile_rows, dtype=jnp.int32)[None, :]
    packed_place = jnp.where(live, packed_place, -1).reshape(rows)
    room = -(-13 * rows // 256) * 16

    def pack(first, last, x):
        pick = packed_place[None, :] == jnp.arange(first, last, dtype=jnp.int32)[:, None]
        return jnp.dot(pick.astype(x.dtype), x, preferred_element_type=jnp.float32).astype(x.dtype)

    past = []

    def cross(value, axis, size, m):
        if len(past) > 1:
            value = after(value, past[-2])
        past.append(flip(value, axis, size, m))
        return past[-1]

    def spread(held, first, last):
        for i in range(first, last):
            axis, size, m, bit = steps[i]
            got = cross(held, axis, size, m) if i < over_chips else flip(held, axis, size, m)
            held = jnp.concatenate([jnp.where(bit == 1, got, held), jnp.where(bit == 1, held, got)])
        return held

    keys = list(weights)
    for key in keys[:2]:
        weights[key] = spread(weights[key], 0, over_chips)

    listed = []
    for offset in range(1, chips):
        wanted = need[chip ^ offset, chip]
        place = position[chip ^ offset, chip]
        listed.append(
            jnp.sum(
                jnp.where(
                    wanted[None, :] & (place[None, :] == slot_range[:, None]), chip_range[None, :], 0
                ),
                axis=1,
            )
        )
    up_pool = jnp.where(core == 0, adapter_up_weight, mate_up), jnp.where(core == 0, mate_up, adapter_up_weight)
    up_pool = jnp.concatenate(up_pool)

    sent_lists = []
    for offset in range(1, chips):
        halves = [
            listed[offset - 1][low:high].reshape(2, (high - low) // 2)
            for low, high in zip(firsts[:-1], firsts[1:])
        ]
        halves = jnp.concatenate(halves, axis=1)
        sent = jnp.where(core == 0, halves[0], halves[1])
        mine = ((sent // local_pages) == core).astype(jnp.int32)
        at = sent % local_pages
        sent_lists.append((sent, (at * mine, at * (1 - mine), mine)))

    picked = {}
    for offset in range(1, chips):
        for i in range(3):
            picked[offset, i] = pick_pages(
                sent_lists[offset - 1][1],
                cuts[i],
                cuts[i + 1] - cuts[i],
                adapter_down_weight,
                mate_down,
            )
    pools = [adapter_down_weight, mate_down]
    pool_of = {}

    def send_pages(offset, i):
        got = cross(picked[offset, i], "dp", ranks, 2 * offset)
        pool_of[offset, i] = len(pools)
        pools.extend([got, flip(got, "dp", ranks, 1)])

    for offset in range(1, chips):
        send_pages(offset, 0)
    for key in keys[2:]:
        weights[key] = spread(weights[key], 0, over_chips)
    for offset in range(1, chips):
        send_pages(offset, 1)
        send_pages(offset, 2)
    near_ups = [
        cross(up_pool[sent_lists[offset - 1][0][:usual]], "dp", ranks, 2 * offset)
        for offset in range(1, chips)
    ]
    near_up = jnp.concatenate(near_ups)
    up_pools = [up_pool, near_up, flip(near_up, "dp", ranks, 1)]

    for key in keys:
        weights[key] = spread(weights[key], over_chips, len(steps))
    def weight_of(weights, k, which):
        if (k, which) in weights:
            return weights[k, which]
        return weights[k, 2][:, which * column_width : (which + 1) * column_width]

    def own_weight(weight):
        at = share * plane + jnp.arange(plane, dtype=jnp.int32)
        return side_by_side(at, weight, part, 0, plane).reshape(features, columns)

    def project(packed, weights, own=None):
        sums = {}
        for k in turns:
            for which in range(2):
                sums[k, which] = jnp.dot(
                    packed, weight_of(weights, k, which), preferred_element_type=jnp.float32
                )
            if k == turns[0] and own is None:
                sent = [sums[k, which].astype(jnp.bfloat16) for which in range(2)]
                own = own_weight(after(key_value_weight, *sent))
        for which in range(2):
            sums[0, which] = jnp.dot(
                packed,
                own[:, which * column_width : (which + 1) * column_width],
                preferred_element_type=jnp.float32,
            )
        for m in bits(shares):
            arrived = {
                (k, which): flip(sums.pop((k, which)).astype(jnp.bfloat16), "tensor", shares, m)
                for k in turns
                for which in range(2)
                if (k, which) in sums and k & m
            }
            for (k, which), value in arrived.items():
                sums[k ^ m, which] = sums[k ^ m, which] + value.astype(jnp.float32)
        return [sums[0, which] for which in range(2)], own

    packed = pack(0, room, after(input_rows, *picked.values()))
    totals, own = project(packed, weights)
    rest = lax.cond(
        live_total > room,
        lambda operands: project(pack(room, rows, operands[0]), *operands[1:])[0],
        lambda operands: [jnp.zeros((rows - room, column_width), jnp.float32)] * 2,
        (input_rows, weights, own),
    )

    for stage in (1, 2):

        def send_more(sources):
            own_down, other_down, ups = sources
            got = []
            for offset in range(1, chips):
                low, count = firsts[stage] // 2, (firsts[stage + 1] - firsts[stage]) // 2
                numbers, lists = sent_lists[offset - 1]
                send = numbers[low : low + count]
                down = pick_pages(lists, low, count, own_down, other_down)
                got.append((flip(down, "dp", ranks, 2 * offset), flip(ups[send], "dp", ranks, 2 * offset)))
            down = jnp.concatenate([pair[0] for pair in got])
            up = jnp.concatenate([pair[1] for pair in got])
            return down, flip(down, "dp", ranks, 1), up, flip(up, "dp", ranks, 1)

        def send_none(sources):
            own_down, other_down, ups = sources
            count = (chips - 1) * (firsts[stage + 1] - firsts[stage]) // 2
            down = jnp.zeros((count,) + own_down.shape[1:], own_down.dtype)
            up = jnp.zeros((count,) + ups.shape[1:], ups.dtype)
            return down, down, up, up

        if firsts[stage + 1] > firsts[stage]:
            near, far, near_up, far_up = lax.cond(
                most_pages > firsts[stage],
                send_more,
                send_none,
                (adapter_down_weight, mate_down, up_pool),
            )
            pool_of[stage] = len(pools)
            pools += [near, far]
            up_pools += [near_up, far_up]

    pages = tile_page_index.reshape(ranks, tiles)[rank]
    owner = pages // local_pages
    owner_chip = owner // 2
    step = owner_chip ^ chip
    entry = position[chip, owner_chip, pages % chip_pages]
    kind = jnp.where(owner == rank, 0, 1)
    places = pages % local_pages
    up_at = pages % chip_pages
    up_first = up_pool.shape[0]
    for stage in range(3):
        count = (firsts[stage + 1] - firsts[stage]) // 2
        if count == 0:
            continue
        here = (owner_chip != chip) & (entry >= firsts[stage])
        sender, at = (entry - firsts[stage]) // count, (entry - firsts[stage]) % count
        far = (sender != core).astype(jnp.int32)
        up_at = jnp.where(here, up_first + (far * (chips - 1) + step - 1) * count + at, up_at)
        up_first += 2 * (chips - 1) * count
        if stage:
            kind = jnp.where(here, pool_of[stage] + far, kind)
            places = jnp.where(here, (step - 1) * count + at, places)
            continue
        for offset in range(1, chips):
            for i in range(3):
                chosen = here & (step == offset) & (at >= cuts[i])
                kind = jnp.where(chosen, pool_of[offset, i] + far, kind)
                places = jnp.where(chosen, at - cuts[i], places)

    shrink = tile_shrink(
        kind.astype(jnp.int32), places.astype(jnp.int32), input_rows, pools, tiles
    ).astype(jnp.float32)
    for m in bits(shares):
        sent = shrink.astype(jnp.bfloat16)
        shrink = shrink + flip(sent, "tensor", shares, m).astype(jnp.float32)
    return finish(
        offsets,
        tile_live_rows,
        up_at.astype(jnp.int32),
        totals,
        rest,
        shrink.astype(jnp.bfloat16),
        jnp.concatenate(up_pools),
    )


def solution(mesh):
    return jax.shard_map(
        on_device,
        mesh=mesh,
        in_specs=(
            P(("groups", "dp"), "tensor"),
            P(None, None, "tensor"),
            P("dp", "tensor", None),
            P("dp", None, None, "tensor"),
            P("groups"),
            P(("groups", "dp")),
        ),
        out_specs=P(("groups", "dp"), None, "tensor"),
        check_vma=False,
    )
```

time: 342 us -> 250 us (0.73)
  waiting for transfers between devices: 187 us -> 90.6 us
  blocking collectives: 64.4 us -> 0 us
  Pallas kernels: 0 us -> 39.4 us
  starting transfers between devices: 10.7 us -> 42.5 us
  other arithmetic: 0.65 us -> 27.9 us
  local copies, waits for them, and re-layouts: 40.1 us -> 23.1 us
  between operations: 13.5 us -> 2.33 us
    all_gather x1 -> x0, waiting for transfers between devices: 110 us -> none  [on_device(): lax.all_gather(input_rows, 'tensor', axis=1, tiled=True)]
    ppermute x0 -> x34, waiting for transfers between devices: none -> 90.6 us  [flip(): return lax.ppermute(x, axis, [(i, i ^ mask) for i in range(size)])]
    all_to_all x2 -> x0, waiting for transfers between devices: 76.7 us -> none  [the longest x1 72 us: on_device(): lax.all_to_all(outgoing_down, 'dp', split_axis=0, concat_axis=0, tiled=True)]
    psum x1 -> x0, blocking collectives: 64.4 us -> none  [on_device(): shrink_part = lax.psum(partial_value, 'tensor')]
    ppermute x0 -> x34, starting transfers between devices: none -> 42.5 us  [flip(): return lax.ppermute(x, axis, [(i, i ^ mask) for i in range(size)])]
    pallas_call x0 -> x9, Pallas kernels: none -> 39.4 us  [the longest x4 17 us: side_by_side(): pl.pallas_call(side_kernel, out_shape=jax.ShapeDtypeStruct((count, part,...]
    gather x4 -> x2, local copies, waits for them, and re-layouts: 17.7 us -> 3.55 us  [the longest x1 2.89 us: on_device(): up_pool[sent_lists[offset - 1][0][:usual]]]
    dot_general x1 -> x0, local copies, waits for them, and re-layouts: 11.4 us -> none  [on_device(): jnp.dot(lax.all_gather(input_rows, 'tensor', axis=1, tiled=True), weight_...]
  transfers between devices with their start and end apart: 3 -> 34, of which waited for: 3 -> 12; matrix products, arithmetic and copies ran while one was open for 13% -> 27% of each run, Pallas kernels for 0% -> 14%
where the time goes in v2:
time: 250 us; the launch traced here: 247 us
  waiting for transfers between devices  90.6 us (36%)
  starting transfers between devices  42.5 us (17%)
  Pallas kernels  39.4 us (16%)
  other arithmetic  27.9 us (11%)
  local copies, waits for them, and re-layouts  23.1 us (9%)
  matrix products  21.6 us (9%)
    ppermute x34, waiting for transfers between devices, flip(): return lax.ppermute(x, axis, [(i, i ^ mask) for i in range(size)])  90.6 us
    ppermute x34, starting transfers between devices, flip(): return lax.ppermute(x, axis, [(i, i ^ mask) for i in range(size)])  42.5 us
    pallas_call x4, Pallas kernels, side_by_side(): pl.pallas_call(side_kernel, out_shape=jax.ShapeDtypeStruct((count, part,...  17 us
    dot_general x6, matrix products, project(): jnp.dot(packed, weight_of(weights, k, which), preferred_element_type=jnp....  13.1 us
    unnamed x89, local copies, waits for them, and re-layouts  9.15 us
    pallas_call x3, Pallas kernels, pick_pages(): pl.pallas_call(functools.partial(pick_kernel, low), out_shape=jax.ShapeDt...  8.42 us
    pallas_call x1, Pallas kernels, tile_shrink(): pl.pallas_call(functools.partial(shrink_kernel, len(pools)), out_shape=ja...  8.16 us
    concatenate x12, other arithmetic, spread(): jnp.concatenate([jnp.where(bit == 1, got, held), jnp.where(bit == 1, held...  7.7 us
  transfers between devices with their start and end apart: 34, of which 12 were waited for; matrix products, arithmetic and copies ran while one was open for 27% of the time, Pallas kernels for 14%

profile of v2, /device:TPU:3, one launch (start us, length us, event | category | flops | bytes accessed | tf_op | source)
XLA Modules:
  0.0 247.4 jit_solution(18262686201376339673)
XLA Ops:
  5.7 3.4 %collective-permute-start.19 = (bf16[256,256]{1,0:T(8,128)(2,1)S(1)}, bf16[256,256]{1,0:T(8,128)(2,1)S(1)}, u32[]{:S(2)}, u32[]{:S(2)}) collective-permute-start(bf16[256,256]{1,0:T(8,128)(2,1)S(1)} %get-tuple-element.182), channel_id=1, source_target_pairs={{0,3},{1,2},{2,1},{3,0},{4,7},{5,6},{6,5},{7,4},{8,11},{9,10},{10,... | collective-permute-start | bytes 393224 | tf_op jit(solution)/shard_map/ppermute | solution.py:12
  18.7 3.3 %collective-permute-done.15 = bf16[256,256]{1,0:T(8,128)(2,1)S(1)} collective-permute-done((bf16[256,256]{1,0:T(8,128)(2,1)S(1)}, bf16[256,256]{1,0:T(8,128)(2,1)S(1)}, u32[]{:S(2)}, u32[]{:S(2)}) %collective-permute-start.15) | collective-permute-done | bytes 131104 | tf_op jit(solution)/shard_map/ppermute | solution.py:12
  23.3 2.9 %shard_map.78 = bf16[1,256,512]{2,1,0:T(8,128)(2,1)} custom-call(s32[3]{0:T(128)} %multiply_add_fusion.at, bf16[8192,2,256]{2,1,0:T(2,128)(2,1)} %weight.6), custom_call_target="tpu_custom_call" | custom-call | tf_op jit(solution)/shard_map/pallas_call | solution.py:64
  26.3 10.1 %collective-permute-start.23 = (bf16[256,512]{1,0:T(8,128)(2,1)}, bf16[256,512]{1,0:T(8,128)(2,1)}, u32[]{:S(2)}, u32[]{:S(2)}) collective-permute-start(bf16[256,512]{1,0:T(8,128)(2,1)} %bitcast.155), channel_id=1, source_target_pairs={{0,1},{1,0},{2,3},{3,2},{4,5},{5,4},{6,7},{7,6},{8,9},{9,8},{10,11... | collective-permute-start | bytes 786440 | tf_op jit(solution)/shard_map/ppermute | solution.py:12
  39.8 3.5 %collective-permute-done.21 = bf16[512,256]{1,0:T(8,128)(2,1)S(1)} collective-permute-done((bf16[512,256]{1,0:T(8,128)(2,1)S(1)}, bf16[512,256]{1,0:T(8,128)(2,1)S(1)}, u32[]{:S(2)}, u32[]{:S(2)}) %collective-permute-start.21) | collective-permute-done | bytes 262176 | tf_op jit(solution)/shard_map/ppermute | solution.py:12
  44.5 4.6 %collective-permute-done.17 = bf16[512,256]{1,0:T(8,128)(2,1)S(1)} collective-permute-done((bf16[512,256]{1,0:T(8,128)(2,1)S(1)}, bf16[512,256]{1,0:T(8,128)(2,1)S(1)}, u32[]{:S(2)}, u32[]{:S(2)}) %collective-permute-start.17) | collective-permute-done | bytes 262176 | tf_op jit(solution)/shard_map/ppermute | solution.py:12
  66.3 8.4 %collective-permute-done.24.refs_15_ = bf16[1,2048,128]{2,1,0:T(8,128)(2,1)} collective-permute-done((bf16[1,2048,128]{2,1,0:T(8,128)(2,1)}, bf16[1,2048,128]{2,1,0:T(8,128)(2,1)}, u32[]{:S(2)}, u32[]{:S(2)}) %collective-permute-start.24) | collective-permute-done | bytes 524320 | tf_op jit(solution)/shard_map/ppermute | solution.py:12
  76.5 2.9 %gather_fusion.2 = bf16[5,2,64,256]{3,2,1,0:T(8,128)(2,1)} fusion(bf16[32,2,64,256]{3,2,1,0:T(8,128)(2,1)} %pad_maximum_fusion.2, s32[1024]{0:T(1024)S(1)} %pad_clamp_fusion.1), kind=kCustom, calls=%fused_computation.2 | custom fusion | bytes 655380 | tf_op jit(solution)/shard_map/gather | solution.py:315
  91.6 4.0 %convolution_convert_fusion.5 = bf16[832,2048]{1,0:T(8,128)(2,1)S(1)} fusion(bf16[1024,2048]{1,0:T(8,128)(2,1)S(1)} %copy-done.22, s32[1024]{0:T(1024)S(1)} %select_bitcast_fusion.1), kind=kOutput, calls=%fused_computation.30 | convolution fusion | flops 3492216832 | bytes 7606272 | tf_op jit(solution)/shard_map/dot_general | solution.py:241
  95.6 6.9 %collective-permute-done.31 = bf16[512,512]{1,0:T(8,128)(2,1)S(1)} collective-permute-done((bf16[512,512]{1,0:T(8,128)(2,1)S(1)}, bf16[512,512]{1,0:T(8,128)(2,1)S(1)}, u32[]{:S(2)}, u32[]{:S(2)}) %collective-permute-start.31) | collective-permute-done | bytes 524320 | tf_op jit(solution)/shard_map/ppermute | solution.py:12
  103.9 3.4 %collective-permute-start.32 = (bf16[1024,512]{1,0:T(8,128)(2,1)}, bf16[1024,512]{1,0:T(8,128)(2,1)}, u32[]{:S(2)}, u32[]{:S(2)}) collective-permute-start(bf16[1024,512]{1,0:T(8,128)(2,1)} %pad_maximum_fusion.6), channel_id=1, source_target_pairs={{0,4},{4,0},{8,12},{12,8},{1,5},{5,1},{9,13},{13,9},{2,6},{6,2},{1... | collective-permute-start | bytes 3145736 | tf_op jit(solution)/shard_map/ppermute | solution.py:12
  107.3 6.4 %collective-permute-done.26 = bf16[512,512]{1,0:T(8,128)(2,1)S(1)} collective-permute-done((bf16[512,512]{1,0:T(8,128)(2,1)S(1)}, bf16[512,512]{1,0:T(8,128)(2,1)S(1)}, u32[]{:S(2)}, u32[]{:S(2)}) %collective-permute-start.26) | collective-permute-done | bytes 524320 | tf_op jit(solution)/shard_map/ppermute | solution.py:12
  121.4 8.4 %shard_map.77 = bf16[8,256,512]{2,1,0:T(8,128)(2,1)} custom-call(s32[8]{0:T(128)} %iota_add_fusion.1.at, bf16[8192,2,256]{2,1,0:T(2,128)(2,1)} %weight.6), custom_call_target="tpu_custom_call" | custom-call | tf_op jit(solution)/shard_map/pallas_call | solution.py:64
  140.8 3.0 %conditional.4 = (bf16[1,2048,128]{2,1,0:T(8,128)(2,1)}, bf16[1,2048,128]{2,1,0:T(8,128)(2,1)}, bf16[1,2,64,256]{3,2,1,0:T(8,128)(2,1)}, bf16[1,2,64,256]{3,2,1,0:T(8,128)(2,1)}) conditional(s32[]{:T(128)} %convert_element_type.175, () %tuple.46, (s32[8]{0:T(128)S(1)}, s32[8]{0:T(128)S(1)}, s32[8]{0:T(128)S(1)}, bf16[16,2048,128]{2,1,0:T(8,128)(2,1)}, ...), branch_computations={%region_10.11_spmd, %region_11.12_spmd} | conditional | flops 3 | bytes 4849902 | solution.py:391
  143.8 3.6 %conditional.5 = (bf16[2,2048,128]{2,1,0:T(8,128)(2,1)}, bf16[2,2048,128]{2,1,0:T(8,128)(2,1)}, bf16[2,2,64,256]{3,2,1,0:T(8,128)(2,1)}, bf16[2,2,64,256]{3,2,1,0:T(8,128)(2,1)}) conditional(s32[]{:T(128)} %convert_element_type.176, () %tuple.48, (s32[8]{0:T(128)S(1)}, s32[8]{0:T(128)S(1)}, s32[8]{0:T(128)S(1)}, bf16[16,2048,128]{2,1,0:T(8,128)(2,1)}, ...), branch_computations={%region_12.13_spmd, %region_13.14_spmd} | conditional | flops 1030 | bytes 9703648 | solution.py:391
  147.7 3.4 %fusion.24 = f32[832,256]{1,0:T(8,128)S(1)} fusion(bf16[832,2048]{1,0:T(8,128)(2,1)} %copy-done.40, bf16[2048,512]{1,0:T(8,128)(2,1)} %bitcast.150), kind=kOutput, calls=%fused_computation.56 | convolution fusion | flops 872415232 | bytes 5308416 | tf_op jit(solution)/shard_map/dot_general | solution.py:343
  152.9 3.6 %collective-permute-done.46 = bf16[5,2,64,256]{3,2,1,0:T(8,128)(2,1)S(1)} collective-permute-done((bf16[5,2,64,256]{3,2,1,0:T(8,128)(2,1)}, bf16[5,2,64,256]{3,2,1,0:T(8,128)(2,1)S(1)}, u32[]{:S(2)}, u32[]{:S(2)}) %collective-permute-start.46) | collective-permute-done | bytes 327712 | tf_op jit(solution)/shard_map/ppermute | solution.py:12
  164.2 14.6 %collective-permute-done.41.refs_19_ = bf16[2,2048,128]{2,1,0:T(8,128)(2,1)S(1)} collective-permute-done((bf16[2,2048,128]{2,1,0:T(8,128)(2,1)S(1)}, bf16[2,2048,128]{2,1,0:T(8,128)(2,1)S(1)}, u32[]{:S(2)}, u32[]{:S(2)}) %collective-permute-start.41) | collective-permute-done | bytes 1048608 | tf_op jit(solution)/shard_map/ppermute | solution.py:12
  188.3 3.0 %fusion.14 = bf16[832,256]{1,0:T(8,128)(2,1)} fusion(bf16[832,2048]{1,0:T(8,128)(2,1)S(1)} %copy-done.41, bf16[1024,512]{1,0:T(8,128)(2,1)S(1)} %copy-done.13, bf16[1024,512]{1,0:T(8,128)(2,1)S(1)} %copy-done.11, bf16[832,256]{1,0:T(8,128)(2,1)} %collective-permute-done.33), kind=kOutput, calls=%fused_computation.50 | convolution fusion | flops 875151360 | bytes 6356992 | tf_op jit(solution)/shard_map/dot_general | solution.py:336
  193.6 8.2 %shard_map.80 = bf16[1024,128]{1,0:T(8,128)(2,1)S(1)} custom-call(s32[8]{0:T(128)S(1)} %get-tuple-element.148.kind, s32[8]{0:T(128)S(1)} %get-tuple-element.140.refs_0_, s32[8]{0:T(128)S(1)} %get-tuple-element.139.refs_1_, s32[8]{0:T(128)S(1)} %get-tuple-element.138.refs_2_, s32[8]{0:T(128)S(1)} %get-tuple-element.137.refs_3_, ...), custom_call_target="tpu_custom_call" | custom-call | tf_op jit(solution)/shard_map/pallas_call | solution.py:99
  201.9 4.5 %collective-permute-done.37 = bf16[832,256]{1,0:T(8,128)(2,1)S(1)} collective-permute-done((bf16[832,256]{1,0:T(8,128)(2,1)}, bf16[832,256]{1,0:T(8,128)(2,1)S(1)}, u32[]{:S(2)}, u32[]{:S(2)}) %collective-permute-start.37) | collective-permute-done | bytes 426016 | tf_op jit(solution)/shard_map/ppermute | solution.py:12
  206.6 20.2 %collective-permute-done.44 = bf16[1024,128]{1,0:T(8,128)(2,1)S(1)} collective-permute-done((bf16[1024,128]{1,0:T(8,128)(2,1)S(1)}, bf16[1024,128]{1,0:T(8,128)(2,1)S(1)}, u32[]{:S(2)}, u32[]{:S(2)}) %collective-permute-start.44) | collective-permute-done | bytes 262176 | tf_op jit(solution)/shard_map/ppermute | solution.py:12
  227.3 14.3 %collective-permute-done.45 = bf16[1024,128]{1,0:T(8,128)(2,1)S(1)} collective-permute-done((bf16[1024,128]{1,0:T(8,128)(2,1)S(1)}, bf16[1024,128]{1,0:T(8,128)(2,1)S(1)}, u32[]{:S(2)}, u32[]{:S(2)}) %collective-permute-start.45) | collective-permute-done | bytes 262176 | tf_op jit(solution)/shard_map/ppermute | solution.py:12
  241.6 5.8 %shard_map.81 = bf16[1024,2,256]{2,1,0:T(2,128)(2,1)} custom-call(s32[8]{0:T(128)S(1)} %get-tuple-element.184.offsets, s32[8]{0:T(128)S(1)} %copy-done, s32[8]{0:T(128)S(1)} %add_select_fusion.up_at, f32[832,256]{1,0:T(8,128)S(1)} %convert_add_fusion.3.refs_0_, f32[832,256]{1,0:T(8,128)S(1)} %convert_add_fusion.2.refs_1_, ...), custom_call_target="tpu_custom_call" | custom-call | tf_op jit(solution)/shard_map/pallas_call | solution.py:150
  (237 shorter events, 99.9 us)
Async XLA Ops:
  0.0 58.3 %collective-permute-start.14 = (bf16[16,2048,128]{2,1,0:T(8,128)(2,1)}, bf16[16,2048,128]{2,1,0:T(8,128)(2,1)}, u32[]{:S(2)}, u32[]{:S(2)}) collective-permute-start(bf16[16,2048,128]{2,1,0:T(8,128)(2,1)} %refs_13_.1), channel_id=1, source_target_pairs={{0,4},{4,0},{8,12},{12,8},{1,5},{5,1},{9,13},{13,9},{2,6},{6,2},{1... | collective-permute-start | bytes 25165832 | tf_op jit(solution)/shard_map/ppermute | solution.py:12
  0.7 52.4 %collective-permute-start.43 = (bf16[16,2,64,256]{3,2,1,0:T(8,128)(2,1)}, bf16[16,2,64,256]{3,2,1,0:T(8,128)(2,1)S(1)}, u32[]{:S(2)}, u32[]{:S(2)}) collective-permute-start(bf16[16,2,64,256]{3,2,1,0:T(8,128)(2,1)} %param.16), channel_id=1, source_target_pairs={{0,4},{4,0},{8,12},{12,8},{1,5},{5,1},{9,13},{13,9},{2,6},{6,2},{1... | collective-permute-start | bytes 3145736 | tf_op jit(solution)/shard_map/ppermute | solution.py:12
  12.0 27.5 %collective-permute-start.29 = (bf16[256,512]{1,0:T(8,128)(2,1)}, bf16[256,512]{1,0:T(8,128)(2,1)}, u32[]{:S(2)}, u32[]{:S(2)}) collective-permute-start(bf16[256,512]{1,0:T(8,128)(2,1)} %bitcast.154), channel_id=1, source_target_pairs={{0,2},{1,3},{2,0},{3,1},{4,6},{5,7},{6,4},{7,5},{8,10},{9,11},{10,... | collective-permute-start | bytes 786440 | tf_op jit(solution)/shard_map/ppermute | solution.py:12
  22.0 14.4 %collective-permute-start.16 = (bf16[256,256]{1,0:T(8,128)(2,1)S(1)}, bf16[256,256]{1,0:T(8,128)(2,1)S(1)}, u32[]{:S(2)}, u32[]{:S(2)}) collective-permute-start(bf16[256,256]{1,0:T(8,128)(2,1)S(1)} %collective-permute-done.15), channel_id=1, source_target_pairs={{0,8},{4,12},{8,0},{12,4},{1,9},{5,13},{9,1},{13,5},{2,10},{6,14},... | collective-permute-start | bytes 393224 | tf_op jit(solution)/shard_map/ppermute | solution.py:12
  26.3 40.0 %collective-permute-start.23 = (bf16[256,512]{1,0:T(8,128)(2,1)}, bf16[256,512]{1,0:T(8,128)(2,1)}, u32[]{:S(2)}, u32[]{:S(2)}) collective-permute-start(bf16[256,512]{1,0:T(8,128)(2,1)} %bitcast.155), channel_id=1, source_target_pairs={{0,1},{1,0},{2,3},{3,2},{4,5},{5,4},{6,7},{7,6},{8,9},{9,8},{10,11... | collective-permute-start | bytes 786440 | tf_op jit(solution)/shard_map/ppermute | solution.py:12
  39.5 45.1 %collective-permute-start.30 = (bf16[256,512]{1,0:T(8,128)(2,1)}, bf16[256,512]{1,0:T(8,128)(2,1)}, u32[]{:S(2)}, u32[]{:S(2)}) collective-permute-start(bf16[256,512]{1,0:T(8,128)(2,1)} %collective-permute-done.29), channel_id=1, source_target_pairs={{0,8},{4,12},{8,0},{12,4},{1,9},{5,13},{9,1},{13,5},{2,10},{6,14},... | collective-permute-start | bytes 786440 | tf_op jit(solution)/shard_map/ppermute | solution.py:12
  61.2 13.6 %collective-permute-start.24 = (bf16[1,2048,128]{2,1,0:T(8,128)(2,1)}, bf16[1,2048,128]{2,1,0:T(8,128)(2,1)}, u32[]{:S(2)}, u32[]{:S(2)}) collective-permute-start(bf16[1,2048,128]{2,1,0:T(8,128)(2,1)} %shard_map.73), channel_id=1, source_target_pairs={{0,8},{4,12},{8,0},{12,4},{1,9},{5,13},{9,1},{13,5},{2,10},{6,14},... | collective-permute-start | bytes 1572872 | tf_op jit(solution)/shard_map/ppermute | solution.py:12
  74.8 13.8 %collective-permute-start.25 = (bf16[256,512]{1,0:T(8,128)(2,1)}, bf16[256,512]{1,0:T(8,128)(2,1)S(1)}, u32[]{:S(2)}, u32[]{:S(2)}) collective-permute-start(bf16[256,512]{1,0:T(8,128)(2,1)} %collective-permute-done.23), channel_id=1, source_target_pairs={{0,8},{4,12},{8,0},{12,4},{1,9},{5,13},{9,1},{13,5},{2,10},{6,14},... | collective-permute-start | bytes 786440 | tf_op jit(solution)/shard_map/ppermute | solution.py:12
  84.5 62.9 %collective-permute-start.39 = (bf16[2,2048,128]{2,1,0:T(8,128)(2,1)}, bf16[2,2048,128]{2,1,0:T(8,128)(2,1)}, u32[]{:S(2)}, u32[]{:S(2)}) collective-permute-start(bf16[2,2048,128]{2,1,0:T(8,128)(2,1)} %shard_map.74), channel_id=1, source_target_pairs={{0,8},{4,12},{8,0},{12,4},{1,9},{5,13},{9,1},{13,5},{2,10},{6,14},... | collective-permute-start | bytes 3145736 | tf_op jit(solution)/shard_map/ppermute | solution.py:12
  90.3 23.3 %collective-permute-start.26 = (bf16[512,512]{1,0:T(8,128)(2,1)S(1)}, bf16[512,512]{1,0:T(8,128)(2,1)S(1)}, u32[]{:S(2)}, u32[]{:S(2)}) collective-permute-start(bf16[512,512]{1,0:T(8,128)(2,1)S(1)} %pad_maximum_fusion.9), channel_id=1, source_target_pairs={{0,16},{16,0},{1,17},{17,1},{2,18},{18,2},{3,19},{19,3},{4,20},{20... | collective-permute-start | bytes 1572872 | tf_op jit(solution)/shard_map/ppermute | solution.py:12
  103.9 25.9 %collective-permute-start.32 = (bf16[1024,512]{1,0:T(8,128)(2,1)}, bf16[1024,512]{1,0:T(8,128)(2,1)}, u32[]{:S(2)}, u32[]{:S(2)}) collective-permute-start(bf16[1024,512]{1,0:T(8,128)(2,1)} %pad_maximum_fusion.6), channel_id=1, source_target_pairs={{0,4},{4,0},{8,12},{12,8},{1,5},{5,1},{9,13},{13,9},{2,6},{6,2},{1... | collective-permute-start | bytes 3145736 | tf_op jit(solution)/shard_map/ppermute | solution.py:12
  115.7 17.3 %collective-permute-start.27 = (bf16[1024,512]{1,0:T(8,128)(2,1)}, bf16[1024,512]{1,0:T(8,128)(2,1)}, u32[]{:S(2)}, u32[]{:S(2)}) collective-permute-start(bf16[1024,512]{1,0:T(8,128)(2,1)} %pad_maximum_fusion.5), channel_id=1, source_target_pairs={{0,4},{4,0},{8,12},{12,8},{1,5},{5,1},{9,13},{13,9},{2,6},{6,2},{1... | collective-permute-start | bytes 3145736 | tf_op jit(solution)/shard_map/ppermute | solution.py:12
  139.3 42.8 %collective-permute-start.36 = (bf16[832,256]{1,0:T(8,128)(2,1)}, bf16[832,256]{1,0:T(8,128)(2,1)}, u32[]{:S(2)}, u32[]{:S(2)}) collective-permute-start(bf16[832,256]{1,0:T(8,128)(2,1)} %convolution_convert_fusion.8), channel_id=1, source_target_pairs={{0,1},{1,0},{2,3},{3,2},{4,5},{5,4},{6,7},{7,6},{8,9},{9,8},{10,11... | collective-permute-start | bytes 1277960 | tf_op jit(solution)/shard_map/ppermute | solution.py:12
  139.3 45.7 %collective-permute-start.33 = (bf16[832,256]{1,0:T(8,128)(2,1)}, bf16[832,256]{1,0:T(8,128)(2,1)}, u32[]{:S(2)}, u32[]{:S(2)}) collective-permute-start(bf16[832,256]{1,0:T(8,128)(2,1)} %convolution_convert_fusion.9), channel_id=1, source_target_pairs={{0,1},{1,0},{2,3},{3,2},{4,5},{5,4},{6,7},{7,6},{8,9},{9,8},{10,11... | collective-permute-start | bytes 1277960 | tf_op jit(solution)/shard_map/ppermute | solution.py:12
  151.2 27.7 %collective-permute-start.41 = (bf16[2,2048,128]{2,1,0:T(8,128)(2,1)S(1)}, bf16[2,2048,128]{2,1,0:T(8,128)(2,1)S(1)}, u32[]{:S(2)}, u32[]{:S(2)}) collective-permute-start(bf16[2,2048,128]{2,1,0:T(8,128)(2,1)S(1)} %copy-done.38), channel_id=1, source_target_pairs={{0,8},{4,12},{8,0},{12,4},{1,9},{5,13},{9,1},{13,5},{2,10},{6,14},... | collective-permute-start | bytes 3145736 | tf_op jit(solution)/shard_map/ppermute | solution.py:12
  160.0 31.3 %collective-permute-start.38 = (bf16[1,2048,128]{2,1,0:T(8,128)(2,1)}, bf16[1,2048,128]{2,1,0:T(8,128)(2,1)S(1)}, u32[]{:S(2)}, u32[]{:S(2)}) collective-permute-start(bf16[1,2048,128]{2,1,0:T(8,128)(2,1)} %collective-permute-done.24.refs_15_), channel_id=1, source_target_pairs={{0,4},{4,0},{8,12},{12,8},{1,5},{5,1},{9,13},{13,9},{2,6},{6,2},{1... | collective-permute-start | bytes 1572872 | tf_op jit(solution)/shard_map/ppermute | solution.py:12
  160.1 31.2 %collective-permute-start.40 = (bf16[2,2048,128]{2,1,0:T(8,128)(2,1)}, bf16[2,2048,128]{2,1,0:T(8,128)(2,1)S(1)}, u32[]{:S(2)}, u32[]{:S(2)}) collective-permute-start(bf16[2,2048,128]{2,1,0:T(8,128)(2,1)} %collective-permute-done.39.refs_17_), channel_id=1, source_target_pairs={{0,4},{4,0},{8,12},{12,8},{1,5},{5,1},{9,13},{13,9},{2,6},{6,2},{1... | collective-permute-start | bytes 3145736 | tf_op jit(solution)/shard_map/ppermute | solution.py:12
  178.9 14.7 %collective-permute-start.42 = (bf16[2,2048,128]{2,1,0:T(8,128)(2,1)S(1)}, bf16[2,2048,128]{2,1,0:T(8,128)(2,1)S(1)}, u32[]{:S(2)}, u32[]{:S(2)}) collective-permute-start(bf16[2,2048,128]{2,1,0:T(8,128)(2,1)S(1)} %collective-permute-done.41.refs_19_), channel_id=1, source_target_pairs={{0,4},{4,0},{8,12},{12,8},{1,5},{5,1},{9,13},{13,9},{2,6},{6,2},{1... | collective-permute-start | bytes 3145736 | tf_op jit(solution)/shard_map/ppermute | solution.py:12
  182.1 19.8 %collective-permute-start.35 = (bf16[832,256]{1,0:T(8,128)(2,1)}, bf16[832,256]{1,0:T(8,128)(2,1)S(1)}, u32[]{:S(2)}, u32[]{:S(2)}) collective-permute-start(bf16[832,256]{1,0:T(8,128)(2,1)} %convolution_convert_fusion.6), channel_id=1, source_target_pairs={{0,1},{1,0},{2,3},{3,2},{4,5},{5,4},{6,7},{7,6},{8,9},{9,8},{10,11... | collective-permute-start | bytes 1277960 | tf_op jit(solution)/shard_map/ppermute | solution.py:12
  185.0 21.4 %collective-permute-start.37 = (bf16[832,256]{1,0:T(8,128)(2,1)}, bf16[832,256]{1,0:T(8,128)(2,1)S(1)}, u32[]{:S(2)}, u32[]{:S(2)}) collective-permute-start(bf16[832,256]{1,0:T(8,128)(2,1)} %fusion.15), channel_id=1, source_target_pairs={{0,2},{1,3},{2,0},{3,1},{4,6},{5,7},{6,4},{7,5},{8,10},{9,11},{10,... | collective-permute-start | bytes 1277960 | tf_op jit(solution)/shard_map/ppermute | solution.py:12
  191.3 35.8 %collective-permute-start.28 = (bf16[832,256]{1,0:T(8,128)(2,1)}, bf16[832,256]{1,0:T(8,128)(2,1)S(1)}, u32[]{:S(2)}, u32[]{:S(2)}) collective-permute-start(bf16[832,256]{1,0:T(8,128)(2,1)} %convolution_convert_fusion.7), channel_id=1, source_target_pairs={{0,1},{1,0},{2,3},{3,2},{4,5},{5,4},{6,7},{7,6},{8,9},{9,8},{10,11... | collective-permute-start | bytes 1277960 | tf_op jit(solution)/shard_map/ppermute | solution.py:12
  191.3 35.8 %collective-permute-start.34 = (bf16[832,256]{1,0:T(8,128)(2,1)}, bf16[832,256]{1,0:T(8,128)(2,1)S(1)}, u32[]{:S(2)}, u32[]{:S(2)}) collective-permute-start(bf16[832,256]{1,0:T(8,128)(2,1)} %fusion.14), channel_id=1, source_target_pairs={{0,2},{1,3},{2,0},{3,1},{4,6},{5,7},{6,4},{7,5},{8,10},{9,11},{10,... | collective-permute-start | bytes 1277960 | tf_op jit(solution)/shard_map/ppermute | solution.py:12
  201.8 25.0 %collective-permute-start.44 = (bf16[1024,128]{1,0:T(8,128)(2,1)S(1)}, bf16[1024,128]{1,0:T(8,128)(2,1)S(1)}, u32[]{:S(2)}, u32[]{:S(2)}) collective-permute-start(bf16[1024,128]{1,0:T(8,128)(2,1)S(1)} %shard_map.80), channel_id=1, source_target_pairs={{0,1},{1,0},{2,3},{3,2},{4,5},{5,4},{6,7},{7,6},{8,9},{9,8},{10,11... | collective-permute-start | bytes 786440 | tf_op jit(solution)/shard_map/ppermute | solution.py:12
  226.9 14.7 %collective-permute-start.45 = (bf16[1024,128]{1,0:T(8,128)(2,1)S(1)}, bf16[1024,128]{1,0:T(8,128)(2,1)S(1)}, u32[]{:S(2)}, u32[]{:S(2)}) collective-permute-start(bf16[1024,128]{1,0:T(8,128)(2,1)S(1)} %fusion.28), channel_id=1, source_target_pairs={{0,2},{1,3},{2,0},{3,1},{4,6},{5,7},{6,4},{7,5},{8,10},{9,11},{10,... | collective-permute-start | bytes 786440 | tf_op jit(solution)/shard_map/ppermute | solution.py:12
  (52 other events, 388.9 us)

commit v3 on v2

v3 whole, which is shorter than its diff:
```python
import functools

import jax
import jax.numpy as jnp
from jax import lax
from jax.experimental import pallas as pl
from jax.experimental.pallas import tpu as pltpu
from jax.sharding import PartitionSpec as P


def flip(x, axis, size, mask):
    return lax.ppermute(x, axis, [(i, i ^ mask) for i in range(size)])


def bits(size, first=1):
    out = []
    while first < size:
        out.append(first)
        first *= 2
    return out


def after(value, *others):
    return lax.optimization_barrier((value,) + others)[0]


def pick_kernel(low, cuts, own_at, mate_at, mine, own, mate, own_up, mate_up, *refs):
    *downs, up, sems = refs
    moves = []
    for j in range(cuts[-1]):
        chunk = sum(j >= cut for cut in cuts[1:])
        for place, out, one, other in (
            (0, downs[chunk].at[j - cuts[chunk]], own, mate),
            (1, up.at[j], own_up, mate_up),
        ):
            sem = sems.at[2 * j + place]
            from_own = pltpu.make_async_copy(one.at[own_at[low + j]], out, sem)
            from_mate = pltpu.make_async_copy(other.at[mate_at[low + j]], out, sem)
            pl.when(mine[low + j] == 1)(from_own.start)
            pl.when(mine[low + j] != 1)(from_mate.start)
            moves.append(from_own)
    for move in moves:
        move.wait()


def pick_pages(lists, low, cuts, own, mate, own_up, mate_up):
    counts = [last - first for first, last in zip(cuts[:-1], cuts[1:])]
    return pl.pallas_call(
        functools.partial(pick_kernel, low, cuts),
        out_shape=[jax.ShapeDtypeStruct((count,) + own.shape[1:], own.dtype) for count in counts]
        + [jax.ShapeDtypeStruct((cuts[-1],) + own_up.shape[1:], own_up.dtype)],
        grid_spec=pltpu.PrefetchScalarGridSpec(
            num_scalar_prefetch=3,
            grid=(1,),
            in_specs=[pl.BlockSpec(memory_space=pl.ANY)] * 4,
            out_specs=[pl.BlockSpec((count,) + own.shape[1:], lambda i, *s: (0, 0, 0)) for count in counts]
            + [pl.BlockSpec((cuts[-1],) + own_up.shape[1:], lambda i, *s: (0, 0, 0, 0))],
            scratch_shapes=[pltpu.SemaphoreType.DMA((2 * cuts[-1],))],
        ),
        compiler_params=pltpu.CompilerParams(vmem_limit_bytes=32 << 20),
    )(*lists, own, mate, own_up, mate_up)


def blank(*shapes):
    return pl.pallas_call(
        lambda *refs: None,
        out_shape=list(shapes),
        out_specs=[pl.BlockSpec(memory_space=pl.ANY)] * len(shapes),
    )()


def side_kernel(weight, out):
    width = weight.shape[2]
    for which in range(2):
        out[0, :, which * width : (which + 1) * width] = weight[:, which, :]


def apart_kernel(weight, keys, values):
    keys[0], values[0] = weight[:, 0, :], weight[:, 1, :]


def side_by_side(at, weight, part, low, count, split=False):
    _, two, width = weight.shape
    wide = width if split else two * width
    outs = 2 if split else 1
    kernel = apart_kernel if split else side_kernel
    return pl.pallas_call(
        lambda at, *refs: kernel(*refs),
        out_shape=[jax.ShapeDtypeStruct((count, part, wide), weight.dtype)] * outs,
        grid_spec=pltpu.PrefetchScalarGridSpec(
            num_scalar_prefetch=1,
            grid=(count,),
            in_specs=[pl.BlockSpec((part, two, width), lambda j, at: (at[low + j], 0, 0))],
            out_specs=[pl.BlockSpec((1, part, wide), lambda j, at: (j, 0, 0))] * outs,
        ),
    )(at, weight)


def pack_kernel(first, at, place, x, straight, aside, picks):
    @pl.when(pl.program_id(0) == 0)
    def _():
        row = first + lax.broadcasted_iota(jnp.int32, picks.shape, 0)
        picks[...] = jnp.where(place[...] == row, 1.0, 0.0).astype(picks.dtype)

    packed = jnp.dot(picks[...], x[...], preferred_element_type=jnp.float32).astype(x.dtype)
    straight[...] = packed
    aside[...] = packed


def pack(place, x, at, part, first, last):
    rows, features = x.shape
    count = last - first
    if part % 128:
        pick = place[None, :] == jnp.arange(first, last, dtype=jnp.int32)[:, None]
        packed = jnp.dot(pick.astype(x.dtype), x, preferred_element_type=jnp.float32).astype(x.dtype)
        return packed, packed.reshape(count, -1, part)[:, at].reshape(count, features)
    return pl.pallas_call(
        functools.partial(pack_kernel, first),
        out_shape=[jax.ShapeDtypeStruct((count, features), x.dtype)] * 2,
        grid_spec=pltpu.PrefetchScalarGridSpec(
            num_scalar_prefetch=1,
            grid=(features // part,),
            in_specs=[
                pl.BlockSpec((1, rows), lambda j, at: (0, 0)),
                pl.BlockSpec((rows, part), lambda j, at: (0, j)),
            ],
            out_specs=[
                pl.BlockSpec((count, part), lambda j, at: (0, j)),
                pl.BlockSpec((count, part), lambda j, at: (0, at[j])),
            ],
            scratch_shapes=[pltpu.VMEM((count, rows), x.dtype)],
        ),
        compiler_params=pltpu.CompilerParams(vmem_limit_bytes=32 << 20),
    )(at, place.reshape(1, rows), x)


def multiply_kernel(parts, adds, x, *refs):
    weights, refs = refs[:parts], refs[parts:]
    added, outs = refs[: len(adds)], refs[len(adds) :]
    width = outs[0].shape[1]
    total, low = None, 0
    for weight in weights:
        high = low + weight.shape[0]
        piece = jnp.dot(x[:, low:high], weight[...], preferred_element_type=jnp.float32)
        total, low = piece if total is None else total + piece, high
    for i, out in enumerate(outs):
        value = total[:, i * width : (i + 1) * width]
        for ref, which in zip(added, adds):
            if which == i:
                value = value + ref[...].astype(jnp.float32)
        out[...] = value.astype(out.dtype)


def multiply(x, weights, width, added, dtype):
    rows, features = x.shape
    block = rows // 4 if rows % 64 == 0 else rows
    outs = weights[0].shape[1] // width
    adds = [(i, value) for i, values in enumerate(added) for value in values]
    piece = pl.BlockSpec((block, width), lambda j: (j, 0))
    return pl.pallas_call(
        functools.partial(multiply_kernel, len(weights), [i for i, _ in adds]),
        out_shape=[jax.ShapeDtypeStruct((rows, width), dtype)] * outs,
        grid=(rows // block,),
        in_specs=[pl.BlockSpec((block, features), lambda j: (j, 0))]
        + [pl.BlockSpec(weight.shape, lambda j: (0, 0)) for weight in weights]
        + [piece] * len(adds),
        out_specs=[piece] * outs,
        compiler_params=pltpu.CompilerParams(vmem_limit_bytes=40 << 20),
    )(x, *weights, *[value for _, value in adds])


def shrink_kernel(count, tiles, kind, places, x, *refs):
    pools, (out, pages, sems) = refs[:count], refs[count:]
    tile_rows = x.shape[0] // tiles
    for t in range(tiles):
        for number, pool in enumerate(pools):
            move = pltpu.make_async_copy(pool.at[places[t]], pages.at[t], sems.at[t])
            pl.when(kind[t] == number)(move.start)
    for t in range(tiles):
        pltpu.make_async_copy(pools[0].at[0], pages.at[t], sems.at[t]).wait()
        rows = pl.ds(t * tile_rows, tile_rows)
        out[rows, :] = jnp.dot(
            x[rows, :], pages[t], preferred_element_type=jnp.float32
        ).astype(out.dtype)


def tile_shrink(kind, places, rows, pools, tiles):
    features, columns = pools[0].shape[1:]
    return pl.pallas_call(
        functools.partial(shrink_kernel, len(pools), tiles),
        out_shape=jax.ShapeDtypeStruct((rows.shape[0], columns), jnp.bfloat16),
        grid_spec=pltpu.PrefetchScalarGridSpec(
            num_scalar_prefetch=2,
            grid=(1,),
            in_specs=[pl.BlockSpec(rows.shape, lambda i, *s: (0, 0))]
            + [pl.BlockSpec(memory_space=pl.ANY)] * len(pools),
            out_specs=pl.BlockSpec((rows.shape[0], columns), lambda i, *s: (0, 0)),
            scratch_shapes=[
                pltpu.VMEM((tiles, features, columns), pools[0].dtype),
                pltpu.SemaphoreType.DMA((tiles,)),
            ],
        ),
        compiler_params=pltpu.CompilerParams(vmem_limit_bytes=32 << 20),
    )(kind, places, rows, *pools)


def finish_kernel(count, terms, offsets, live, kind, places, *refs):
    keys, values, more_keys, more_values = refs[:4]
    parts, pools = refs[4 : 4 + terms], refs[4 + terms : 4 + terms + count]
    out, held, ups, sems = refs[4 + terms + count :]
    t = pl.program_id(0)
    tiles = ups.shape[0]
    tile_rows, two, width = out.shape
    half = ups.shape[2]
    room, rest = keys.shape[0], more_keys.shape[0]

    @pl.when(t == 0)
    def _():
        for tile in range(tiles):
            for number, pool in enumerate(pools):
                move = pltpu.make_async_copy(pool.at[places[tile]], ups.at[tile], sems.at[tile])
                pl.when(kind[tile] == number)(move.start)
        for which, (first, second) in enumerate(((keys, more_keys), (values, more_values))):
            held[which, :room] = first[...]
            held[which, room : room + rest] = second[...]
            held[which, room + rest :] = jnp.zeros((tile_rows, width), jnp.float32)

    pltpu.make_async_copy(pools[0].at[0], ups.at[t], sems.at[t]).wait()
    low = pl.multiple_of((offsets[t] // 8) * 8, 8)
    shift = offsets[t] % 8
    alive = lax.broadcasted_iota(jnp.int32, (tile_rows, width), 0) < live[t]
    shrink = parts[0][...].astype(jnp.float32)
    for part in parts[1:]:
        shrink = shrink + part[...].astype(jnp.float32)
    shrink = shrink.astype(jnp.bfloat16)
    for which in range(2):
        expand = jnp.dot(
            shrink[:, which * half : (which + 1) * half],
            ups[t, which],
            preferred_element_type=jnp.float32,
        )
        wide = held[which, pl.ds(low, tile_rows + 8), :]
        base = pltpu.roll(wide, tile_rows + 8 - shift, 0)[:tile_rows]
        out[:, which, :] = jnp.where(alive, base + expand, 0.0).astype(out.dtype)


def finish(offsets, live, kind, places, totals, rest, parts, pools):
    tiles = offsets.shape[0]
    rows, columns = parts[0].shape
    tile_rows = rows // tiles
    width = totals[0].shape[1]

    def whole(array):
        return pl.BlockSpec(array.shape, lambda t, *s: (0, 0))

    return pl.pallas_call(
        functools.partial(finish_kernel, len(pools), len(parts)),
        out_shape=jax.ShapeDtypeStruct((rows, 2, width), jnp.bfloat16),
        grid_spec=pltpu.PrefetchScalarGridSpec(
            num_scalar_prefetch=4,
            grid=(tiles,),
            in_specs=[whole(array) for array in (*totals, *rest)]
            + [pl.BlockSpec((tile_rows, columns), lambda t, *s: (t, 0))] * len(parts)
            + [pl.BlockSpec(memory_space=pl.ANY)] * len(pools),
            out_specs=pl.BlockSpec((tile_rows, 2, width), lambda t, *s: (t, 0, 0)),
            scratch_shapes=[
                pltpu.VMEM((2, rows + tile_rows, width), jnp.float32),
                pltpu.VMEM((tiles,) + pools[0].shape[1:], pools[0].dtype),
                pltpu.SemaphoreType.DMA((tiles,)),
            ],
        ),
        compiler_params=pltpu.CompilerParams(vmem_limit_bytes=48 << 20),
    )(offsets, live, kind, places, *totals, *rest, *parts, *pools)


def on_device(
    input_rows,
    key_value_weight,
    adapter_down_weight,
    adapter_up_weight,
    tile_page_index,
    tile_live_rows,
):
    groups = lax.axis_size("groups")
    ranks = lax.axis_size("dp")
    shares = lax.axis_size("tensor")
    group = lax.axis_index("groups")
    rank = lax.axis_index("dp")
    share = lax.axis_index("tensor")
    chips = ranks // 2
    chip, core = rank // 2, rank % 2
    tiles = tile_live_rows.shape[0]
    local_pages = adapter_down_weight.shape[0]
    chip_pages = 2 * local_pages
    capacity = max(2, (2 * tiles + ranks - 1) // ranks)
    most_slots = 2 * capacity
    rows, features = input_rows.shape
    tile_rows = rows // tiles
    column_width = key_value_weight.shape[2]
    half = adapter_down_weight.shape[2] // 2

    columns = 2 * column_width
    plane = groups * ranks
    part = features // plane

    line = []

    def ready(value):
        return after(value, line[-1]) if line else value

    def mark(value):
        line.append(jax.tree.leaves(value)[0])
        return value

    def wait(value):
        return mark(ready(value))

    mate_up = flip(adapter_up_weight, "dp", ranks, 1)
    mate_down = flip(adapter_down_weight, "dp", ranks, 1)

    steps = [("dp", ranks, m, (rank // m) % 2) for m in bits(ranks, 2)]
    steps += [("groups", groups, m, (group // m) % 2) for m in bits(groups)]
    steps += [("dp", ranks, 1, core)]
    over_chips = len(bits(ranks, 2))
    last_step = len(steps) - 1
    spot = sum(bit << i for i, (_, _, _, bit) in enumerate(steps))
    turns = list(range(shares - 1, 0, -1))
    order = spot ^ jnp.arange(plane, dtype=jnp.int32)
    entries = [(turns[0], 0)] + [(k, i) for k in turns[1:] for i in range(chips)]
    starts = (share ^ jnp.array([k for k, _ in entries], jnp.int32)) * plane + (
        spot ^ jnp.array([i for _, i in entries], jnp.int32)
    )
    pieces = mark(side_by_side(starts, key_value_weight, part, 0, 1, split=True))
    weights = {}
    for which in range(2):
        weights[turns[0], which] = flip(pieces[which][0], "tensor", shares, turns[0])
    first_keys = list(weights)
    for k in turns[1:]:
        piece = mark(
            side_by_side(starts, ready(key_value_weight), part, entries.index((k, 0)), chips)
        )[0]
        weights[k, 2] = flip(piece.reshape(chips * part, columns), "tensor", shares, k)
    later_keys = list(weights)[2:]
    moving = {}

    def begin(key, step):
        axis, size, m, _ = steps[step]
        moving[key, step] = flip(weights[key], axis, size, m)

    def end(key, step):
        got = wait(moving.pop((key, step)))
        weights[key] = mark(jnp.concatenate([weights[key], got]))

    def begin_last(key):
        begin(key, last_step - 1)
        begin(key, last_step)

    def go_on(key):
        got = wait(moving.pop((key, last_step - 1)))
        axis, size, m, _ = steps[last_step]
        gathered[key] = [weights[key], got, moving.pop((key, last_step)), flip(got, axis, size, m)]

    def get_all(key):
        gathered[key] = gathered[key][:2] + [wait(value) for value in gathered[key][2:]]
        return gathered[key]

    gathered = {}
    arrived = {}

    def lowest(k):
        return k & -k if k else shares

    def take(k, which, arrived):
        return [arrived.pop((k + m, which)) for m in bits(lowest(k))]

    table = tile_page_index.reshape(chips, 2 * tiles)
    page_range = jnp.arange(ranks * local_pages, dtype=jnp.int32)
    need = jnp.any(table[:, :, None] == page_range[None, None, :], axis=1)
    need = need.reshape(chips, chips, chip_pages)
    position = jnp.cumsum(need.astype(jnp.int32), axis=2) - 1
    usual = -(-5 * most_slots // 8)
    more = -(-6 * most_slots // 8)
    cuts = [0, max(1, usual // 5), max(2, 3 * usual // 5), usual]
    firsts = [0, 2 * usual, 2 * more, 2 * most_slots]
    most_pages = jnp.max(
        jnp.where(jnp.eye(chips, dtype=jnp.bool_), 0, position[:, :, -1] + 1)
    )
    slot_range = jnp.arange(2 * most_slots, dtype=jnp.int32)
    chip_range = jnp.arange(chip_pages, dtype=jnp.int32)

    offsets = jnp.cumsum(tile_live_rows) - tile_live_rows
    live_total = jnp.sum(tile_live_rows)
    live = jnp.arange(tile_rows, dtype=jnp.int32)[None, :] < tile_live_rows[:, None]
    packed_place = offsets[:, None] + jnp.arange(tile_rows, dtype=jnp.int32)[None, :]
    packed_place = jnp.where(live, packed_place, -1).reshape(rows)
    room = -(-13 * rows // 256) * 16

    listed = []
    for offset in range(1, chips):
        wanted = need[chip ^ offset, chip]
        place = position[chip ^ offset, chip]
        listed.append(
            jnp.sum(
                jnp.where(
                    wanted[None, :] & (place[None, :] == slot_range[:, None]), chip_range[None, :], 0
                ),
                axis=1,
            )
        )
    sent_lists = []
    for offset in range(1, chips):
        halves = [
            listed[offset - 1][low:high].reshape(2, (high - low) // 2)
            for low, high in zip(firsts[:-1], firsts[1:])
        ]
        halves = jnp.concatenate(halves, axis=1)
        sent = jnp.where(core == 0, halves[0], halves[1])
        mine = ((sent // local_pages) == core).astype(jnp.int32)
        at = sent % local_pages
        sent_lists.append((at * mine, at * (1 - mine), mine))

    for key in first_keys:
        weights[key] = wait(weights[key])
        begin(key, 0) if over_chips else begin_last(key)
    mate_up, mate_down = wait(mate_up), wait(mate_down)
    pools = [adapter_down_weight, mate_down]
    pool_of = {}
    crossing = {}
    picked = [
        mark(
            pick_pages(
                lists, 0, cuts, adapter_down_weight, ready(mate_down), adapter_up_weight, mate_up
            )
        )
        for lists in sent_lists
    ]
    near_ups = [flip(up, "dp", ranks, 2 * (i + 1)) for i, (*_, up) in enumerate(picked)]

    def cross(i):
        for offset in range(1, chips):
            crossing[offset, i] = flip(ready(picked[offset - 1][i]), "dp", ranks, 2 * offset)

    def share_pages(i):
        for offset in range(1, chips):
            got = wait(crossing[offset, i])
            pool_of[offset, i] = len(pools)
            pools.extend([got, flip(got, "dp", ranks, 1)])

    cross(0)
    for step in range(over_chips):
        for key in first_keys:
            end(key, step)
            begin(key, step + 1) if step + 1 < over_chips else begin_last(key)
    packed, aside = pack(packed_place, ready(input_rows), order, part, 0, room)
    mark(aside)
    near_up = jnp.concatenate([wait(up) for up in near_ups])
    up_pools = [adapter_up_weight, mate_up, near_up, flip(near_up, "dp", ranks, 1)]
    cross(1)
    for key in first_keys:
        go_on(key)
    for key in later_keys[:1]:
        weights[key] = wait(weights[key])
        begin_last(key)

    for key in first_keys:
        (sent,) = multiply(ready(aside), get_all(key), column_width, [[]], jnp.bfloat16)
        arrived[key] = flip(mark(sent), "tensor", shares, lowest(key[0]))
    share_pages(0)
    cross(2)
    at = share * plane + jnp.arange(plane, dtype=jnp.int32)
    for i, key in enumerate(later_keys):
        go_on(key)
        if i + 1 < len(later_keys):
            following = later_keys[i + 1]
            weights[following] = wait(weights[following])
            begin_last(following)
        held = get_all(key)
        if i == 0:
            own = mark(side_by_side(at, ready(key_value_weight), part, 0, plane)[0])
            own = own.reshape(features, columns)
        added = [[wait(value) for value in take(key[0], which, arrived)] for which in range(2)]
        sent = mark(multiply(ready(aside), held, column_width, added, jnp.bfloat16))
        for which in range(2):
            arrived[key[0], which] = flip(sent[which], "tensor", shares, lowest(key[0]))
        if i + 2 == len(later_keys):
            share_pages(1)
    added = [[wait(value) for value in take(0, which, arrived)] for which in range(2)]
    totals = mark(multiply(ready(packed), [own], column_width, added, jnp.float32))
    share_pages(2)

    def project_rest(operands):
        x, gathered, own = operands
        packed, aside = pack(packed_place, x, order, part, room, rows)
        arrived = {}
        for key in first_keys + later_keys:
            halves = [key[1]] if key in first_keys else [0, 1]
            added = [take(key[0], which, arrived) for which in halves]
            sent = multiply(aside, gathered[key], column_width, added, jnp.bfloat16)
            for which, value in zip(halves, sent):
                arrived[key[0], which] = flip(value, "tensor", shares, lowest(key[0]))
        added = [take(0, which, arrived) for which in range(2)]
        return multiply(packed, [own], column_width, added, jnp.float32)

    rest_shape = jax.ShapeDtypeStruct((rows - room, column_width), jnp.float32)
    rest = lax.cond(
        live_total > room,
        project_rest,
        lambda operands: blank(rest_shape, rest_shape),
        (input_rows, gathered, own),
    )

    for stage in (1, 2):

        def send_more(sources):
            low, count = firsts[stage] // 2, (firsts[stage + 1] - firsts[stage]) // 2
            got = []
            for offset in range(1, chips):
                down, up = pick_pages(sent_lists[offset - 1], low, [0, count], *sources)
                got.append((flip(down, "dp", ranks, 2 * offset), flip(up, "dp", ranks, 2 * offset)))
            down = jnp.concatenate([pair[0] for pair in got])
            up = jnp.concatenate([pair[1] for pair in got])
            return down, flip(down, "dp", ranks, 1), up, flip(up, "dp", ranks, 1)

        def send_none(sources):
            own_down, _, own_up, _ = sources
            count = (chips - 1) * (firsts[stage + 1] - firsts[stage]) // 2
            down = jax.ShapeDtypeStruct((count,) + own_down.shape[1:], own_down.dtype)
            up = jax.ShapeDtypeStruct((count,) + own_up.shape[1:], own_up.dtype)
            return tuple(blank(down, down, up, up))

        if firsts[stage + 1] > firsts[stage]:
            near, far, near_up, far_up = lax.cond(
                most_pages > firsts[stage],
                send_more,
                send_none,
                (adapter_down_weight, mate_down, adapter_up_weight, mate_up),
            )
            pool_of[stage] = len(pools)
            pools += [near, far]
            up_pools += [near_up, far_up]

    pages = tile_page_index.reshape(ranks, tiles)[rank]
    owner = pages // local_pages
    owner_chip = owner // 2
    step = owner_chip ^ chip
    entry = position[chip, owner_chip, pages % chip_pages]
    kind = jnp.where(owner == rank, 0, 1)
    places = pages % local_pages
    up_kind, up_places = kind, places
    for stage in range(3):
        count = (firsts[stage + 1] - firsts[stage]) // 2
        if count == 0:
            continue
        here = (owner_chip != chip) & (entry >= firsts[stage])
        sender, at = (entry - firsts[stage]) // count, (entry - firsts[stage]) % count
        far = (sender != core).astype(jnp.int32)
        up_kind = jnp.where(here, 2 + 2 * stage + far, up_kind)
        up_places = jnp.where(here, (step - 1) * count + at, up_places)
        if stage:
            kind = jnp.where(here, pool_of[stage] + far, kind)
            places = jnp.where(here, (step - 1) * count + at, places)
            continue
        for offset in range(1, chips):
            for i in range(3):
                chosen = here & (step == offset) & (at >= cuts[i])
                kind = jnp.where(chosen, pool_of[offset, i] + far, kind)
                places = jnp.where(chosen, at - cuts[i], places)

    shrink = tile_shrink(
        kind.astype(jnp.int32), places.astype(jnp.int32), input_rows, pools, tiles
    )
    parts = [shrink]
    for m in bits(shares):
        sent = sum(value.astype(jnp.float32) for value in parts).astype(jnp.bfloat16)
        parts.append(flip(sent, "tensor", shares, m))
    return finish(
        offsets,
        tile_live_rows,
        up_kind.astype(jnp.int32),
        up_places.astype(jnp.int32),
        totals,
        rest,
        parts,
        up_pools,
    )


def solution(mesh):
    return jax.shard_map(
        on_device,
        mesh=mesh,
        in_specs=(
            P(("groups", "dp"), "tensor"),
            P(None, None, "tensor"),
            P("dp", "tensor", None),
            P("dp", None, None, "tensor"),
            P("groups"),
            P(("groups", "dp")),
        ),
        out_specs=P(("groups", "dp"), None, "tensor"),
        check_vma=False,
    )
```

time: 250 us -> 186 us (0.74)
  waiting for transfers between devices: 90.6 us -> 65.8 us
  other arithmetic: 27.9 us -> 4.49 us
  matrix products: 21.6 us -> 0 us
  Pallas kernels: 39.4 us -> 58.1 us
  local copies, waits for them, and re-layouts: 23.1 us -> 5.26 us
  starting transfers between devices: 42.5 us -> 47.1 us
    ppermute x34 -> x36, waiting for transfers between devices: 90.6 us -> 65.8 us  [flip(): return lax.ppermute(x, axis, [(i, i ^ mask) for i in range(size)])]
    dot_general x9 -> x0, matrix products: 21.6 us -> none  [the longest x6 13.1 us: project(): jnp.dot(packed, weight_of(weights, k, which), preferred_element_type=jnp....]
    pallas_call x9 -> x16, Pallas kernels: 39.4 us -> 58.1 us  [the longest x4 18.2 us: side_by_side(): pl.pallas_call(lambda at, *refs: kernel(*refs), out_shape=[jax.ShapeDtype...]
    select_n x13 -> x1, other arithmetic: 9.6 us -> 0.01 us  [on_device(): up_kind = jnp.where(here, 2 + 2 * stage + far, up_kind)]
    concatenate x13 -> x0, other arithmetic: 9.23 us -> none  [the longest x12 7.7 us: spread(): jnp.concatenate([jnp.where(bit == 1, got, held), jnp.where(bit == 1, held...]
    another operation x10 -> x0, local copies, waits for them, and re-layouts: 7.33 us -> none
    unnamed x89 -> x48, local copies, waits for them, and re-layouts: 9.15 us -> 3.77 us
    ppermute x34 -> x36, starting transfers between devices: 42.5 us -> 47.1 us  [flip(): return lax.ppermute(x, axis, [(i, i ^ mask) for i in range(size)])]
  transfers between devices with their start and end apart: 34 -> 36, of which waited for: 12 -> 9; matrix products, arithmetic and copies ran while one was open for 27% -> 3% of each run, Pallas kernels for 14% -> 25%
where the time goes in v3:
time: 186 us; the launch traced here: 183 us
  waiting for transfers between devices  65.8 us (35%)
  Pallas kernels  58.1 us (31%)
  starting transfers between devices  47.1 us (25%)
  local copies, waits for them, and re-layouts  5.26 us (3%)
  other arithmetic  4.49 us (2%)
  between operations  2.48 us (1%)
    ppermute x36, waiting for transfers between devices, flip(): return lax.ppermute(x, axis, [(i, i ^ mask) for i in range(size)])  65.8 us
    ppermute x36, starting transfers between devices, flip(): return lax.ppermute(x, axis, [(i, i ^ mask) for i in range(size)])  47.1 us
    pallas_call x4, Pallas kernels, side_by_side(): pl.pallas_call(lambda at, *refs: kernel(*refs), out_shape=[jax.ShapeDtype...  18.2 us
    pallas_call x5, Pallas kernels, multiply(): pl.pallas_call(functools.partial(multiply_kernel, len(weights), [i for i,...  15.8 us
    pallas_call x1, Pallas kernels, pack(): pl.pallas_call(functools.partial(pack_kernel, first), out_shape=[jax.Shap...  7.24 us
    pallas_call x1, Pallas kernels, finish(): pl.pallas_call(functools.partial(finish_kernel, len(pools), len(parts)),...  6.74 us
    pallas_call x1, Pallas kernels, tile_shrink(): pl.pallas_call(functools.partial(shrink_kernel, len(pools), tiles), out_s...  6.16 us
    pallas_call x1, Pallas kernels, pick_pages(): pl.pallas_call(functools.partial(pick_kernel, low, cuts), out_shape=[jax....  3.94 us
  transfers between devices with their start and end apart: 36, of which 9 were waited for; matrix products, arithmetic and copies ran while one was open for 3% of the time, Pallas kernels for 25%

profile of v3, /device:TPU:3, one launch (start us, length us, event | category | flops | bytes accessed | tf_op | source)
XLA Modules:
  0.0 183.3 jit_solution(8438917005523366020)
XLA Ops:
  1.9 2.9 %shard_map.82 = (bf16[1,256,256]{2,1,0:T(8,128)(2,1)}, bf16[1,256,256]{2,1,0:T(8,128)(2,1)}) custom-call(s32[5]{0:T(128)} %xor_add_fusion.at, bf16[8192,2,256]{2,1,0:T(2,128)(2,1)} %refs_0_.5), custom_call_target="tpu_custom_call" | custom-call | tf_op jit(solution)/shard_map/pallas_call | solution.py:87
  4.8 3.3 %collective-permute-start.14 = (bf16[256,256]{1,0:T(8,128)(2,1)}, bf16[256,256]{1,0:T(8,128)(2,1)S(1)}, u32[]{:S(2)}, u32[]{:S(2)}) collective-permute-start(bf16[256,256]{1,0:T(8,128)(2,1)} %bitcast.67), channel_id=1, source_target_pairs={{0,3},{1,2},{2,1},{3,0},{4,7},{5,6},{6,5},{7,4},{8,11},{9,10},{10,... | collective-permute-start | bytes 393224 | tf_op jit(solution)/shard_map/ppermute | solution.py:12
  8.7 3.5 %shard_map.83 = bf16[2,256,512]{2,1,0:T(8,128)(2,1)} custom-call(s32[5]{0:T(128)} %xor_add_fusion.at, bf16[8192,2,256]{2,1,0:T(2,128)(2,1)} %refs_0_.5), custom_call_target="tpu_custom_call" | custom-call | tf_op jit(solution)/shard_map/pallas_call | solution.py:87
  13.8 3.4 %shard_map.84 = bf16[2,256,512]{2,1,0:T(8,128)(2,1)} custom-call(s32[5]{0:T(128)} %xor_add_fusion.at, bf16[8192,2,256]{2,1,0:T(2,128)(2,1)} %refs_0_.5), custom_call_target="tpu_custom_call" | custom-call | tf_op jit(solution)/shard_map/pallas_call | solution.py:87
  20.0 3.9 %shard_map.85 = (bf16[1,2048,128]{2,1,0:T(8,128)(2,1)S(1)}, bf16[2,2048,128]{2,1,0:T(8,128)(2,1)}, bf16[2,2048,128]{2,1,0:T(8,128)(2,1)S(1)}, bf16[5,2,64,256]{3,2,1,0:T(8,128)(2,1)S(1)}) custom-call(s32[8]{0:T(128)S(1)} %compare_select_fusion.19.own_at, s32[8]{0:T(128)S(1)} %get-tuple-element.270.mate_at, s32[8]{0:T(128)S(1)} %get-tuple-element.271.mine, ...), custom_call_target="tpu_custom_call" | custom-call | tf_op jit(solution)/shard_map/pallas_call | solution.py:48
  29.0 7.2 %shard_map.86 = (bf16[832,2048]{1,0:T(8,128)(2,1)S(1)}, bf16[832,2048]{1,0:T(8,128)(2,1)S(1)}) custom-call(s32[8]{0:T(128)S(1)} %iota_xor_fusion.at, s32[1,1024]{1,0:T(1,128)S(1)} %bitcast.61, bf16[1024,2048]{1,0:T(8,128)(2,1)S(1)} %copy-done.6), custom_call_target="tpu_custom_call" | custom-call | tf_op jit(solution)/shard_map/pallas_call | solution.py:117
  39.3 2.9 %collective-permute-done.20.refs_0_ = bf16[512,512]{1,0:T(8,128)(2,1)} collective-permute-done((bf16[512,512]{1,0:T(8,128)(2,1)}, bf16[512,512]{1,0:T(8,128)(2,1)}, u32[]{:S(2)}, u32[]{:S(2)}) %collective-permute-start.20) | collective-permute-done | bytes 524320 | tf_op jit(solution)/shard_map/ppermute | solution.py:12
  43.9 10.7 %collective-permute-start.34 = (bf16[512,512]{1,0:T(8,128)(2,1)S(1)}, bf16[512,512]{1,0:T(8,128)(2,1)}, u32[]{:S(2)}, u32[]{:S(2)}) collective-permute-start(bf16[512,512]{1,0:T(8,128)(2,1)S(1)} %bitcast.65), channel_id=1, source_target_pairs={{0,1},{1,0},{2,3},{3,2},{4,5},{5,4},{6,7},{7,6},{8,9},{9,8},{10,11... | collective-permute-start | bytes 1572872 | tf_op jit(solution)/shard_map/ppermute | solution.py:12
  58.3 2.5 %shard_map.88 = bf16[832,256]{1,0:T(8,128)(2,1)} custom-call(bf16[832,2048]{1,0:T(8,128)(2,1)S(1)} %get-tuple-element.242.x, bf16[512,256]{1,0:T(8,128)(2,1)S(1)} %constant_dynamic-update-slice_fusion.2.refs_0_, bf16[512,256]{1,0:T(8,128)(2,1)S(1)} %collective-permute-done.21.refs_1_, bf16[512,256]{1,0:T(8,128)(2,1)S(1)} %collective-permute-done.26.refs_2_, ...), custom_call_target="tpu_custom_call" | custom-call | tf_op jit(solution)/shard_map/pallas_call | solution.py:160
  60.9 5.2 %collective-permute-done.34.refs_0_ = bf16[512,512]{1,0:T(8,128)(2,1)} collective-permute-done((bf16[512,512]{1,0:T(8,128)(2,1)S(1)}, bf16[512,512]{1,0:T(8,128)(2,1)}, u32[]{:S(2)}, u32[]{:S(2)}) %collective-permute-start.34) | collective-permute-done | bytes 524320 | tf_op jit(solution)/shard_map/ppermute | solution.py:12
  69.9 8.4 %shard_map.89 = bf16[8,256,512]{2,1,0:T(8,128)(2,1)} custom-call(s32[8]{0:T(128)} %iota_add_fusion.at, bf16[8192,2,256]{2,1,0:T(2,128)(2,1)} %refs_0_.5), custom_call_target="tpu_custom_call" | custom-call | tf_op jit(solution)/shard_map/pallas_call | solution.py:87
  78.3 3.9 %collective-permute-start.39 = (bf16[512,512]{1,0:T(8,128)(2,1)}, bf16[512,512]{1,0:T(8,128)(2,1)S(1)}, u32[]{:S(2)}, u32[]{:S(2)}) collective-permute-start(bf16[512,512]{1,0:T(8,128)(2,1)} %collective-permute-done.34.refs_0_), channel_id=1, source_target_pairs={{0,4},{4,0},{8,12},{12,8},{1,5},{5,1},{9,13},{13,9},{2,6},{6,2},{1... | collective-permute-start | bytes 1572872 | tf_op jit(solution)/shard_map/ppermute | solution.py:12
  82.2 4.1 %collective-permute-done.28.refs_5_ = bf16[832,256]{1,0:T(8,128)(2,1)} collective-permute-done((bf16[832,256]{1,0:T(8,128)(2,1)}, bf16[832,256]{1,0:T(8,128)(2,1)}, u32[]{:S(2)}, u32[]{:S(2)}) %collective-permute-start.28) | collective-permute-done | bytes 426016 | tf_op jit(solution)/shard_map/ppermute | solution.py:12
  86.3 4.5 %shard_map.90 = (bf16[832,256]{1,0:T(8,128)(2,1)S(1)}, bf16[832,256]{1,0:T(8,128)(2,1)S(1)}) custom-call(bf16[832,2048]{1,0:T(8,128)(2,1)S(1)} %get-tuple-element.242.x, bf16[512,512]{1,0:T(8,128)(2,1)} %collective-permute-done.20.refs_0_, bf16[512,512]{1,0:T(8,128)(2,1)} %collective-permute-done.30.refs_1_, ...), custom_call_target="tpu_custom_call" | custom-call | tf_op jit(solution)/shard_map/pallas_call | solution.py:160
  90.8 2.8 %collective-permute-start.38 = (bf16[512,512]{1,0:T(8,128)(2,1)}, bf16[512,512]{1,0:T(8,128)(2,1)S(1)}, u32[]{:S(2)}, u32[]{:S(2)}) collective-permute-start(bf16[512,512]{1,0:T(8,128)(2,1)} %collective-permute-done.36.refs_1_), channel_id=1, source_target_pairs={{0,4},{4,0},{8,12},{12,8},{1,5},{5,1},{9,13},{13,9},{2,6},{6,2},{1... | collective-permute-start | bytes 1572872 | tf_op jit(solution)/shard_map/ppermute | solution.py:12
  95.4 3.9 %shard_map.91 = (bf16[832,256]{1,0:T(8,128)(2,1)S(1)}, bf16[832,256]{1,0:T(8,128)(2,1)S(1)}) custom-call(bf16[832,2048]{1,0:T(8,128)(2,1)S(1)} %get-tuple-element.242.x, bf16[512,512]{1,0:T(8,128)(2,1)} %collective-permute-done.34.refs_0_, bf16[512,512]{1,0:T(8,128)(2,1)} %collective-permute-done.36.refs_1_, ...), custom_call_target="tpu_custom_call" | custom-call | tf_op jit(solution)/shard_map/pallas_call | solution.py:160
  103.1 16.2 %collective-permute-done.42.refs_1_ = bf16[832,256]{1,0:T(8,128)(2,1)S(1)} collective-permute-done((bf16[832,256]{1,0:T(8,128)(2,1)S(1)}, bf16[832,256]{1,0:T(8,128)(2,1)S(1)}, u32[]{:S(2)}, u32[]{:S(2)}) %collective-permute-start.42) | collective-permute-done | bytes 426016 | tf_op jit(solution)/shard_map/ppermute | solution.py:12
  121.4 16.2 %collective-permute-done.40.refs_3_ = bf16[832,256]{1,0:T(8,128)(2,1)S(1)} collective-permute-done((bf16[832,256]{1,0:T(8,128)(2,1)S(1)}, bf16[832,256]{1,0:T(8,128)(2,1)S(1)}, u32[]{:S(2)}, u32[]{:S(2)}) %collective-permute-start.40) | collective-permute-done | bytes 426016 | tf_op jit(solution)/shard_map/ppermute | solution.py:12
  137.6 2.5 %shard_map.92 = (f32[832,256]{1,0:T(8,128)S(1)}, f32[832,256]{1,0:T(8,128)S(1)}) custom-call(bf16[832,2048]{1,0:T(8,128)(2,1)S(1)} %copy-done.1, bf16[2048,512]{1,0:T(8,128)(2,1)S(1)} %bitcast.64, bf16[832,256]{1,0:T(8,128)(2,1)S(1)} %collective-permute-done.42.refs_1_, bf16[832,256]{1,0:T(8,128)(2,1)S(1)} %collective-permute-done.41.refs_2_, ...), custom_call_target="tpu_custom_call" | custom-call | tf_op jit(solution)/shard_map/pallas_call | solution.py:160
  141.0 3.4 %collective-permute-start.46 = (bf16[2,2048,128]{2,1,0:T(8,128)(2,1)}, bf16[2,2048,128]{2,1,0:T(8,128)(2,1)S(1)}, u32[]{:S(2)}, u32[]{:S(2)}) collective-permute-start(bf16[2,2048,128]{2,1,0:T(8,128)(2,1)} %collective-permute-done.45.refs_6_), channel_id=1, source_target_pairs={{0,4},{4,0},{8,12},{12,8},{1,5},{5,1},{9,13},{13,9},{2,6},{6,2},{1... | collective-permute-start | bytes 3145736 | tf_op jit(solution)/shard_map/ppermute | solution.py:12
  147.9 6.2 %shard_map.93.refs_4_ = bf16[1024,128]{1,0:T(8,128)(2,1)S(1)} custom-call(s32[8]{0:T(128)S(1)} %get-tuple-element.268.kind, s32[8]{0:T(128)S(1)} %get-tuple-element.265.places, bf16[1024,2048]{1,0:T(8,128)(2,1)} %x.2, bf16[16,2048,128]{2,1,0:T(8,128)(2,1)} %refs_0_.6, bf16[16,2048,128]{2,1,0:T(8,128)(2,1)} %collective-permute-done.18.mate.refs_1_, ...), custom_call_target="tpu_custom_call" | custom-call | tf_op jit(solution)/shard_map/pallas_call | solution.py:189
  155.7 5.9 %collective-permute-done.47.refs_5_ = bf16[1024,128]{1,0:T(8,128)(2,1)S(1)} collective-permute-done((bf16[1024,128]{1,0:T(8,128)(2,1)S(1)}, bf16[1024,128]{1,0:T(8,128)(2,1)S(1)}, u32[]{:S(2)}, u32[]{:S(2)}) %collective-permute-start.47) | collective-permute-done | bytes 262176 | tf_op jit(solution)/shard_map/ppermute | solution.py:12
  163.1 13.3 %collective-permute-done.48.refs_6_ = bf16[1024,128]{1,0:T(8,128)(2,1)S(1)} collective-permute-done((bf16[1024,128]{1,0:T(8,128)(2,1)S(1)}, bf16[1024,128]{1,0:T(8,128)(2,1)S(1)}, u32[]{:S(2)}, u32[]{:S(2)}) %collective-permute-start.48) | collective-permute-done | bytes 262176 | tf_op jit(solution)/shard_map/ppermute | solution.py:12
  176.4 6.7 %shard_map.94 = bf16[1024,2,256]{2,1,0:T(2,128)(2,1)} custom-call(s32[8]{0:T(128)S(1)} %get-tuple-element.276.offsets, s32[8]{0:T(128)S(1)} %copy-done.4, s32[8]{0:T(128)S(1)} %select_select_fusion.3.kind, s32[8]{0:T(128)S(1)} %get-tuple-element.274.places, f32[832,256]{1,0:T(8,128)S(1)} %get-tuple-element.250.refs_0_, f32[832,256]{1,0:T(8,128)S(1)} %copy-done.3, ...), custom_call_target="tpu_custom_call" | custom-call | tf_op jit(solution)/shard_map/pallas_call | solution.py:256
  (152 shorter events, 37.4 us)
Async XLA Ops:
  0.0 19.9 %collective-permute-start.18 = (bf16[16,2048,128]{2,1,0:T(8,128)(2,1)}, bf16[16,2048,128]{2,1,0:T(8,128)(2,1)}, u32[]{:S(2)}, u32[]{:S(2)}) collective-permute-start(bf16[16,2048,128]{2,1,0:T(8,128)(2,1)} %refs_0_.6), channel_id=1, source_target_pairs={{0,4},{4,0},{8,12},{12,8},{1,5},{5,1},{9,13},{13,9},{2,6},{6,2},{1... | collective-permute-start | bytes 25165832 | tf_op jit(solution)/shard_map/ppermute | solution.py:12
  4.8 14.8 %collective-permute-start.14 = (bf16[256,256]{1,0:T(8,128)(2,1)}, bf16[256,256]{1,0:T(8,128)(2,1)S(1)}, u32[]{:S(2)}, u32[]{:S(2)}) collective-permute-start(bf16[256,256]{1,0:T(8,128)(2,1)} %bitcast.67), channel_id=1, source_target_pairs={{0,3},{1,2},{2,1},{3,0},{4,7},{5,6},{6,5},{7,4},{8,11},{9,10},{10,... | collective-permute-start | bytes 393224 | tf_op jit(solution)/shard_map/ppermute | solution.py:12
  8.2 11.7 %collective-permute-start.19 = (bf16[16,2,64,256]{3,2,1,0:T(8,128)(2,1)S(1)}, bf16[16,2,64,256]{3,2,1,0:T(8,128)(2,1)S(1)}, u32[]{:S(2)}, u32[]{:S(2)}) collective-permute-start(bf16[16,2,64,256]{3,2,1,0:T(8,128)(2,1)S(1)} %copy-done.9), channel_id=1, source_target_pairs={{0,4},{4,0},{8,12},{12,8},{1,5},{5,1},{9,13},{13,9},{2,6},{6,2},{1... | collective-permute-start | bytes 3145736 | tf_op jit(solution)/shard_map/ppermute | solution.py:12
  12.1 30.1 %collective-permute-start.20 = (bf16[512,512]{1,0:T(8,128)(2,1)}, bf16[512,512]{1,0:T(8,128)(2,1)}, u32[]{:S(2)}, u32[]{:S(2)}) collective-permute-start(bf16[512,512]{1,0:T(8,128)(2,1)} %bitcast.66), channel_id=1, source_target_pairs={{0,2},{1,3},{2,0},{3,1},{4,6},{5,7},{6,4},{7,5},{8,10},{9,11},{10,... | collective-permute-start | bytes 1572872 | tf_op jit(solution)/shard_map/ppermute | solution.py:12
  24.9 13.7 %collective-permute-start.22 = (bf16[512,256]{1,0:T(8,128)(2,1)S(1)}, bf16[512,256]{1,0:T(8,128)(2,1)S(1)}, u32[]{:S(2)}, u32[]{:S(2)}) collective-permute-start(bf16[512,256]{1,0:T(8,128)(2,1)S(1)} %constant_dynamic-update-slice_fusion.refs_0_), channel_id=1, source_target_pairs={{0,16},{16,0},{1,17},{17,1},{2,18},{18,2},{3,19},{19,3},{4,20},{20... | collective-permute-start | bytes 786440 | tf_op jit(solution)/shard_map/ppermute | solution.py:12
  25.2 18.2 %collective-permute-start.24 = (bf16[512,256]{1,0:T(8,128)(2,1)S(1)}, bf16[512,256]{1,0:T(8,128)(2,1)S(1)}, u32[]{:S(2)}, u32[]{:S(2)}) collective-permute-start(bf16[512,256]{1,0:T(8,128)(2,1)S(1)} %constant_dynamic-update-slice_fusion.refs_0_), channel_id=1, source_target_pairs={{0,4},{4,0},{8,12},{12,8},{1,5},{5,1},{9,13},{13,9},{2,6},{6,2},{1... | collective-permute-start | bytes 786440 | tf_op jit(solution)/shard_map/ppermute | solution.py:12
  26.4 12.3 %collective-permute-start.21 = (bf16[512,256]{1,0:T(8,128)(2,1)S(1)}, bf16[512,256]{1,0:T(8,128)(2,1)S(1)}, u32[]{:S(2)}, u32[]{:S(2)}) collective-permute-start(bf16[512,256]{1,0:T(8,128)(2,1)S(1)} %constant_dynamic-update-slice_fusion.2.refs_0_), channel_id=1, source_target_pairs={{0,16},{16,0},{1,17},{17,1},{2,18},{18,2},{3,19},{19,3},{4,20},{20... | collective-permute-start | bytes 786440 | tf_op jit(solution)/shard_map/ppermute | solution.py:12
  38.7 15.9 %collective-permute-start.27 = (bf16[512,256]{1,0:T(8,128)(2,1)S(1)}, bf16[512,256]{1,0:T(8,128)(2,1)S(1)}, u32[]{:S(2)}, u32[]{:S(2)}) collective-permute-start(bf16[512,256]{1,0:T(8,128)(2,1)S(1)} %collective-permute-done.21.refs_1_), channel_id=1, source_target_pairs={{0,4},{4,0},{8,12},{12,8},{1,5},{5,1},{9,13},{13,9},{2,6},{6,2},{1... | collective-permute-start | bytes 786440 | tf_op jit(solution)/shard_map/ppermute | solution.py:12
  42.2 18.6 %collective-permute-start.31 = (bf16[1,2048,128]{2,1,0:T(8,128)(2,1)S(1)}, bf16[1,2048,128]{2,1,0:T(8,128)(2,1)}, u32[]{:S(2)}, u32[]{:S(2)}) collective-permute-start(bf16[1,2048,128]{2,1,0:T(8,128)(2,1)S(1)} %get-tuple-element.224), channel_id=1, source_target_pairs={{0,8},{4,12},{8,0},{12,4},{1,9},{5,13},{9,1},{13,5},{2,10},{6,14},... | collective-permute-start | bytes 1572872 | tf_op jit(solution)/shard_map/ppermute | solution.py:12
  43.4 17.4 %collective-permute-start.30 = (bf16[512,512]{1,0:T(8,128)(2,1)}, bf16[512,512]{1,0:T(8,128)(2,1)}, u32[]{:S(2)}, u32[]{:S(2)}) collective-permute-start(bf16[512,512]{1,0:T(8,128)(2,1)} %collective-permute-done.20.refs_0_), channel_id=1, source_target_pairs={{0,16},{16,0},{1,17},{17,1},{2,18},{18,2},{3,19},{19,3},{4,20},{20... | collective-permute-start | bytes 1572872 | tf_op jit(solution)/shard_map/ppermute | solution.py:12
  43.7 47.1 %collective-permute-start.37 = (bf16[2,2048,128]{2,1,0:T(8,128)(2,1)}, bf16[2,2048,128]{2,1,0:T(8,128)(2,1)}, u32[]{:S(2)}, u32[]{:S(2)}) collective-permute-start(bf16[2,2048,128]{2,1,0:T(8,128)(2,1)} %get-tuple-element.236), channel_id=1, source_target_pairs={{0,8},{4,12},{8,0},{12,4},{1,9},{5,13},{9,1},{13,5},{2,10},{6,14},... | collective-permute-start | bytes 3145736 | tf_op jit(solution)/shard_map/ppermute | solution.py:12
  43.9 22.2 %collective-permute-start.34 = (bf16[512,512]{1,0:T(8,128)(2,1)S(1)}, bf16[512,512]{1,0:T(8,128)(2,1)}, u32[]{:S(2)}, u32[]{:S(2)}) collective-permute-start(bf16[512,512]{1,0:T(8,128)(2,1)S(1)} %bitcast.65), channel_id=1, source_target_pairs={{0,1},{1,0},{2,3},{3,2},{4,5},{5,4},{6,7},{7,6},{8,9},{9,8},{10,11... | collective-permute-start | bytes 1572872 | tf_op jit(solution)/shard_map/ppermute | solution.py:12
  54.6 13.8 %collective-permute-start.33 = (bf16[512,512]{1,0:T(8,128)(2,1)}, bf16[512,512]{1,0:T(8,128)(2,1)}, u32[]{:S(2)}, u32[]{:S(2)}) collective-permute-start(bf16[512,512]{1,0:T(8,128)(2,1)} %collective-permute-done.20.refs_0_), channel_id=1, source_target_pairs={{0,4},{4,0},{8,12},{12,8},{1,5},{5,1},{9,13},{13,9},{2,6},{6,2},{1... | collective-permute-start | bytes 1572872 | tf_op jit(solution)/shard_map/ppermute | solution.py:12
  66.1 24.7 %collective-permute-start.36 = (bf16[512,512]{1,0:T(8,128)(2,1)}, bf16[512,512]{1,0:T(8,128)(2,1)}, u32[]{:S(2)}, u32[]{:S(2)}) collective-permute-start(bf16[512,512]{1,0:T(8,128)(2,1)} %collective-permute-done.34.refs_0_), channel_id=1, source_target_pairs={{0,16},{16,0},{1,17},{17,1},{2,18},{18,2},{3,19},{19,3},{4,20},{20... | collective-permute-start | bytes 1572872 | tf_op jit(solution)/shard_map/ppermute | solution.py:12
  67.3 11.0 %collective-permute-start.29 = (bf16[832,256]{1,0:T(8,128)(2,1)}, bf16[832,256]{1,0:T(8,128)(2,1)}, u32[]{:S(2)}, u32[]{:S(2)}) collective-permute-start(bf16[832,256]{1,0:T(8,128)(2,1)} %shard_map.87), channel_id=1, source_target_pairs={{0,1},{1,0},{2,3},{3,2},{4,5},{5,4},{6,7},{7,6},{8,9},{9,8},{10,11... | collective-permute-start | bytes 1277960 | tf_op jit(solution)/shard_map/ppermute | solution.py:12
  68.5 17.8 %collective-permute-start.28 = (bf16[832,256]{1,0:T(8,128)(2,1)}, bf16[832,256]{1,0:T(8,128)(2,1)}, u32[]{:S(2)}, u32[]{:S(2)}) collective-permute-start(bf16[832,256]{1,0:T(8,128)(2,1)} %shard_map.88), channel_id=1, source_target_pairs={{0,1},{1,0},{2,3},{3,2},{4,5},{5,4},{6,7},{7,6},{8,9},{9,8},{10,11... | collective-permute-start | bytes 1277960 | tf_op jit(solution)/shard_map/ppermute | solution.py:12
  68.8 72.2 %collective-permute-start.45 = (bf16[2,2048,128]{2,1,0:T(8,128)(2,1)}, bf16[2,2048,128]{2,1,0:T(8,128)(2,1)}, u32[]{:S(2)}, u32[]{:S(2)}) collective-permute-start(bf16[2,2048,128]{2,1,0:T(8,128)(2,1)} %copy-done.5), channel_id=1, source_target_pairs={{0,8},{4,12},{8,0},{12,4},{1,9},{5,13},{9,1},{13,5},{2,10},{6,14},... | collective-permute-start | bytes 3145736 | tf_op jit(solution)/shard_map/ppermute | solution.py:12
  78.3 15.3 %collective-permute-start.39 = (bf16[512,512]{1,0:T(8,128)(2,1)}, bf16[512,512]{1,0:T(8,128)(2,1)S(1)}, u32[]{:S(2)}, u32[]{:S(2)}) collective-permute-start(bf16[512,512]{1,0:T(8,128)(2,1)} %collective-permute-done.34.refs_0_), channel_id=1, source_target_pairs={{0,4},{4,0},{8,12},{12,8},{1,5},{5,1},{9,13},{13,9},{2,6},{6,2},{1... | collective-permute-start | bytes 1572872 | tf_op jit(solution)/shard_map/ppermute | solution.py:12
  99.2 20.1 %collective-permute-start.42 = (bf16[832,256]{1,0:T(8,128)(2,1)S(1)}, bf16[832,256]{1,0:T(8,128)(2,1)S(1)}, u32[]{:S(2)}, u32[]{:S(2)}) collective-permute-start(bf16[832,256]{1,0:T(8,128)(2,1)S(1)} %get-tuple-element.244), channel_id=1, source_target_pairs={{0,1},{1,0},{2,3},{3,2},{4,5},{5,4},{6,7},{7,6},{8,9},{9,8},{10,11... | collective-permute-start | bytes 1277960 | tf_op jit(solution)/shard_map/ppermute | solution.py:12
  100.4 20.9 %collective-permute-start.41 = (bf16[832,256]{1,0:T(8,128)(2,1)S(1)}, bf16[832,256]{1,0:T(8,128)(2,1)S(1)}, u32[]{:S(2)}, u32[]{:S(2)}) collective-permute-start(bf16[832,256]{1,0:T(8,128)(2,1)S(1)} %get-tuple-element.237), channel_id=1, source_target_pairs={{0,2},{1,3},{2,0},{3,1},{4,6},{5,7},{6,4},{7,5},{8,10},{9,11},{10,... | collective-permute-start | bytes 1277960 | tf_op jit(solution)/shard_map/ppermute | solution.py:12
  101.8 35.8 %collective-permute-start.40 = (bf16[832,256]{1,0:T(8,128)(2,1)S(1)}, bf16[832,256]{1,0:T(8,128)(2,1)S(1)}, u32[]{:S(2)}, u32[]{:S(2)}) collective-permute-start(bf16[832,256]{1,0:T(8,128)(2,1)S(1)} %get-tuple-element.243), channel_id=1, source_target_pairs={{0,1},{1,0},{2,3},{3,2},{4,5},{5,4},{6,7},{7,6},{8,9},{9,8},{10,11... | collective-permute-start | bytes 1277960 | tf_op jit(solution)/shard_map/ppermute | solution.py:12
  102.9 34.7 %collective-permute-start.35 = (bf16[832,256]{1,0:T(8,128)(2,1)S(1)}, bf16[832,256]{1,0:T(8,128)(2,1)S(1)}, u32[]{:S(2)}, u32[]{:S(2)}) collective-permute-start(bf16[832,256]{1,0:T(8,128)(2,1)S(1)} %get-tuple-element.234), channel_id=1, source_target_pairs={{0,2},{1,3},{2,0},{3,1},{4,6},{5,7},{6,4},{7,5},{8,10},{9,11},{10,... | collective-permute-start | bytes 1277960 | tf_op jit(solution)/shard_map/ppermute | solution.py:12
  119.3 28.5 %collective-permute-start.44 = (bf16[2,2048,128]{2,1,0:T(8,128)(2,1)}, bf16[2,2048,128]{2,1,0:T(8,128)(2,1)S(1)}, u32[]{:S(2)}, u32[]{:S(2)}) collective-permute-start(bf16[2,2048,128]{2,1,0:T(8,128)(2,1)} %collective-permute-done.37.refs_4_), channel_id=1, source_target_pairs={{0,4},{4,0},{8,12},{12,8},{1,5},{5,1},{9,13},{13,9},{2,6},{6,2},{1... | collective-permute-start | bytes 3145736 | tf_op jit(solution)/shard_map/ppermute | solution.py:12
  161.7 14.7 %collective-permute-start.48 = (bf16[1024,128]{1,0:T(8,128)(2,1)S(1)}, bf16[1024,128]{1,0:T(8,128)(2,1)S(1)}, u32[]{:S(2)}, u32[]{:S(2)}) collective-permute-start(bf16[1024,128]{1,0:T(8,128)(2,1)S(1)} %add_convert_fusion), channel_id=1, source_target_pairs={{0,2},{1,3},{2,0},{3,1},{4,6},{5,7},{6,4},{7,5},{8,10},{9,11},{10,... | collective-permute-start | bytes 786440 | tf_op jit(solution)/shard_map/ppermute | solution.py:12
  (35 other events, 432.7 us)

commit v4 on v3

v4 whole, which is shorter than its diff:
```python
import functools

import jax
import jax.numpy as jnp
from jax import lax
from jax.experimental import pallas as pl
from jax.experimental.pallas import tpu as pltpu
from jax.sharding import PartitionSpec as P


def flip(x, axis, size, mask):
    return lax.ppermute(x, axis, [(i, i ^ mask) for i in range(size)])


def bits(size, first=1):
    out = []
    while first < size:
        out.append(first)
        first *= 2
    return out


def after(value, *others):
    return lax.optimization_barrier((value,) + others)[0]


def pick_kernel(low, cuts, own_at, mate_at, mine, own, mate, own_up, mate_up, *refs):
    *downs, up, sems = refs
    moves = []
    for j in range(cuts[-1]):
        chunk = sum(j >= cut for cut in cuts[1:])
        for place, out, one, other in (
            (0, downs[chunk].at[j - cuts[chunk]], own, mate),
            (1, up.at[j], own_up, mate_up),
        ):
            sem = sems.at[2 * j + place]
            from_own = pltpu.make_async_copy(one.at[own_at[low + j]], out, sem)
            from_mate = pltpu.make_async_copy(other.at[mate_at[low + j]], out, sem)
            pl.when(mine[low + j] == 1)(from_own.start)
            pl.when(mine[low + j] != 1)(from_mate.start)
            moves.append(from_own)
    for move in moves:
        move.wait()


def pick_pages(lists, low, cuts, own, mate, own_up, mate_up):
    counts = [last - first for first, last in zip(cuts[:-1], cuts[1:])]
    return pl.pallas_call(
        functools.partial(pick_kernel, low, cuts),
        out_shape=[jax.ShapeDtypeStruct((count,) + own.shape[1:], own.dtype) for count in counts]
        + [jax.ShapeDtypeStruct((cuts[-1],) + own_up.shape[1:], own_up.dtype)],
        grid_spec=pltpu.PrefetchScalarGridSpec(
            num_scalar_prefetch=3,
            grid=(1,),
            in_specs=[pl.BlockSpec(memory_space=pl.ANY)] * 4,
            out_specs=[pl.BlockSpec((count,) + own.shape[1:], lambda i, *s: (0, 0, 0)) for count in counts]
            + [pl.BlockSpec((cuts[-1],) + own_up.shape[1:], lambda i, *s: (0, 0, 0, 0))],
            scratch_shapes=[pltpu.SemaphoreType.DMA((2 * cuts[-1],))],
        ),
        compiler_params=pltpu.CompilerParams(vmem_limit_bytes=32 << 20),
    )(*lists, own, mate, own_up, mate_up)


def blank(*shapes):
    return pl.pallas_call(
        lambda *refs: None,
        out_shape=list(shapes),
        out_specs=[pl.BlockSpec(memory_space=pl.ANY)] * len(shapes),
    )()


def side_kernel(weight, out):
    width = weight.shape[2]
    for which in range(2):
        out[0, :, which * width : (which + 1) * width] = weight[:, which, :]


def apart_kernel(weight, keys, values):
    keys[0], values[0] = weight[:, 0, :], weight[:, 1, :]


def side_by_side(at, weight, part, low, count, split=False):
    _, two, width = weight.shape
    wide = width if split else two * width
    outs = 2 if split else 1
    kernel = apart_kernel if split else side_kernel
    return pl.pallas_call(
        lambda at, *refs: kernel(*refs),
        out_shape=[jax.ShapeDtypeStruct((count, part, wide), weight.dtype)] * outs,
        grid_spec=pltpu.PrefetchScalarGridSpec(
            num_scalar_prefetch=1,
            grid=(count,),
            in_specs=[pl.BlockSpec((part, two, width), lambda j, at: (at[low + j], 0, 0))],
            out_specs=[pl.BlockSpec((1, part, wide), lambda j, at: (j, 0, 0))] * outs,
        ),
    )(at, weight)


def pack_kernel(first, at, place, x, straight, aside, picks):
    @pl.when(pl.program_id(0) == 0)
    def _():
        row = first + lax.broadcasted_iota(jnp.int32, picks.shape, 0)
        picks[...] = jnp.where(place[...] == row, 1.0, 0.0).astype(picks.dtype)

    packed = jnp.dot(picks[...], x[...], preferred_element_type=jnp.float32).astype(x.dtype)
    straight[...] = packed
    aside[...] = packed


def pack(place, x, at, part, first, last):
    rows, features = x.shape
    count = last - first
    if part % 128:
        pick = place[None, :] == jnp.arange(first, last, dtype=jnp.int32)[:, None]
        packed = jnp.dot(pick.astype(x.dtype), x, preferred_element_type=jnp.float32).astype(x.dtype)
        return packed, packed.reshape(count, -1, part)[:, at].reshape(count, features)
    return pl.pallas_call(
        functools.partial(pack_kernel, first),
        out_shape=[jax.ShapeDtypeStruct((count, features), x.dtype)] * 2,
        grid_spec=pltpu.PrefetchScalarGridSpec(
            num_scalar_prefetch=1,
            grid=(features // part,),
            in_specs=[
                pl.BlockSpec((1, rows), lambda j, at: (0, 0)),
                pl.BlockSpec((rows, part), lambda j, at: (0, j)),
            ],
            out_specs=[
                pl.BlockSpec((count, part), lambda j, at: (0, j)),
                pl.BlockSpec((count, part), lambda j, at: (0, at[j])),
            ],
            scratch_shapes=[pltpu.VMEM((count, rows), x.dtype)],
        ),
        compiler_params=pltpu.CompilerParams(vmem_limit_bytes=32 << 20),
    )(at, place.reshape(1, rows), x)


def multiply_kernel(parts, x, *refs):
    weights, added, out = refs[:parts], refs[parts:-1], refs[-1]
    total, low = None, 0
    for weight in weights:
        high = low + weight.shape[0]
        piece = jnp.dot(x[:, low:high], weight[...], preferred_element_type=jnp.float32)
        total, low = piece if total is None else total + piece, high
    for ref in added:
        total = total + ref[...].astype(jnp.float32)
    out[...] = total.astype(out.dtype)


def multiply(x, weights, added, dtype):
    rows, features = x.shape
    block = rows // 4 if rows % 64 == 0 else rows
    width = weights[0].shape[1]
    piece = pl.BlockSpec((block, width), lambda j: (j, 0))
    return pl.pallas_call(
        functools.partial(multiply_kernel, len(weights)),
        out_shape=jax.ShapeDtypeStruct((rows, width), dtype),
        grid=(rows // block,),
        in_specs=[pl.BlockSpec((block, features), lambda j: (j, 0))]
        + [pl.BlockSpec(weight.shape, lambda j: (0, 0)) for weight in weights]
        + [piece] * len(added),
        out_specs=piece,
        compiler_params=pltpu.CompilerParams(vmem_limit_bytes=40 << 20),
    )(x, *weights, *added)


def shrink_kernel(count, tiles, kind, places, *refs):
    (own_x, mate_x), pools, outs = refs[:2], refs[2 : 2 + count], refs[2 + count : 4 + count]
    rows_in, pages, row_sems, sems = refs[4 + count :]
    tile_rows = outs[0].shape[0] // tiles
    for i in range(2 * tiles):
        rows = pl.ds(i % tiles * tile_rows, tile_rows)
        x = own_x if i < tiles else mate_x
        for number, pool in enumerate(pools):
            move = pltpu.make_async_copy(pool.at[places[i]], pages.at[i], sems.at[i])
            pl.when(kind[i] == number)(move.start)
        move = pltpu.make_async_copy(x.at[rows], rows_in.at[i], row_sems.at[i])
        pl.when(kind[i] >= 0)(move.start)
    for i in range(2 * tiles):
        rows = pl.ds(i % tiles * tile_rows, tile_rows)
        x, out = (own_x, outs[0]) if i < tiles else (mate_x, outs[1])

        @pl.when(kind[i] >= 0)
        def _(i=i, rows=rows, x=x, out=out):
            pltpu.make_async_copy(pools[0].at[0], pages.at[i], sems.at[i]).wait()
            pltpu.make_async_copy(x.at[rows], rows_in.at[i], row_sems.at[i]).wait()
            out[rows, :] = jnp.dot(
                rows_in[i], pages[i], preferred_element_type=jnp.float32
            ).astype(out.dtype)

        @pl.when(kind[i] < 0)
        def _(rows=rows, out=out):
            out[rows, :] = jnp.zeros((tile_rows, out.shape[1]), out.dtype)


def tile_shrink(kind, places, own_x, mate_x, pools, tiles):
    features, columns = pools[0].shape[1:]
    rows = own_x.shape[0]
    out = pl.BlockSpec((rows, columns), lambda i, *s: (0, 0))
    return pl.pallas_call(
        functools.partial(shrink_kernel, len(pools), tiles),
        out_shape=[jax.ShapeDtypeStruct((rows, columns), jnp.bfloat16)] * 2,
        grid_spec=pltpu.PrefetchScalarGridSpec(
            num_scalar_prefetch=2,
            grid=(1,),
            in_specs=[pl.BlockSpec(memory_space=pl.ANY)] * (2 + len(pools)),
            out_specs=[out, out],
            scratch_shapes=[
                pltpu.VMEM((2 * tiles, rows // tiles, features), own_x.dtype),
                pltpu.VMEM((2 * tiles, features, columns), pools[0].dtype),
                pltpu.SemaphoreType.DMA((2 * tiles,)),
                pltpu.SemaphoreType.DMA((2 * tiles,)),
            ],
        ),
        compiler_params=pltpu.CompilerParams(vmem_limit_bytes=48 << 20),
    )(kind, places, own_x, mate_x, *pools)


def finish_kernel(count, terms, offsets, live, kind, places, *refs):
    base, more = refs[:2]
    parts, pools = refs[2 : 2 + terms], refs[2 + terms : 2 + terms + count]
    out, held, ups, sems = refs[2 + terms + count :]
    t = pl.program_id(0)
    tiles = ups.shape[0]
    tile_rows, two, width = out.shape
    half = ups.shape[2]
    room, rest = base.shape[0], more.shape[0]

    @pl.when(t == 0)
    def _():
        for tile in range(tiles):
            for number, pool in enumerate(pools):
                move = pltpu.make_async_copy(pool.at[places[tile]], ups.at[tile], sems.at[tile])
                pl.when(kind[tile] == number)(move.start)
        held[:room] = base[...]
        held[room : room + rest] = more[...]
        held[room + rest :] = jnp.zeros((tile_rows, 2 * width), jnp.float32)

    pltpu.make_async_copy(pools[0].at[0], ups.at[t], sems.at[t]).wait()
    low = pl.multiple_of((offsets[t] // 8) * 8, 8)
    shift = offsets[t] % 8
    alive = lax.broadcasted_iota(jnp.int32, (tile_rows, width), 0) < live[t]
    shrink = parts[0][...].astype(jnp.float32)
    for part in parts[1:]:
        shrink = shrink + part[...].astype(jnp.float32)
    shrink = shrink.astype(jnp.bfloat16)
    for which in range(2):
        expand = jnp.dot(
            shrink[:, which * half : (which + 1) * half],
            ups[t, which],
            preferred_element_type=jnp.float32,
        )
        wide = held[pl.ds(low, tile_rows + 8), which * width : (which + 1) * width]
        part = pltpu.roll(wide, tile_rows + 8 - shift, 0)[:tile_rows]
        out[:, which, :] = jnp.where(alive, part + expand, 0.0).astype(out.dtype)


def finish(offsets, live, kind, places, totals, rest, parts, pools):
    tiles = offsets.shape[0]
    rows, columns = parts[0].shape
    tile_rows = rows // tiles
    width = totals.shape[1] // 2

    def whole(array):
        return pl.BlockSpec(array.shape, lambda t, *s: (0, 0))

    return pl.pallas_call(
        functools.partial(finish_kernel, len(pools), len(parts)),
        out_shape=jax.ShapeDtypeStruct((rows, 2, width), jnp.bfloat16),
        grid_spec=pltpu.PrefetchScalarGridSpec(
            num_scalar_prefetch=4,
            grid=(tiles,),
            in_specs=[whole(totals), whole(rest)]
            + [pl.BlockSpec((tile_rows, columns), lambda t, *s: (t, 0))] * len(parts)
            + [pl.BlockSpec(memory_space=pl.ANY)] * len(pools),
            out_specs=pl.BlockSpec((tile_rows, 2, width), lambda t, *s: (t, 0, 0)),
            scratch_shapes=[
                pltpu.VMEM((rows + tile_rows, 2 * width), jnp.float32),
                pltpu.VMEM((tiles,) + pools[0].shape[1:], pools[0].dtype),
                pltpu.SemaphoreType.DMA((tiles,)),
            ],
        ),
        compiler_params=pltpu.CompilerParams(vmem_limit_bytes=48 << 20),
    )(offsets, live, kind, places, totals, rest, *parts, *pools)


def on_device(
    input_rows,
    key_value_weight,
    adapter_down_weight,
    adapter_up_weight,
    tile_page_index,
    tile_live_rows,
):
    groups = lax.axis_size("groups")
    ranks = lax.axis_size("dp")
    shares = lax.axis_size("tensor")
    group = lax.axis_index("groups")
    rank = lax.axis_index("dp")
    share = lax.axis_index("tensor")
    chips = ranks // 2
    chip, core = rank // 2, rank % 2
    tiles = tile_live_rows.shape[0]
    local_pages = adapter_down_weight.shape[0]
    chip_pages = 2 * local_pages
    capacity = max(2, (2 * tiles + ranks - 1) // ranks)
    most_slots = 2 * capacity
    rows, features = input_rows.shape
    tile_rows = rows // tiles
    column_width = key_value_weight.shape[2]
    half = adapter_down_weight.shape[2] // 2

    columns = 2 * column_width
    plane = groups * ranks
    part = features // plane

    line = []

    def ready(value):
        return after(value, line[-1]) if line else value

    def mark(value):
        line.append(jax.tree.leaves(value)[0])
        return value

    def wait(value):
        return mark(ready(value))

    mate_up = flip(adapter_up_weight, "dp", ranks, 1)
    mate_down = flip(adapter_down_weight, "dp", ranks, 1)
    mate_rows = flip(input_rows, "dp", ranks, 1)

    steps = [("dp", ranks, m, (rank // m) % 2) for m in bits(ranks, 2)]
    steps += [("groups", groups, m, (group // m) % 2) for m in bits(groups)]
    steps += [("dp", ranks, 1, core)]
    over_chips = len(bits(ranks, 2))
    last_step = len(steps) - 1
    spot = sum(bit << i for i, (_, _, _, bit) in enumerate(steps))
    turns = list(range(shares - 1, 0, -1))
    order = spot ^ jnp.arange(plane, dtype=jnp.int32)
    entries = [(turns[0], 0)] + [(k, i) for k in turns[1:] for i in range(chips)]
    starts = (share ^ jnp.array([k for k, _ in entries], jnp.int32)) * plane + (
        spot ^ jnp.array([i for _, i in entries], jnp.int32)
    )
    weights = {}
    for k in turns:
        count = 1 if k == turns[0] else chips
        piece = mark(
            side_by_side(starts, ready(key_value_weight), part, entries.index((k, 0)), count)
        )[0]
        weights[k] = piece.reshape(count * part, columns)
        if k == turns[0]:
            weights[k] = flip(weights[k], "tensor", shares, k)

    moving = {}

    def begin(key, step):
        axis, size, m, _ = steps[step]
        moving[key, step] = flip(weights[key], axis, size, m)

    def end(key, step):
        got = wait(moving.pop((key, step)))
        weights[key] = mark(jnp.concatenate([weights[key], got]))

    def go_on(key):
        got = wait(moving.pop((key, last_step - 1)))
        axis, size, m, _ = steps[last_step]
        gathered[key] = [weights[key], got] + [flip(v, axis, size, m) for v in (weights[key], got)]

    def get_all(key):
        gathered[key] = gathered[key][:2] + [wait(value) for value in gathered[key][2:]]
        return gathered[key]

    gathered = {}
    arrived = {}

    def lowest(k):
        return k & -k if k else shares

    def take(k, arrived):
        return [arrived.pop(k + m) for m in bits(lowest(k))]

    table = tile_page_index.reshape(chips, 2 * tiles)
    page_range = jnp.arange(ranks * local_pages, dtype=jnp.int32)
    need = jnp.any(table[:, :, None] == page_range[None, None, :], axis=1)
    need = need.reshape(chips, chips, chip_pages)
    position = jnp.cumsum(need.astype(jnp.int32), axis=2) - 1
    usual = -(-5 * most_slots // 8)
    more = -(-6 * most_slots // 8)
    cuts = [0, max(1, 2 * usual // 5), max(2, 4 * usual // 5), usual]
    firsts = [0, 2 * usual, 2 * more, 2 * most_slots]
    most_pages = jnp.max(
        jnp.where(jnp.eye(chips, dtype=jnp.bool_), 0, position[:, :, -1] + 1)
    )
    slot_range = jnp.arange(2 * most_slots, dtype=jnp.int32)
    chip_range = jnp.arange(chip_pages, dtype=jnp.int32)

    offsets = jnp.cumsum(tile_live_rows) - tile_live_rows
    live_total = jnp.sum(tile_live_rows)
    live = jnp.arange(tile_rows, dtype=jnp.int32)[None, :] < tile_live_rows[:, None]
    packed_place = offsets[:, None] + jnp.arange(tile_rows, dtype=jnp.int32)[None, :]
    packed_place = jnp.where(live, packed_place, -1).reshape(rows)
    room = -(-13 * rows // 256) * 16

    listed = []
    for offset in range(1, chips):
        wanted = need[chip ^ offset, chip]
        place = position[chip ^ offset, chip]
        listed.append(
            jnp.sum(
                jnp.where(
                    wanted[None, :] & (place[None, :] == slot_range[:, None]), chip_range[None, :], 0
                ),
                axis=1,
            )
        )
    sent_lists = []
    for offset in range(1, chips):
        halves = [
            listed[offset - 1][low:high].reshape(2, (high - low) // 2)
            for low, high in zip(firsts[:-1], firsts[1:])
        ]
        halves = jnp.concatenate(halves, axis=1)
        sent = jnp.where(core == 0, halves[0], halves[1])
        mine = ((sent // local_pages) == core).astype(jnp.int32)
        at = sent % local_pages
        sent_lists.append((at * mine, at * (1 - mine), mine))

    def locate(pages):
        owner = pages // local_pages
        entry = position[chip, owner // 2, pages % chip_pages]
        return pages % local_pages, owner, (owner // 2) ^ chip, entry

    page_lists = tile_page_index.reshape(ranks, tiles)
    at_home, owner, step, entry = locate(
        jnp.concatenate([page_lists[rank], page_lists[rank ^ 1]])
    )
    kind, places = jnp.where(owner == rank, 0, -1), at_home
    up_kind, up_places = jnp.where(owner == rank, 0, 1), at_home
    for stage in range(3):
        count = (firsts[stage + 1] - firsts[stage]) // 2
        if count == 0:
            continue
        here = (step != 0) & (entry >= firsts[stage])
        sender, at = (entry - firsts[stage]) // count, (entry - firsts[stage]) % count
        far = (sender != core).astype(jnp.int32)
        up_kind = jnp.where(here, 2 + 2 * stage + far, up_kind)
        up_places = jnp.where(here, (step - 1) * count + at, up_places)
        if stage:
            kind = jnp.where(here, (len(cuts) - 1) * (chips - 1) + stage, kind)
            places = jnp.where(here, (step - 1) * count + at, places)
        else:
            for offset in range(1, chips):
                for i in range(len(cuts) - 1):
                    chosen = here & (step == offset) & (at >= cuts[i])
                    kind = jnp.where(chosen, i * (chips - 1) + offset, kind)
                    places = jnp.where(chosen, at - cuts[i], places)
        kind = jnp.where(here & (far == 1), -1, kind)
    up_kind = up_kind[:tiles].astype(jnp.int32)
    up_places = up_places[:tiles].astype(jnp.int32)
    kind, places = kind.astype(jnp.int32), places.astype(jnp.int32)

    mate_up = wait(mate_up)
    first = turns[0]
    weights[first] = wait(weights[first])
    begin(first, 0)
    for k in turns[1:]:
        weights[k] = flip(ready(weights[k]), "tensor", shares, k)
    mate_down, mate_rows = wait(mate_down), wait(mate_rows)
    pools = [adapter_down_weight]
    crossing = {}
    picked = [
        mark(
            pick_pages(
                lists, 0, cuts, adapter_down_weight, ready(mate_down), adapter_up_weight, mate_up
            )
        )
        for lists in sent_lists
    ]

    def cross(i):
        for offset in range(1, chips):
            crossing[offset, i] = flip(ready(picked[offset - 1][i]), "dp", ranks, 2 * offset)

    def share_pages(i):
        for offset in range(1, chips):
            pools.append(wait(crossing[offset, i]))

    cross(0)
    for value in (kind, places, up_kind, up_places):
        mark(value)
    for step in range(over_chips):
        end(first, step)
        begin(first, step + 1)
    packed, aside = pack(packed_place, ready(input_rows), order, part, 0, room)
    mark(aside)
    for k in turns[1:]:
        weights[k] = wait(weights[k])
        begin(k, last_step - 1)
    go_on(first)

    def product(k):
        added = [wait(value) for value in take(k, arrived)]
        sent = mark(multiply(ready(aside), gathered[k], added, jnp.bfloat16))
        arrived[k] = flip(sent, "tensor", shares, lowest(k))

    get_all(first)
    product(first)
    share_pages(0)
    cross(1)
    at = share * plane + jnp.arange(plane, dtype=jnp.int32)
    own = mark(side_by_side(at, ready(key_value_weight), part, 0, plane)[0])
    own = own.reshape(features, columns)
    near_ups = [
        flip(ready(up), "dp", ranks, 2 * (i + 1)) for i, (*_, up) in enumerate(picked)
    ]
    cross(2)
    for k in turns[1:]:
        go_on(k)
    for k in turns[1:]:
        get_all(k)
        product(k)
    share_pages(1)
    usual_up = jnp.concatenate([wait(up) for up in near_ups])
    usual_ups = [usual_up, flip(usual_up, "dp", ranks, 1)]

    up_pools = [adapter_up_weight, mate_up]
    for stage in (1, 2):

        def send_more(sources):
            low, count = firsts[stage] // 2, (firsts[stage + 1] - firsts[stage]) // 2
            got = []
            for offset in range(1, chips):
                down, up = pick_pages(sent_lists[offset - 1], low, [0, count], *sources)
                got.append((flip(down, "dp", ranks, 2 * offset), flip(up, "dp", ranks, 2 * offset)))
            down = jnp.concatenate([pair[0] for pair in got])
            up = jnp.concatenate([pair[1] for pair in got])
            return down, up, flip(up, "dp", ranks, 1)

        def send_none(sources):
            own_down, _, own_up, _ = sources
            count = (chips - 1) * (firsts[stage + 1] - firsts[stage]) // 2
            down = jax.ShapeDtypeStruct((count,) + own_down.shape[1:], own_down.dtype)
            up = jax.ShapeDtypeStruct((count,) + own_up.shape[1:], own_up.dtype)
            return tuple(blank(down, up, up))

        if firsts[stage + 1] > firsts[stage]:
            near, near_up, far_up = lax.cond(
                most_pages > firsts[stage],
                send_more,
                send_none,
                (ready(adapter_down_weight), mate_down, adapter_up_weight, mate_up),
            )
            pools.append(near)
            up_pools += [near_up, far_up]

    more_pools = pools[1 + 2 * (chips - 1) :]
    del pools[1 + 2 * (chips - 1) :]
    share_pages(2)
    pools += more_pools

    shrink, mate_shrink = tile_shrink(
        kind,
        places,
        ready(input_rows),
        mate_rows,
        pools,
        tiles,
    )
    shrink = shrink + wait(flip(mark(mate_shrink), "dp", ranks, 1))
    parts = [mark(shrink)]
    for m in bits(shares):
        sent = sum(value.astype(jnp.float32) for value in parts).astype(jnp.bfloat16)
        parts.append(flip(sent, "tensor", shares, m))
        if m == 1:
            final = [wait(value) for value in take(0, arrived)]
            totals = mark(multiply(ready(packed), [own], final, jnp.float32))
            parts[-1] = wait(parts[-1])
            up_pools[2:2] = usual_ups
        else:
            parts[-1] = wait(parts[-1])

    def project_rest(operands):
        x, gathered, own = operands
        packed, aside = pack(packed_place, x, order, part, room, rows)
        arrived = {}
        for k in turns:
            sent = multiply(aside, gathered[k], take(k, arrived), jnp.bfloat16)
            arrived[k] = flip(sent, "tensor", shares, lowest(k))
        return multiply(packed, [own], take(0, arrived), jnp.float32)

    rest_shape = jax.ShapeDtypeStruct((rows - room, columns), jnp.float32)
    rest = lax.cond(
        live_total > room,
        project_rest,
        lambda operands: blank(rest_shape)[0],
        (input_rows, gathered, own),
    )
    return finish(
        offsets,
        tile_live_rows,
        up_kind,
        up_places,
        totals,
        rest,
        parts,
        up_pools,
    )


def solution(mesh):
    return jax.shard_map(
        on_device,
        mesh=mesh,
        in_specs=(
            P(("groups", "dp"), "tensor"),
            P(None, None, "tensor"),
            P("dp", "tensor", None),
            P("dp", None, None, "tensor"),
            P("groups"),
            P(("groups", "dp")),
        ),
        out_specs=P(("groups", "dp"), None, "tensor"),
        check_vma=False,
    )
```

time: 186 us -> 153 us (0.82)
  waiting for transfers between devices: 65.8 us -> 49 us
  starting transfers between devices: 47.1 us -> 30.8 us
    ppermute x36 -> x27, waiting for transfers between devices: 65.8 us -> 49 us  [flip(): return lax.ppermute(x, axis, [(i, i ^ mask) for i in range(size)])]
    ppermute x36 -> x27, starting transfers between devices: 47.1 us -> 30.8 us  [flip(): return lax.ppermute(x, axis, [(i, i ^ mask) for i in range(size)])]
    pallas_call x5 -> x4, Pallas kernels: 15.8 us -> 15.6 us  [multiply(): pl.pallas_call(functools.partial(multiply_kernel, len(weights)), out_shap...]
    unnamed x48 -> x41, local copies, waits for them, and re-layouts: 3.77 us -> 3.83 us
  transfers between devices with their start and end apart: 36 -> 27, of which waited for: 9 -> 11; matrix products, arithmetic and copies ran while one was open for 3% -> 5% of each run, Pallas kernels for 25% -> 34%
where the time goes in v4:
time: 153 us; the launch traced here: 150 us
  Pallas kernels  57 us (37%)
  waiting for transfers between devices  49 us (32%)
  starting transfers between devices  30.8 us (20%)
  other arithmetic  5.38 us (4%)
  local copies, waits for them, and re-layouts  5.37 us (4%)
  between operations  2.43 us (2%)
    ppermute x27, waiting for transfers between devices, flip(): return lax.ppermute(x, axis, [(i, i ^ mask) for i in range(size)])  49 us
    ppermute x27, starting transfers between devices, flip(): return lax.ppermute(x, axis, [(i, i ^ mask) for i in range(size)])  30.8 us
    pallas_call x4, Pallas kernels, side_by_side(): pl.pallas_call(lambda at, *refs: kernel(*refs), out_shape=[jax.ShapeDtype...  18.4 us
    pallas_call x4, Pallas kernels, multiply(): pl.pallas_call(functools.partial(multiply_kernel, len(weights)), out_shap...  15.6 us
    pallas_call x1, Pallas kernels, pack(): pl.pallas_call(functools.partial(pack_kernel, first), out_shape=[jax.Shap...  7.23 us
    pallas_call x1, Pallas kernels, finish(): pl.pallas_call(functools.partial(finish_kernel, len(pools), len(parts)),...  6.67 us
    pallas_call x1, Pallas kernels, tile_shrink(): pl.pallas_call(functools.partial(shrink_kernel, len(pools), tiles), out_s...  5.53 us
    unnamed x41, local copies, waits for them, and re-layouts  3.83 us
  transfers between devices with their start and end apart: 27, of which 11 were waited for; matrix products, arithmetic and copies ran while one was open for 5% of the time, Pallas kernels for 34%

profile of v4, /device:TPU:3, one launch (start us, length us, event | category | flops | bytes accessed | tf_op | source)
XLA Modules:
  0.0 149.9 jit_solution(4039717464883655960)
XLA Ops:
  2.4 3.0 %shard_map.82 = bf16[1,256,512]{2,1,0:T(8,128)(2,1)} custom-call(s32[5]{0:T(128)} %xor_add_fusion.at, bf16[8192,2,256]{2,1,0:T(2,128)(2,1)} %refs_0_.4), custom_call_target="tpu_custom_call" | custom-call | tf_op jit(solution)/shard_map/pallas_call | solution.py:87
  5.4 3.3 %collective-permute-start.9 = (bf16[256,512]{1,0:T(8,128)(2,1)}, bf16[256,512]{1,0:T(8,128)(2,1)S(1)}, u32[]{:S(2)}, u32[]{:S(2)}) collective-permute-start(bf16[256,512]{1,0:T(8,128)(2,1)} %bitcast.44), channel_id=1, source_target_pairs={{0,3},{1,2},{2,1},{3,0},{4,7},{5,6},{6,5},{7,4},{8,11},{9,10},{10,... | collective-permute-start | bytes 786440 | tf_op jit(solution)/shard_map/ppermute | solution.py:12
  11.0 3.5 %shard_map.83 = bf16[2,256,512]{2,1,0:T(8,128)(2,1)} custom-call(s32[5]{0:T(128)} %xor_add_fusion.at, bf16[8192,2,256]{2,1,0:T(2,128)(2,1)} %refs_0_.4), custom_call_target="tpu_custom_call" | custom-call | tf_op jit(solution)/shard_map/pallas_call | solution.py:87
  14.5 3.6 %shard_map.84 = bf16[2,256,512]{2,1,0:T(8,128)(2,1)} custom-call(s32[5]{0:T(128)} %xor_add_fusion.at, bf16[8192,2,256]{2,1,0:T(2,128)(2,1)} %refs_0_.4), custom_call_target="tpu_custom_call" | custom-call | tf_op jit(solution)/shard_map/pallas_call | solution.py:87
  20.3 2.5 %collective-permute-start.14 = (bf16[512,512]{1,0:T(8,128)(2,1)}, bf16[512,512]{1,0:T(8,128)(2,1)}, u32[]{:S(2)}, u32[]{:S(2)}) collective-permute-start(bf16[512,512]{1,0:T(8,128)(2,1)} %bitcast.11), channel_id=1, source_target_pairs={{0,2},{1,3},{2,0},{3,1},{4,6},{5,7},{6,4},{7,5},{8,10},{9,11},{10,... | collective-permute-start | bytes 1572872 | tf_op jit(solution)/shard_map/ppermute | solution.py:12
  22.8 3.8 %collective-permute-done.11 = bf16[256,512]{1,0:T(8,128)(2,1)S(1)} collective-permute-done((bf16[256,512]{1,0:T(8,128)(2,1)S(1)}, bf16[256,512]{1,0:T(8,128)(2,1)S(1)}, u32[]{:S(2)}, u32[]{:S(2)}) %collective-permute-start.11) | collective-permute-done | bytes 262176 | tf_op jit(solution)/shard_map/ppermute | solution.py:12
  27.0 3.6 %shard_map.87 = (bf16[2,2048,128]{2,1,0:T(8,128)(2,1)}, bf16[2,2048,128]{2,1,0:T(8,128)(2,1)S(1)}, bf16[1,2048,128]{2,1,0:T(8,128)(2,1)S(1)}, bf16[5,2,64,256]{3,2,1,0:T(8,128)(2,1)S(1)}) custom-call(s32[8]{0:T(128)S(1)} %compare_select_fusion.18.own_at, s32[8]{0:T(128)S(1)} %get-tuple-element.233.mate_at, s32[8]{0:T(128)S(1)} %get-tuple-element.234.mine, ...), custom_call_target="tpu_custom_call" | custom-call | tf_op jit(solution)/shard_map/pallas_call | solution.py:48
  33.7 7.2 %shard_map.85 = (bf16[832,2048]{1,0:T(8,128)(2,1)S(1)}, bf16[832,2048]{1,0:T(8,128)(2,1)S(1)}) custom-call(s32[8]{0:T(128)S(1)} %iota_xor_fusion.at, s32[1,1024]{1,0:T(1,128)S(1)} %bitcast.37, bf16[1024,2048]{1,0:T(8,128)(2,1)S(1)} %copy-done.8), custom_call_target="tpu_custom_call" | custom-call | tf_op jit(solution)/shard_map/pallas_call | solution.py:117
  42.6 3.1 %collective-permute-done.14.refs_0_ = bf16[512,512]{1,0:T(8,128)(2,1)} collective-permute-done((bf16[512,512]{1,0:T(8,128)(2,1)}, bf16[512,512]{1,0:T(8,128)(2,1)}, u32[]{:S(2)}, u32[]{:S(2)}) %collective-permute-start.14) | collective-permute-done | bytes 524320 | tf_op jit(solution)/shard_map/ppermute | solution.py:12
  45.7 1.8 %collective-permute-start.15 = (bf16[512,512]{1,0:T(8,128)(2,1)S(1)}, bf16[512,512]{1,0:T(8,128)(2,1)S(1)}, u32[]{:S(2)}, u32[]{:S(2)}) collective-permute-start(bf16[512,512]{1,0:T(8,128)(2,1)S(1)} %collective-permute-done.12.refs_1_), channel_id=1, source_target_pairs={{0,4},{4,0},{8,12},{12,8},{1,5},{5,1},{9,13},{13,9},{2,6},{6,2},{1... | collective-permute-start | bytes 1572872 | tf_op jit(solution)/shard_map/ppermute | solution.py:12
  49.6 3.2 %shard_map.86 = bf16[832,512]{1,0:T(8,128)(2,1)} custom-call(bf16[832,2048]{1,0:T(8,128)(2,1)S(1)} %get-tuple-element.204.x, bf16[512,512]{1,0:T(8,128)(2,1)S(1)} %constant_dynamic-update-slice_fusion.refs_0_, bf16[512,512]{1,0:T(8,128)(2,1)S(1)} %collective-permute-done.12.refs_1_, bf16[512,512]{1,0:T(8,128)(2,1)S(1)} %collective-permute-done.16.refs_2_, ...), custom_call_target="tpu_custom_call" | custom-call | tf_op jit(solution)/shard_map/pallas_call | solution.py:154
  56.2 8.4 %shard_map.88 = bf16[8,256,512]{2,1,0:T(8,128)(2,1)} custom-call(s32[8]{0:T(128)} %iota_add_fusion.at, bf16[8192,2,256]{2,1,0:T(2,128)(2,1)} %refs_0_.4), custom_call_target="tpu_custom_call" | custom-call | tf_op jit(solution)/shard_map/pallas_call | solution.py:87
  64.6 2.5 %collective-permute-start.22 = (bf16[512,512]{1,0:T(8,128)(2,1)}, bf16[512,512]{1,0:T(8,128)(2,1)S(1)}, u32[]{:S(2)}, u32[]{:S(2)}) collective-permute-start(bf16[512,512]{1,0:T(8,128)(2,1)} %collective-permute-done.18.refs_1_), channel_id=1, source_target_pairs={{0,4},{4,0},{8,12},{12,8},{1,5},{5,1},{9,13},{13,9},{2,6},{6,2},{1... | collective-permute-start | bytes 1572872 | tf_op jit(solution)/shard_map/ppermute | solution.py:12
  67.1 5.5 %collective-permute-done.24.refs_1_ = bf16[512,512]{1,0:T(8,128)(2,1)} collective-permute-done((bf16[512,512]{1,0:T(8,128)(2,1)}, bf16[512,512]{1,0:T(8,128)(2,1)}, u32[]{:S(2)}, u32[]{:S(2)}) %collective-permute-start.24) | collective-permute-done | bytes 524320 | tf_op jit(solution)/shard_map/ppermute | solution.py:12
  75.0 5.1 %shard_map.89 = bf16[832,512]{1,0:T(8,128)(2,1)} custom-call(bf16[832,2048]{1,0:T(8,128)(2,1)S(1)} %get-tuple-element.204.x, bf16[512,512]{1,0:T(8,128)(2,1)} %collective-permute-done.14.refs_0_, bf16[512,512]{1,0:T(8,128)(2,1)} %collective-permute-done.18.refs_1_, bf16[512,512]{1,0:T(8,128)(2,1)} %collective-permute-done.23.refs_2_, ...), custom_call_target="tpu_custom_call" | custom-call | tf_op jit(solution)/shard_map/pallas_call | solution.py:154
  80.1 4.8 %shard_map.90 = bf16[832,512]{1,0:T(8,128)(2,1)} custom-call(bf16[832,2048]{1,0:T(8,128)(2,1)S(1)} %get-tuple-element.204.x, bf16[512,512]{1,0:T(8,128)(2,1)} %collective-permute-done.13.refs_0_, bf16[512,512]{1,0:T(8,128)(2,1)} %collective-permute-done.24.refs_1_, bf16[512,512]{1,0:T(8,128)(2,1)S(1)} %collective-permute-done.27.refs_2_, ...), custom_call_target="tpu_custom_call" | custom-call | tf_op jit(solution)/shard_map/pallas_call | solution.py:154
  88.4 6.8 %collective-permute-done.30.refs_7_ = bf16[5,2,64,256]{3,2,1,0:T(8,128)(2,1)} collective-permute-done((bf16[5,2,64,256]{3,2,1,0:T(8,128)(2,1)}, bf16[5,2,64,256]{3,2,1,0:T(8,128)(2,1)}, u32[]{:S(2)}, u32[]{:S(2)}) %collective-permute-start.30) | collective-permute-done | bytes 327712 | tf_op jit(solution)/shard_map/ppermute | solution.py:12
  95.2 5.5 %shard_map.91 = (bf16[1024,128]{1,0:T(8,128)(2,1)S(1)}, bf16[1024,128]{1,0:T(8,128)(2,1)S(1)}) custom-call(s32[16]{0:T(128)S(1)} %get-tuple-element.241.kind, s32[16]{0:T(128)S(1)} %get-tuple-element.230.places, bf16[1024,2048]{1,0:T(8,128)(2,1)} %refs_0_.5, bf16[1024,2048]{1,0:T(8,128)(2,1)} %collective-permute-done.20.refs_1_, ...), custom_call_target="tpu_custom_call" | custom-call | tf_op jit(solution)/shard_map/pallas_call | solution.py:199
  100.8 4.2 %collective-permute-start.32 = (bf16[1024,128]{1,0:T(8,128)(2,1)S(1)}, bf16[1024,128]{1,0:T(8,128)(2,1)S(1)}, u32[]{:S(2)}, u32[]{:S(2)}) collective-permute-start(bf16[1024,128]{1,0:T(8,128)(2,1)S(1)} %get-tuple-element.219), channel_id=1, source_target_pairs={{0,4},{4,0},{8,12},{12,8},{1,5},{5,1},{9,13},{13,9},{2,6},{6,2},{1... | collective-permute-start | bytes 786440 | tf_op jit(solution)/shard_map/ppermute | solution.py:12
  107.4 14.1 %collective-permute-done.28.refs_1_ = bf16[832,512]{1,0:T(8,128)(2,1)S(1)} collective-permute-done((bf16[832,512]{1,0:T(8,128)(2,1)}, bf16[832,512]{1,0:T(8,128)(2,1)S(1)}, u32[]{:S(2)}, u32[]{:S(2)}) %collective-permute-start.28) | collective-permute-done | bytes 852000 | tf_op jit(solution)/shard_map/ppermute | solution.py:12
  124.0 2.5 %shard_map.92.refs_0_ = f32[832,512]{1,0:T(8,128)S(1)} custom-call(bf16[832,2048]{1,0:T(8,128)(2,1)S(1)} %copy-done.1, bf16[2048,512]{1,0:T(8,128)(2,1)S(1)} %bitcast.42, bf16[832,512]{1,0:T(8,128)(2,1)S(1)} %collective-permute-done.28.refs_1_, bf16[832,512]{1,0:T(8,128)(2,1)S(1)} %copy-done.3), custom_call_target="tpu_custom_call" | custom-call | tf_op jit(solution)/shard_map/pallas_call | solution.py:154
  126.5 1.9 %collective-permute-done.33.refs_3_ = bf16[1024,128]{1,0:T(8,128)(2,1)S(1)} collective-permute-done((bf16[1024,128]{1,0:T(8,128)(2,1)S(1)}, bf16[1024,128]{1,0:T(8,128)(2,1)S(1)}, u32[]{:S(2)}, u32[]{:S(2)}) %collective-permute-start.33) | collective-permute-done | bytes 262176 | tf_op jit(solution)/shard_map/ppermute | solution.py:12
  131.1 12.0 %collective-permute-done.34.refs_4_ = bf16[1024,128]{1,0:T(8,128)(2,1)S(1)} collective-permute-done((bf16[1024,128]{1,0:T(8,128)(2,1)}, bf16[1024,128]{1,0:T(8,128)(2,1)S(1)}, u32[]{:S(2)}, u32[]{:S(2)}) %collective-permute-start.34) | collective-permute-done | bytes 262176 | tf_op jit(solution)/shard_map/ppermute | solution.py:12
  143.1 6.7 %shard_map.93 = bf16[1024,2,256]{2,1,0:T(2,128)(2,1)} custom-call(s32[8]{0:T(128)S(1)} %get-tuple-element.246.offsets, s32[8]{0:T(128)S(1)} %copy-done.4, s32[8]{0:T(128)S(1)} %bitcast.39, s32[8]{0:T(128)S(1)} %bitcast.40, f32[832,512]{1,0:T(8,128)S(1)} %shard_map.92.refs_0_, f32[192,512]{1,0:T(8,128)} %get-tuple-element.262.refs_1_, ...), custom_call_target="tpu_custom_call" | custom-call | tf_op jit(solution)/shard_map/pallas_call | solution.py:266
  (125 shorter events, 29.1 us)
Async XLA Ops:
  0.0 27.0 %collective-permute-start.19 = (bf16[16,2048,128]{2,1,0:T(8,128)(2,1)}, bf16[16,2048,128]{2,1,0:T(8,128)(2,1)}, u32[]{:S(2)}, u32[]{:S(2)}) collective-permute-start(bf16[16,2048,128]{2,1,0:T(8,128)(2,1)} %refs_2_.1), channel_id=1, source_target_pairs={{0,4},{4,0},{8,12},{12,8},{1,5},{5,1},{9,13},{13,9},{2,6},{6,2},{1... | collective-permute-start | bytes 25165832 | tf_op jit(solution)/shard_map/ppermute | solution.py:12
  0.7 26.3 %collective-permute-start.20 = (bf16[1024,2048]{1,0:T(8,128)(2,1)}, bf16[1024,2048]{1,0:T(8,128)(2,1)}, u32[]{:S(2)}, u32[]{:S(2)}) collective-permute-start(bf16[1024,2048]{1,0:T(8,128)(2,1)} %refs_0_.5), channel_id=1, source_target_pairs={{0,4},{4,0},{8,12},{12,8},{1,5},{5,1},{9,13},{13,9},{2,6},{6,2},{1... | collective-permute-start | bytes 12582920 | tf_op jit(solution)/shard_map/ppermute | solution.py:12
  0.7 18.2 %collective-permute-start.10 = (bf16[16,2,64,256]{3,2,1,0:T(8,128)(2,1)}, bf16[16,2,64,256]{3,2,1,0:T(8,128)(2,1)S(1)}, u32[]{:S(2)}, u32[]{:S(2)}) collective-permute-start(bf16[16,2,64,256]{3,2,1,0:T(8,128)(2,1)} %refs_5_.1), channel_id=1, source_target_pairs={{0,4},{4,0},{8,12},{12,8},{1,5},{5,1},{9,13},{13,9},{2,6},{6,2},{1... | collective-permute-start | bytes 3145736 | tf_op jit(solution)/shard_map/ppermute | solution.py:12
  5.4 13.5 %collective-permute-start.9 = (bf16[256,512]{1,0:T(8,128)(2,1)}, bf16[256,512]{1,0:T(8,128)(2,1)S(1)}, u32[]{:S(2)}, u32[]{:S(2)}) collective-permute-start(bf16[256,512]{1,0:T(8,128)(2,1)} %bitcast.44), channel_id=1, source_target_pairs={{0,3},{1,2},{2,1},{3,0},{4,7},{5,6},{6,5},{7,4},{8,11},{9,10},{10,... | collective-permute-start | bytes 786440 | tf_op jit(solution)/shard_map/ppermute | solution.py:12
  18.9 7.7 %collective-permute-start.11 = (bf16[256,512]{1,0:T(8,128)(2,1)S(1)}, bf16[256,512]{1,0:T(8,128)(2,1)S(1)}, u32[]{:S(2)}, u32[]{:S(2)}) collective-permute-start(bf16[256,512]{1,0:T(8,128)(2,1)S(1)} %collective-permute-done.9), channel_id=1, source_target_pairs={{0,8},{4,12},{8,0},{12,4},{1,9},{5,13},{9,1},{13,5},{2,10},{6,14},... | collective-permute-start | bytes 786440 | tf_op jit(solution)/shard_map/ppermute | solution.py:12
  20.3 25.4 %collective-permute-start.14 = (bf16[512,512]{1,0:T(8,128)(2,1)}, bf16[512,512]{1,0:T(8,128)(2,1)}, u32[]{:S(2)}, u32[]{:S(2)}) collective-permute-start(bf16[512,512]{1,0:T(8,128)(2,1)} %bitcast.11), channel_id=1, source_target_pairs={{0,2},{1,3},{2,0},{3,1},{4,6},{5,7},{6,4},{7,5},{8,10},{9,11},{10,... | collective-permute-start | bytes 1572872 | tf_op jit(solution)/shard_map/ppermute | solution.py:12
  22.8 22.9 %collective-permute-start.13 = (bf16[512,512]{1,0:T(8,128)(2,1)}, bf16[512,512]{1,0:T(8,128)(2,1)}, u32[]{:S(2)}, u32[]{:S(2)}) collective-permute-start(bf16[512,512]{1,0:T(8,128)(2,1)} %bitcast.43), channel_id=1, source_target_pairs={{0,1},{1,0},{2,3},{3,2},{4,5},{5,4},{6,7},{7,6},{8,9},{9,8},{10,11... | collective-permute-start | bytes 1572872 | tf_op jit(solution)/shard_map/ppermute | solution.py:12
  26.6 19.1 %collective-permute-start.12 = (bf16[512,512]{1,0:T(8,128)(2,1)S(1)}, bf16[512,512]{1,0:T(8,128)(2,1)S(1)}, u32[]{:S(2)}, u32[]{:S(2)}) collective-permute-start(bf16[512,512]{1,0:T(8,128)(2,1)S(1)} %constant_dynamic-update-slice_fusion.refs_0_), channel_id=1, source_target_pairs={{0,16},{16,0},{1,17},{17,1},{2,18},{18,2},{3,19},{19,3},{4,20},{20... | collective-permute-start | bytes 1572872 | tf_op jit(solution)/shard_map/ppermute | solution.py:12
  30.6 23.7 %collective-permute-start.21 = (bf16[2,2048,128]{2,1,0:T(8,128)(2,1)}, bf16[2,2048,128]{2,1,0:T(8,128)(2,1)}, u32[]{:S(2)}, u32[]{:S(2)}) collective-permute-start(bf16[2,2048,128]{2,1,0:T(8,128)(2,1)} %get-tuple-element.193), channel_id=1, source_target_pairs={{0,8},{4,12},{8,0},{12,4},{1,9},{5,13},{9,1},{13,5},{2,10},{6,14},... | collective-permute-start | bytes 3145736 | tf_op jit(solution)/shard_map/ppermute | solution.py:12
  32.0 17.0 %collective-permute-start.16 = (bf16[512,512]{1,0:T(8,128)(2,1)S(1)}, bf16[512,512]{1,0:T(8,128)(2,1)S(1)}, u32[]{:S(2)}, u32[]{:S(2)}) collective-permute-start(bf16[512,512]{1,0:T(8,128)(2,1)S(1)} %constant_dynamic-update-slice_fusion.refs_0_), channel_id=1, source_target_pairs={{0,4},{4,0},{8,12},{12,8},{1,5},{5,1},{9,13},{13,9},{2,6},{6,2},{1... | collective-permute-start | bytes 1572872 | tf_op jit(solution)/shard_map/ppermute | solution.py:12
  47.5 17.1 %collective-permute-start.18 = (bf16[512,512]{1,0:T(8,128)(2,1)}, bf16[512,512]{1,0:T(8,128)(2,1)}, u32[]{:S(2)}, u32[]{:S(2)}) collective-permute-start(bf16[512,512]{1,0:T(8,128)(2,1)} %collective-permute-done.14.refs_0_), channel_id=1, source_target_pairs={{0,16},{16,0},{1,17},{17,1},{2,18},{18,2},{3,19},{19,3},{4,20},{20... | collective-permute-start | bytes 1572872 | tf_op jit(solution)/shard_map/ppermute | solution.py:12
  47.8 24.8 %collective-permute-start.24 = (bf16[512,512]{1,0:T(8,128)(2,1)}, bf16[512,512]{1,0:T(8,128)(2,1)}, u32[]{:S(2)}, u32[]{:S(2)}) collective-permute-start(bf16[512,512]{1,0:T(8,128)(2,1)} %collective-permute-done.13.refs_0_), channel_id=1, source_target_pairs={{0,16},{16,0},{1,17},{17,1},{2,18},{18,2},{3,19},{19,3},{4,20},{20... | collective-permute-start | bytes 1572872 | tf_op jit(solution)/shard_map/ppermute | solution.py:12
  49.0 24.4 %collective-permute-start.23 = (bf16[512,512]{1,0:T(8,128)(2,1)}, bf16[512,512]{1,0:T(8,128)(2,1)}, u32[]{:S(2)}, u32[]{:S(2)}) collective-permute-start(bf16[512,512]{1,0:T(8,128)(2,1)} %collective-permute-done.14.refs_0_), channel_id=1, source_target_pairs={{0,4},{4,0},{8,12},{12,8},{1,5},{5,1},{9,13},{13,9},{2,6},{6,2},{1... | collective-permute-start | bytes 1572872 | tf_op jit(solution)/shard_map/ppermute | solution.py:12
  52.9 20.9 %collective-permute-start.17 = (bf16[832,512]{1,0:T(8,128)(2,1)}, bf16[832,512]{1,0:T(8,128)(2,1)}, u32[]{:S(2)}, u32[]{:S(2)}) collective-permute-start(bf16[832,512]{1,0:T(8,128)(2,1)} %shard_map.86), channel_id=1, source_target_pairs={{0,1},{1,0},{2,3},{3,2},{4,5},{5,4},{6,7},{7,6},{8,9},{9,8},{10,11... | collective-permute-start | bytes 2555912 | tf_op jit(solution)/shard_map/ppermute | solution.py:12
  54.3 34.1 %collective-permute-start.31 = (bf16[2,2048,128]{2,1,0:T(8,128)(2,1)}, bf16[2,2048,128]{2,1,0:T(8,128)(2,1)}, u32[]{:S(2)}, u32[]{:S(2)}) collective-permute-start(bf16[2,2048,128]{2,1,0:T(8,128)(2,1)} %copy-done.5), channel_id=1, source_target_pairs={{0,8},{4,12},{8,0},{12,4},{1,9},{5,13},{9,1},{13,5},{2,10},{6,14},... | collective-permute-start | bytes 3145736 | tf_op jit(solution)/shard_map/ppermute | solution.py:12
  64.6 8.8 %collective-permute-start.22 = (bf16[512,512]{1,0:T(8,128)(2,1)}, bf16[512,512]{1,0:T(8,128)(2,1)S(1)}, u32[]{:S(2)}, u32[]{:S(2)}) collective-permute-start(bf16[512,512]{1,0:T(8,128)(2,1)} %collective-permute-done.18.refs_1_), channel_id=1, source_target_pairs={{0,4},{4,0},{8,12},{12,8},{1,5},{5,1},{9,13},{13,9},{2,6},{6,2},{1... | collective-permute-start | bytes 1572872 | tf_op jit(solution)/shard_map/ppermute | solution.py:12
  72.6 7.5 %collective-permute-start.27 = (bf16[512,512]{1,0:T(8,128)(2,1)}, bf16[512,512]{1,0:T(8,128)(2,1)S(1)}, u32[]{:S(2)}, u32[]{:S(2)}) collective-permute-start(bf16[512,512]{1,0:T(8,128)(2,1)} %collective-permute-done.13.refs_0_), channel_id=1, source_target_pairs={{0,4},{4,0},{8,12},{12,8},{1,5},{5,1},{9,13},{13,9},{2,6},{6,2},{1... | collective-permute-start | bytes 1572872 | tf_op jit(solution)/shard_map/ppermute | solution.py:12
  73.4 21.8 %collective-permute-start.29 = (bf16[1,2048,128]{2,1,0:T(8,128)(2,1)}, bf16[1,2048,128]{2,1,0:T(8,128)(2,1)}, u32[]{:S(2)}, u32[]{:S(2)}) collective-permute-start(bf16[1,2048,128]{2,1,0:T(8,128)(2,1)} %copy-done.6), channel_id=1, source_target_pairs={{0,8},{4,12},{8,0},{12,4},{1,9},{5,13},{9,1},{13,5},{2,10},{6,14},... | collective-permute-start | bytes 1572872 | tf_op jit(solution)/shard_map/ppermute | solution.py:12
  73.8 21.4 %collective-permute-start.30 = (bf16[5,2,64,256]{3,2,1,0:T(8,128)(2,1)}, bf16[5,2,64,256]{3,2,1,0:T(8,128)(2,1)}, u32[]{:S(2)}, u32[]{:S(2)}) collective-permute-start(bf16[5,2,64,256]{3,2,1,0:T(8,128)(2,1)} %copy-done.7), channel_id=1, source_target_pairs={{0,8},{4,12},{8,0},{12,4},{1,9},{5,13},{9,1},{13,5},{2,10},{6,14},... | collective-permute-start | bytes 983048 | tf_op jit(solution)/shard_map/ppermute | solution.py:12
  84.9 36.7 %collective-permute-start.28 = (bf16[832,512]{1,0:T(8,128)(2,1)}, bf16[832,512]{1,0:T(8,128)(2,1)S(1)}, u32[]{:S(2)}, u32[]{:S(2)}) collective-permute-start(bf16[832,512]{1,0:T(8,128)(2,1)} %shard_map.90), channel_id=1, source_target_pairs={{0,1},{1,0},{2,3},{3,2},{4,5},{5,4},{6,7},{7,6},{8,9},{9,8},{10,11... | collective-permute-start | bytes 2555912 | tf_op jit(solution)/shard_map/ppermute | solution.py:12
  86.1 35.8 %collective-permute-start.25 = (bf16[832,512]{1,0:T(8,128)(2,1)}, bf16[832,512]{1,0:T(8,128)(2,1)S(1)}, u32[]{:S(2)}, u32[]{:S(2)}) collective-permute-start(bf16[832,512]{1,0:T(8,128)(2,1)} %shard_map.89), channel_id=1, source_target_pairs={{0,2},{1,3},{2,0},{3,1},{4,6},{5,7},{6,4},{7,5},{8,10},{9,11},{10,... | collective-permute-start | bytes 2555912 | tf_op jit(solution)/shard_map/ppermute | solution.py:12
  106.2 22.2 %collective-permute-start.33 = (bf16[1024,128]{1,0:T(8,128)(2,1)S(1)}, bf16[1024,128]{1,0:T(8,128)(2,1)S(1)}, u32[]{:S(2)}, u32[]{:S(2)}) collective-permute-start(bf16[1024,128]{1,0:T(8,128)(2,1)S(1)} %add.203.refs_2_), channel_id=1, source_target_pairs={{0,1},{1,0},{2,3},{3,2},{4,5},{5,4},{6,7},{7,6},{8,9},{9,8},{10,11... | collective-permute-start | bytes 786440 | tf_op jit(solution)/shard_map/ppermute | solution.py:12
  106.8 36.3 %collective-permute-start.35 = (bf16[5,2,64,256]{3,2,1,0:T(8,128)(2,1)}, bf16[5,2,64,256]{3,2,1,0:T(8,128)(2,1)S(1)}, u32[]{:S(2)}, u32[]{:S(2)}) collective-permute-start(bf16[5,2,64,256]{3,2,1,0:T(8,128)(2,1)} %collective-permute-done.30.refs_7_), channel_id=1, source_target_pairs={{0,4},{4,0},{8,12},{12,8},{1,5},{5,1},{9,13},{13,9},{2,6},{6,2},{1... | collective-permute-start | bytes 983048 | tf_op jit(solution)/shard_map/ppermute | solution.py:12
  129.2 13.9 %collective-permute-start.34 = (bf16[1024,128]{1,0:T(8,128)(2,1)}, bf16[1024,128]{1,0:T(8,128)(2,1)S(1)}, u32[]{:S(2)}, u32[]{:S(2)}) collective-permute-start(bf16[1024,128]{1,0:T(8,128)(2,1)} %add_convert_fusion), channel_id=1, source_target_pairs={{0,2},{1,3},{2,0},{3,1},{4,6},{5,7},{6,4},{7,5},{8,10},{9,11},{10,... | collective-permute-start | bytes 786440 | tf_op jit(solution)/shard_map/ppermute | solution.py:12
  (23 other events, 186.2 us)

commit v5 on v4

--- a/solution.py
+++ b/solution.py
@@ -52,7 +52,7 @@
         grid_spec=pltpu.PrefetchScalarGridSpec(
             num_scalar_prefetch=3,
             grid=(1,),
-            in_specs=[pl.BlockSpec(memory_space=pl.ANY)] * 4,
+            in_specs=[pl.BlockSpec(memory_space=pltpu.HBM)] * 4,
             out_specs=[pl.BlockSpec((count,) + own.shape[1:], lambda i, *s: (0, 0, 0)) for count in counts]
             + [pl.BlockSpec((cuts[-1],) + own_up.shape[1:], lambda i, *s: (0, 0, 0, 0))],
             scratch_shapes=[pltpu.SemaphoreType.DMA((2 * cuts[-1],))],
@@ -65,33 +65,24 @@
     return pl.pallas_call(
         lambda *refs: None,
         out_shape=list(shapes),
-        out_specs=[pl.BlockSpec(memory_space=pl.ANY)] * len(shapes),
+        out_specs=[pl.BlockSpec(memory_space=pltpu.HBM)] * len(shapes),
     )()
 
 
 def side_kernel(weight, out):
-    width = weight.shape[2]
-    for which in range(2):
-        out[0, :, which * width : (which + 1) * width] = weight[:, which, :]
-
-
-def apart_kernel(weight, keys, values):
-    keys[0], values[0] = weight[:, 0, :], weight[:, 1, :]
-
-
-def side_by_side(at, weight, part, low, count, split=False):
+    out[0] = weight[...].reshape(out.shape[1:])
+
+
+def side_by_side(at, weight, part, low, count):
     _, two, width = weight.shape
-    wide = width if split else two * width
-    outs = 2 if split else 1
-    kernel = apart_kernel if split else side_kernel
     return pl.pallas_call(
-        lambda at, *refs: kernel(*refs),
-        out_shape=[jax.ShapeDtypeStruct((count, part, wide), weight.dtype)] * outs,
+        lambda at, *refs: side_kernel(*refs),
+        out_shape=[jax.ShapeDtypeStruct((count, part, two * width), weight.dtype)],
         grid_spec=pltpu.PrefetchScalarGridSpec(
             num_scalar_prefetch=1,
             grid=(count,),
             in_specs=[pl.BlockSpec((part, two, width), lambda j, at: (at[low + j], 0, 0))],
-            out_specs=[pl.BlockSpec((1, part, wide), lambda j, at: (j, 0, 0))] * outs,
+            out_specs=[pl.BlockSpec((1, part, two * width), lambda j, at: (j, 0, 0))],
         ),
     )(at, weight)
 
@@ -134,31 +125,80 @@
     )(at, place.reshape(1, rows), x)
 
 
-def multiply_kernel(parts, x, *refs):
-    weights, added, out = refs[:parts], refs[parts:-1], refs[-1]
+def add_up_kernel(*refs):
+    total = refs[0][...].astype(jnp.float32)
+    for ref in refs[1:-1]:
+        total = total + ref[...].astype(jnp.float32)
+    refs[-1][...] = total.astype(refs[-1].dtype)
+
+
+def add_up(values, dtype):
+    rows, width = values[0].shape
+    block = rows // 2 if rows % 32 == 0 else rows
+    piece = pl.BlockSpec((block, width), lambda j: (j, 0))
+    return pl.pallas_call(
+        add_up_kernel,
+        out_shape=jax.ShapeDtypeStruct((rows, width), dtype),
+        grid=(rows // block,),
+        in_specs=[piece] * len(values),
+        out_specs=piece,
+        compiler_params=pltpu.CompilerParams(vmem_limit_bytes=32 << 20),
+    )(*values)
+
+
+def multiply_kernel(parts, adds, x, *refs):
+    weights, added, refs = refs[:parts], refs[parts : parts + adds], refs[parts + adds :]
+    out = refs[0]
+    j = pl.program_id(0)
+    block = x.shape[0]
+    moves = []
+    if adds:
+        added_in, sems = refs[1:]
+        moves = [
+            pltpu.make_async_copy(ref, added_in.at[i], sems.at[i]) for i, ref in enumerate(added)
+        ]
+
+    @pl.when(j == 0)
+    def _():
+        for move in moves:
+            move.start()
+
     total, low = None, 0
     for weight in weights:
         high = low + weight.shape[0]
         piece = jnp.dot(x[:, low:high], weight[...], preferred_element_type=jnp.float32)
         total, low = piece if total is None else total + piece, high
-    for ref in added:
-        total = total + ref[...].astype(jnp.float32)
+
+    @pl.when(j == 0)
+    def _():
+        for move in moves:
+            move.wait()
+
+    for i in range(adds):
+        rows = pl.ds(pl.multiple_of(j * block, block), block)
+        total = total + added_in[i, rows, :].astype(jnp.float32)
     out[...] = total.astype(out.dtype)
 
 
-def multiply(x, weights, added, dtype):
+def multiply(x, weights, added, dtype, spare=0):
     rows, features = x.shape
-    block = rows // 4 if rows % 64 == 0 else rows
+    block = rows // 2 if rows % 32 == 0 else rows
     width = weights[0].shape[1]
-    piece = pl.BlockSpec((block, width), lambda j: (j, 0))
+    scratch = []
+    if added:
+        scratch = [
+            pltpu.VMEM((len(added), rows, width), added[0].dtype),
+            pltpu.SemaphoreType.DMA((len(added),)),
+        ]
     return pl.pallas_call(
-        functools.partial(multiply_kernel, len(weights)),
-        out_shape=jax.ShapeDtypeStruct((rows, width), dtype),
+        functools.partial(multiply_kernel, len(weights), len(added)),
+        out_shape=jax.ShapeDtypeStruct((rows + spare, width), dtype),
         grid=(rows // block,),
         in_specs=[pl.BlockSpec((block, features), lambda j: (j, 0))]
         + [pl.BlockSpec(weight.shape, lambda j: (0, 0)) for weight in weights]
-        + [piece] * len(added),
-        out_specs=piece,
+        + [pl.BlockSpec(memory_space=pl.ANY)] * len(added),
+        out_specs=pl.BlockSpec((block, width), lambda j: (j, 0)),
+        scratch_shapes=scratch,
         compiler_params=pltpu.CompilerParams(vmem_limit_bytes=40 << 20),
     )(x, *weights, *added)
 
@@ -202,7 +242,7 @@
         grid_spec=pltpu.PrefetchScalarGridSpec(
             num_scalar_prefetch=2,
             grid=(1,),
-            in_specs=[pl.BlockSpec(memory_space=pl.ANY)] * (2 + len(pools)),
+            in_specs=[pl.BlockSpec(memory_space=pltpu.HBM)] * (2 + len(pools)),
             out_specs=[out, out],
             scratch_shapes=[
                 pltpu.VMEM((2 * tiles, rows // tiles, features), own_x.dtype),
@@ -218,40 +258,70 @@
 def finish_kernel(count, terms, offsets, live, kind, places, *refs):
     base, more = refs[:2]
     parts, pools = refs[2 : 2 + terms], refs[2 + terms : 2 + terms + count]
-    out, held, ups, sems = refs[2 + terms + count :]
+    out, held, ups, terms_in, sems, term_sems, more_sem = refs[2 + terms + count :]
     t = pl.program_id(0)
     tiles = ups.shape[0]
-    tile_rows, two, width = out.shape
+    tile_rows, width = parts[0].shape[0] // tiles, out.shape[2]
+    per_step = out.shape[0] // tile_rows
     half = ups.shape[2]
-    room, rest = base.shape[0], more.shape[0]
+    rest = more.shape[0]
+    rows = held.shape[0] - tile_rows
+    room = rows - rest
+    over = offsets[tiles - 1] + live[tiles - 1] > room
+
+    part_moves = [
+        pltpu.make_async_copy(part, terms_in.at[i], term_sems.at[i]) for i, part in enumerate(parts)
+    ]
 
     @pl.when(t == 0)
     def _():
+        for move in part_moves:
+            move.start()
         for tile in range(tiles):
             for number, pool in enumerate(pools):
                 move = pltpu.make_async_copy(pool.at[places[tile]], ups.at[tile], sems.at[tile])
                 pl.when(kind[tile] == number)(move.start)
-        held[:room] = base[...]
-        held[room : room + rest] = more[...]
-        held[room + rest :] = jnp.zeros((tile_rows, 2 * width), jnp.float32)
-
-    pltpu.make_async_copy(pools[0].at[0], ups.at[t], sems.at[t]).wait()
-    low = pl.multiple_of((offsets[t] // 8) * 8, 8)
-    shift = offsets[t] % 8
-    alive = lax.broadcasted_iota(jnp.int32, (tile_rows, width), 0) < live[t]
-    shrink = parts[0][...].astype(jnp.float32)
-    for part in parts[1:]:
-        shrink = shrink + part[...].astype(jnp.float32)
-    shrink = shrink.astype(jnp.bfloat16)
-    for which in range(2):
-        expand = jnp.dot(
-            shrink[:, which * half : (which + 1) * half],
-            ups[t, which],
-            preferred_element_type=jnp.float32,
-        )
-        wide = held[pl.ds(low, tile_rows + 8), which * width : (which + 1) * width]
-        part = pltpu.roll(wide, tile_rows + 8 - shift, 0)[:tile_rows]
-        out[:, which, :] = jnp.where(alive, part + expand, 0.0).astype(out.dtype)
+
+    @pl.when((t == 0) & over)
+    def _():
+        move = pltpu.make_async_copy(more, held.at[pl.ds(room, rest)], more_sem)
+        move.start()
+        held[:room] = base[:room]
+        held[rows:] = jnp.zeros((tile_rows, 2 * width), jnp.float32)
+        move.wait()
+
+    @pl.when(t == 0)
+    def _():
+        for move in part_moves:
+            move.wait()
+
+    def put(tile, source, rows):
+        low = pl.multiple_of((offsets[tile] // 8) * 8, 8)
+        alive = lax.broadcasted_iota(jnp.int32, (tile_rows, 2 * width), 0) < live[tile]
+        span = pl.ds(pl.multiple_of(tile * tile_rows, tile_rows), tile_rows)
+        shrink = terms_in[0, span, :].astype(jnp.float32)
+        for i in range(1, terms):
+            shrink = shrink + terms_in[i, span, :].astype(jnp.float32)
+        shrink = shrink.astype(jnp.bfloat16)
+        wide = source[pl.ds(low, tile_rows + 8), :]
+        base = pltpu.roll(wide, tile_rows + 8 - offsets[tile] % 8, 0)[:tile_rows]
+        expand = [
+            jnp.dot(
+                shrink[:, which * half : (which + 1) * half],
+                ups[tile, which],
+                preferred_element_type=jnp.float32,
+            )
+            for which in range(2)
+        ]
+        value = jnp.where(alive, base + jnp.concatenate(expand, axis=1), 0.0)
+        out[rows] = value.astype(out.dtype).reshape(tile_rows, 2, width)
+
+    for i in range(per_step):
+        tile = t * per_step + i
+        rows = slice(i * tile_rows, (i + 1) * tile_rows)
+        pltpu.make_async_copy(pools[0].at[0], ups.at[tile], sems.at[tile]).wait()
+        pl.when(over)(functools.partial(put, tile, held, rows))
+        pl.when(jnp.logical_not(over))(functools.partial(put, tile, base, rows))
 
 
 def finish(offsets, live, kind, places, totals, rest, parts, pools):
@@ -259,24 +329,26 @@
     rows, columns = parts[0].shape
     tile_rows = rows // tiles
     width = totals.shape[1] // 2
-
-    def whole(array):
-        return pl.BlockSpec(array.shape, lambda t, *s: (0, 0))
-
+    per_step = 2 if tiles % 2 == 0 else 1
     return pl.pallas_call(
         functools.partial(finish_kernel, len(pools), len(parts)),
         out_shape=jax.ShapeDtypeStruct((rows, 2, width), jnp.bfloat16),
         grid_spec=pltpu.PrefetchScalarGridSpec(
             num_scalar_prefetch=4,
-            grid=(tiles,),
-            in_specs=[whole(totals), whole(rest)]
-            + [pl.BlockSpec((tile_rows, columns), lambda t, *s: (t, 0))] * len(parts)
-            + [pl.BlockSpec(memory_space=pl.ANY)] * len(pools),
-            out_specs=pl.BlockSpec((tile_rows, 2, width), lambda t, *s: (t, 0, 0)),
+            grid=(tiles // per_step,),
+            in_specs=[
+                pl.BlockSpec(totals.shape, lambda t, *s: (0, 0)),
+                pl.BlockSpec(memory_space=pltpu.HBM),
+            ]
+            + [pl.BlockSpec(memory_space=pltpu.HBM)] * (len(parts) + len(pools)),
+            out_specs=pl.BlockSpec((per_step * tile_rows, 2, width), lambda t, *s: (t, 0, 0)),
             scratch_shapes=[
                 pltpu.VMEM((rows + tile_rows, 2 * width), jnp.float32),
                 pltpu.VMEM((tiles,) + pools[0].shape[1:], pools[0].dtype),
+                pltpu.VMEM((len(parts), rows, columns), parts[0].dtype),
                 pltpu.SemaphoreType.DMA((tiles,)),
+                pltpu.SemaphoreType.DMA((len(parts),)),
+                pltpu.SemaphoreType.DMA,
             ],
         ),
         compiler_params=pltpu.CompilerParams(vmem_limit_bytes=48 << 20),
@@ -341,15 +413,17 @@
     starts = (share ^ jnp.array([k for k, _ in entries], jnp.int32)) * plane + (
         spot ^ jnp.array([i for _, i in entries], jnp.int32)
     )
-    weights = {}
-    for k in turns:
-        count = 1 if k == turns[0] else chips
+    piece = lax.dynamic_slice_in_dim(
+        key_value_weight, (share ^ turns[0]) * features + spot * part, part, 0
+    )
+    piece = mark(piece.reshape(part, columns))
+    weights = {turns[0]: flip(piece, "tensor", shares, turns[0])}
+    for k in turns[1:]:
+        count = chips
         piece = mark(
             side_by_side(starts, ready(key_value_weight), part, entries.index((k, 0)), count)
         )[0]
         weights[k] = piece.reshape(count * part, columns)
-        if k == turns[0]:
-            weights[k] = flip(weights[k], "tensor", shares, k)
 
     moving = {}
 
@@ -459,15 +533,33 @@
     up_places = up_places[:tiles].astype(jnp.int32)
     kind, places = kind.astype(jnp.int32), places.astype(jnp.int32)
 
+    first, direct = turns[0], turns[-1]
+    crossing = {}
+    shared = {}
+
+    def cross(i):
+        for offset in range(1, chips):
+            crossing[offset, i] = flip(ready(picked[offset - 1][i]), "dp", ranks, 2 * offset)
+
+    def share_pages(i):
+        shared[i] = [wait(crossing[offset, i]) for offset in range(1, chips)]
+
+    def product(k):
+        added = [wait(value) for value in take(k, arrived)]
+        sent = mark(multiply(ready(aside), gathered[k], added, jnp.bfloat16))
+        arrived[k] = flip(sent, "tensor", shares, lowest(k))
+
+    def hold(k):
+        arrived[k] = wait(arrived[k])
+
     mate_up = wait(mate_up)
-    first = turns[0]
     weights[first] = wait(weights[first])
     begin(first, 0)
-    for k in turns[1:]:
+    for k in turns[1:-1]:
         weights[k] = flip(ready(weights[k]), "tensor", shares, k)
-    mate_down, mate_rows = wait(mate_down), wait(mate_rows)
-    pools = [adapter_down_weight]
-    crossing = {}
+    weights[direct] = flip(ready(weights[direct]), "tensor", shares, direct)
+    mate_down = wait(mate_down)
+    mate_rows = wait(mate_rows)
     picked = [
         mark(
             pick_pages(
@@ -476,15 +568,6 @@
         )
         for lists in sent_lists
     ]
-
-    def cross(i):
-        for offset in range(1, chips):
-            crossing[offset, i] = flip(ready(picked[offset - 1][i]), "dp", ranks, 2 * offset)
-
-    def share_pages(i):
-        for offset in range(1, chips):
-            pools.append(wait(crossing[offset, i]))
-
     cross(0)
     for value in (kind, places, up_kind, up_places):
         mark(value)
@@ -493,37 +576,35 @@
         begin(first, step + 1)
     packed, aside = pack(packed_place, ready(input_rows), order, part, 0, room)
     mark(aside)
-    for k in turns[1:]:
+    for k in turns[1:-1]:
         weights[k] = wait(weights[k])
         begin(k, last_step - 1)
+    weights[direct] = wait(weights[direct])
+    begin(direct, last_step - 1)
     go_on(first)
-
-    def product(k):
-        added = [wait(value) for value in take(k, arrived)]
-        sent = mark(multiply(ready(aside), gathered[k], added, jnp.bfloat16))
-        arrived[k] = flip(sent, "tensor", shares, lowest(k))
-
     get_all(first)
     product(first)
     share_pages(0)
     cross(1)
-    at = share * plane + jnp.arange(plane, dtype=jnp.int32)
-    own = mark(side_by_side(at, ready(key_value_weight), part, 0, plane)[0])
-    own = own.reshape(features, columns)
-    near_ups = [
-        flip(ready(up), "dp", ranks, 2 * (i + 1)) for i, (*_, up) in enumerate(picked)
-    ]
     cross(2)
-    for k in turns[1:]:
+    for k in turns[1:-1]:
         go_on(k)
-    for k in turns[1:]:
+    go_on(direct)
+    for k in turns[1:-1]:
         get_all(k)
-        product(k)
+    values = {
+        k: mark(multiply(ready(aside), gathered[k], [], jnp.float32)) for k in turns[1:-1]
+    }
+    hold(first)
+    for k in turns[1:-1]:
+        added = [wait(value) for value in take(k, arrived)]
+        sent = mark(add_up([values[k]] + added, jnp.bfloat16))
+        arrived[k] = flip(sent, "tensor", shares, lowest(k))
+    get_all(direct)
+    product(direct)
     share_pages(1)
-    usual_up = jnp.concatenate([wait(up) for up in near_ups])
-    usual_ups = [usual_up, flip(usual_up, "dp", ranks, 1)]
-
     up_pools = [adapter_up_weight, mate_up]
+    more_pools = []
     for stage in (1, 2):
 
         def send_more(sources):
@@ -550,34 +631,42 @@
                 send_none,
                 (ready(adapter_down_weight), mate_down, adapter_up_weight, mate_up),
             )
-            pools.append(near)
+            more_pools.append(near)
             up_pools += [near_up, far_up]
 
-    more_pools = pools[1 + 2 * (chips - 1) :]
-    del pools[1 + 2 * (chips - 1) :]
+    near_ups = [
+        flip(ready(up), "dp", ranks, 2 * (i + 1)) for i, (*_, up) in enumerate(picked)
+    ]
     share_pages(2)
-    pools += more_pools
-
-    shrink, mate_shrink = tile_shrink(
-        kind,
-        places,
-        ready(input_rows),
-        mate_rows,
-        pools,
-        tiles,
-    )
-    shrink = shrink + wait(flip(mark(mate_shrink), "dp", ranks, 1))
-    parts = [mark(shrink)]
-    for m in bits(shares):
+    at = share * plane + jnp.arange(plane, dtype=jnp.int32)
+    own = mark(side_by_side(at, ready(key_value_weight), part, 0, plane)[0])
+    own = own.reshape(features, columns)
+    pools = [adapter_down_weight] + sum((shared[i] for i in range(3)), []) + more_pools
+    shrink, mate_shrink = mark(
+        tile_shrink(kind, places, ready(input_rows), mate_rows, pools, tiles)
+    )
+    mate_shrink = flip(mate_shrink, "dp", ranks, 1)
+    parts = [mark(shrink + wait(mate_shrink))]
+    parts.append(flip(parts[0], "tensor", shares, 1))
+    usual_up = jnp.concatenate([wait(up) for up in near_ups])
+    usual_ups = [usual_up, flip(usual_up, "dp", ranks, 1)]
+    for k in turns[1:-1]:
+        if k in arrived:
+            hold(k)
+    arrived[direct] = wait(arrived[direct])
+    parts[-1] = wait(parts[-1])
+    later = bits(shares, 2)
+    for m in later:
         sent = sum(value.astype(jnp.float32) for value in parts).astype(jnp.bfloat16)
-        parts.append(flip(sent, "tensor", shares, m))
-        if m == 1:
-            final = [wait(value) for value in take(0, arrived)]
-            totals = mark(multiply(ready(packed), [own], final, jnp.float32))
+        parts.append(flip(mark(sent), "tensor", shares, m))
+        if m != later[-1]:
             parts[-1] = wait(parts[-1])
-            up_pools[2:2] = usual_ups
-        else:
-            parts[-1] = wait(parts[-1])
+    final = [wait(value) for value in take(0, arrived)]
+    totals = mark(
+        multiply(ready(packed), [own], final, jnp.float32, rows - room + tile_rows)
+    )
+    up_pools[2:2] = usual_ups
+    parts[-1] = wait(parts[-1])
 
     def project_rest(operands):
         x, gathered, own = operands

time: 153 us -> 153 us (level); the launches traced: 150 us -> 152 us
  waiting for transfers between devices: 49 us -> 61.7 us
  Pallas kernels: 57 us -> 46.9 us
  starting transfers between devices: 30.8 us -> 28.2 us
  local copies, waits for them, and re-layouts: 5.37 us -> 7.89 us
    ppermute x27 -> x30, waiting for transfers between devices: 49 us -> 61.7 us  [flip(): return lax.ppermute(x, axis, [(i, i ^ mask) for i in range(size)])]
    pallas_call x8, Pallas kernels: 34 us -> 26 us  [the longest x4 12.8 us: multiply(): pl.pallas_call(functools.partial(multiply_kernel, len(weights), len(added...]
    ppermute x27 -> x30, starting transfers between devices: 30.8 us -> 28.2 us  [flip(): return lax.ppermute(x, axis, [(i, i ^ mask) for i in range(size)])]
    pallas_call x1, Pallas kernels: 5.53 us -> 3.3 us  [tile_shrink(): pl.pallas_call(functools.partial(shrink_kernel, len(pools), tiles), out_s...]
    pallas_call x1 -> x2, Pallas kernels: 3.59 us -> 5.41 us  [pick_pages(): pl.pallas_call(functools.partial(pick_kernel, low, cuts), out_shape=[jax....]
    pallas_call x1, Pallas kernels: 6.67 us -> 4.95 us  [finish(): pl.pallas_call(functools.partial(finish_kernel, len(pools), len(parts)),...]
    unnamed x41 -> x60, local copies, waits for them, and re-layouts: 3.83 us -> 3.08 us
  transfers between devices with their start and end apart: 27 -> 30, of which waited for: 11 -> 11; matrix products, arithmetic and copies ran while one was open for 5% -> 6% of each run, Pallas kernels for 34% -> 28%
where the time goes in v5:
time: 153 us; the launch traced here: 152 us
  waiting for transfers between devices  61.7 us (40%)
  Pallas kernels  46.9 us (31%)
  starting transfers between devices  28.2 us (18%)
  local copies, waits for them, and re-layouts  7.89 us (5%)
  other arithmetic  5.33 us (3%)
  between operations  2.37 us (2%)
    ppermute x30, waiting for transfers between devices, flip(): return lax.ppermute(x, axis, [(i, i ^ mask) for i in range(size)])  61.7 us
    ppermute x30, starting transfers between devices, flip(): return lax.ppermute(x, axis, [(i, i ^ mask) for i in range(size)])  28.2 us
    pallas_call x4, Pallas kernels, multiply(): pl.pallas_call(functools.partial(multiply_kernel, len(weights), len(added...  12.8 us
    pallas_call x3, Pallas kernels, side_by_side(): pl.pallas_call(lambda at, *refs: side_kernel(*refs), out_shape=[jax.Shape...  12.2 us
    pallas_call x1, Pallas kernels, pack(): pl.pallas_call(functools.partial(pack_kernel, first), out_shape=[jax.Shap...  7.24 us
    pallas_call x2, Pallas kernels, pick_pages(): pl.pallas_call(functools.partial(pick_kernel, low, cuts), out_shape=[jax....  5.41 us
    pallas_call x1, Pallas kernels, finish(): pl.pallas_call(functools.partial(finish_kernel, len(pools), len(parts)),...  4.95 us
    pallas_call x1, Pallas kernels, tile_shrink(): pl.pallas_call(functools.partial(shrink_kernel, len(pools), tiles), out_s...  3.3 us
  transfers between devices with their start and end apart: 30, of which 11 were waited for; matrix products, arithmetic and copies ran while one was open for 6% of the time, Pallas kernels for 28%

profile of v5, /device:TPU:3, one launch (start us, length us, event | category | flops | bytes accessed | tf_op | source)
XLA Modules:
  0.0 152.4 jit_solution(12197265873127760784)
XLA Ops:
  2.4 3.4 %collective-permute-start.9 = (bf16[256,512]{1,0:T(8,128)(2,1)S(1)}, bf16[256,512]{1,0:T(8,128)(2,1)S(1)}, u32[]{:S(2)}, u32[]{:S(2)}) collective-permute-start(bf16[256,512]{1,0:T(8,128)(2,1)S(1)} %bitcast.46), channel_id=1, source_target_pairs={{0,3},{1,2},{2,1},{3,0},{4,7},{5,6},{6,5},{7,4},{8,11},{9,10},{10,... | collective-permute-start | bytes 786440 | tf_op jit(solution)/shard_map/ppermute | solution.py:12
  10.6 2.7 %shard_map.82 = bf16[2,256,512]{2,1,0:T(8,128)(2,1)} custom-call(s32[5]{0:T(128)} %xor_add_fusion.at, bf16[8192,2,256]{2,1,0:T(2,128)(2,1)} %refs_0_.2), custom_call_target="tpu_custom_call" | custom-call | tf_op jit(solution)/shard_map/pallas_call | solution.py:78
  13.2 2.8 %shard_map.83 = bf16[2,256,512]{2,1,0:T(8,128)(2,1)} custom-call(s32[5]{0:T(128)} %xor_add_fusion.at, bf16[8192,2,256]{2,1,0:T(2,128)(2,1)} %refs_0_.2), custom_call_target="tpu_custom_call" | custom-call | tf_op jit(solution)/shard_map/pallas_call | solution.py:78
  19.7 4.9 %collective-permute-done.11 = bf16[256,512]{1,0:T(8,128)(2,1)S(1)} collective-permute-done((bf16[256,512]{1,0:T(8,128)(2,1)S(1)}, bf16[256,512]{1,0:T(8,128)(2,1)S(1)}, u32[]{:S(2)}, u32[]{:S(2)}) %collective-permute-start.11) | collective-permute-done | bytes 262176 | tf_op jit(solution)/shard_map/ppermute | solution.py:12
  25.0 3.8 %shard_map.85 = (bf16[2,2048,128]{2,1,0:T(8,128)(2,1)S(1)}, bf16[2,2048,128]{2,1,0:T(8,128)(2,1)}, bf16[1,2048,128]{2,1,0:T(8,128)(2,1)}, bf16[5,2,64,256]{3,2,1,0:T(8,128)(2,1)S(1)}) custom-call(s32[8]{0:T(128)S(1)} %compare_select_fusion.18.own_at, s32[8]{0:T(128)S(1)} %get-tuple-element.237.mate_at, s32[8]{0:T(128)S(1)} %get-tuple-element.238.mine, ...), custom_call_target="tpu_custom_call" | custom-call | tf_op jit(solution)/shard_map/pallas_call | solution.py:48
  31.8 7.2 %shard_map.84 = (bf16[832,2048]{1,0:T(8,128)(2,1)S(1)}, bf16[832,2048]{1,0:T(8,128)(2,1)S(1)}) custom-call(s32[8]{0:T(128)S(1)} %iota_xor_fusion.at, s32[1,1024]{1,0:T(1,128)S(1)} %bitcast.38, bf16[1024,2048]{1,0:T(8,128)(2,1)S(1)} %copy-done.9), custom_call_target="tpu_custom_call" | custom-call | tf_op jit(solution)/shard_map/pallas_call | solution.py:108
  39.1 5.5 %collective-permute-done.12.refs_0_ = bf16[512,512]{1,0:T(8,128)(2,1)S(1)} collective-permute-done((bf16[512,512]{1,0:T(8,128)(2,1)}, bf16[512,512]{1,0:T(8,128)(2,1)S(1)}, u32[]{:S(2)}, u32[]{:S(2)}) %collective-permute-start.12) | collective-permute-done | bytes 524320 | tf_op jit(solution)/shard_map/ppermute | solution.py:12
  47.5 2.1 %shard_map.86 = bf16[832,512]{1,0:T(8,128)(2,1)S(1)} custom-call(bf16[832,2048]{1,0:T(8,128)(2,1)S(1)} %get-tuple-element.208.x, bf16[512,512]{1,0:T(8,128)(2,1)S(1)} %constant_dynamic-update-slice_fusion.refs_0_, bf16[512,512]{1,0:T(8,128)(2,1)S(1)} %collective-permute-done.17.refs_1_, bf16[512,512]{1,0:T(8,128)(2,1)S(1)} %collective-permute-done.20.refs_2_, ...), custom_call_target="tpu_custom_call" | custom-call | tf_op jit(solution)/shard_map/pallas_call | solution.py:193
  49.9 2.3 %collective-permute-done.16.refs_3_ = bf16[2,2048,128]{2,1,0:T(8,128)(2,1)S(1)} collective-permute-done((bf16[2,2048,128]{2,1,0:T(8,128)(2,1)S(1)}, bf16[2,2048,128]{2,1,0:T(8,128)(2,1)S(1)}, u32[]{:S(2)}, u32[]{:S(2)}) %collective-permute-start.16) | collective-permute-done | bytes 1048608 | tf_op jit(solution)/shard_map/ppermute | solution.py:12
  54.4 4.6 %collective-permute-done.13.refs_1_ = bf16[512,512]{1,0:T(8,128)(2,1)S(1)} collective-permute-done((bf16[512,512]{1,0:T(8,128)(2,1)S(1)}, bf16[512,512]{1,0:T(8,128)(2,1)S(1)}, u32[]{:S(2)}, u32[]{:S(2)}) %collective-permute-start.13) | collective-permute-done | bytes 524320 | tf_op jit(solution)/shard_map/ppermute | solution.py:12
  60.2 10.0 %collective-permute-done.23.refs_1_ = bf16[512,512]{1,0:T(8,128)(2,1)S(1)} collective-permute-done((bf16[512,512]{1,0:T(8,128)(2,1)S(1)}, bf16[512,512]{1,0:T(8,128)(2,1)S(1)}, u32[]{:S(2)}, u32[]{:S(2)}) %collective-permute-start.23) | collective-permute-done | bytes 524320 | tf_op jit(solution)/shard_map/ppermute | solution.py:12
  71.4 2.1 %shard_map.87.refs_0_ = f32[832,512]{1,0:T(8,128)S(1)} custom-call(bf16[832,2048]{1,0:T(8,128)(2,1)S(1)} %get-tuple-element.208.x, bf16[512,512]{1,0:T(8,128)(2,1)S(1)} %collective-permute-done.12.refs_0_, bf16[512,512]{1,0:T(8,128)(2,1)S(1)} %collective-permute-done.13.refs_1_, bf16[512,512]{1,0:T(8,128)(2,1)S(1)} %collective-permute-done.22.refs_2_, ...), custom_call_target="tpu_custom_call" | custom-call | tf_op jit(solution)/shard_map/pallas_call | solution.py:193
  74.7 2.9 %shard_map.89 = bf16[832,512]{1,0:T(8,128)(2,1)} custom-call(bf16[832,2048]{1,0:T(8,128)(2,1)S(1)} %get-tuple-element.208.x, bf16[512,512]{1,0:T(8,128)(2,1)S(1)} %collective-permute-done.18.refs_0_, bf16[512,512]{1,0:T(8,128)(2,1)S(1)} %collective-permute-done.23.refs_1_, bf16[512,512]{1,0:T(8,128)(2,1)S(1)} %collective-permute-done.28.refs_2_, ...), custom_call_target="tpu_custom_call" | custom-call | tf_op jit(solution)/shard_map/pallas_call | solution.py:193
  80.6 6.5 %collective-permute-done.30.refs_5_ = bf16[1,2048,128]{2,1,0:T(8,128)(2,1)} collective-permute-done((bf16[1,2048,128]{2,1,0:T(8,128)(2,1)}, bf16[1,2048,128]{2,1,0:T(8,128)(2,1)}, u32[]{:S(2)}, u32[]{:S(2)}) %collective-permute-start.30) | collective-permute-done | bytes 524320 | tf_op jit(solution)/shard_map/ppermute | solution.py:12
  87.1 6.7 %shard_map.90 = bf16[8,256,512]{2,1,0:T(8,128)(2,1)} custom-call(s32[8]{0:T(128)} %iota_add_fusion.at, bf16[8192,2,256]{2,1,0:T(2,128)(2,1)} %refs_0_.2), custom_call_target="tpu_custom_call" | custom-call | tf_op jit(solution)/shard_map/pallas_call | solution.py:78
  93.8 19.6 %conditional.3 = ((bf16[1,2048,128]{2,1,0:T(8,128)(2,1)}, bf16[1,2,64,256]{3,2,1,0:T(8,128)(2,1)}, bf16[1,2,64,256]{3,2,1,0:T(8,128)(2,1)})) conditional(s32[]{:T(128)} %convert_element_type.38, () %tuple.105, (s32[8]{0:T(128)S(1)}, s32[8]{0:T(128)S(1)}, s32[8]{0:T(128)S(1)}, bf16[16,2048,128]{2,1,0:T(8,128)(2,1)}, bf16[16,2048,128]{2,1,0:T(8,128)(2,1)}, ...), branch_computations={%region_5.6_spmd, %region_6.7_spmd} | conditional | bytes 4718772 | solution.py:628
  97.0 10.3 %collective-permute-done.1 = bf16[1,2,64,256]{3,2,1,0:T(8,128)(2,1)} collective-permute-done((bf16[1,2,64,256]{3,2,1,0:T(8,128)(2,1)S(1)}, bf16[1,2,64,256]{3,2,1,0:T(8,128)(2,1)}, u32[]{:S(2)}, u32[]{:S(2)}) %collective-permute-start.1) | collective-permute-done | bytes 65568 | tf_op jit(solution)/shard_map/cond/branch_1_fun/ppermute | solution.py:12
  107.2 4.1 %collective-permute-start.2 = (bf16[1,2,64,256]{3,2,1,0:T(8,128)(2,1)}, bf16[1,2,64,256]{3,2,1,0:T(8,128)(2,1)}, u32[]{:S(2)}, u32[]{:S(2)}) collective-permute-start(bf16[1,2,64,256]{3,2,1,0:T(8,128)(2,1)} %collective-permute-done.1), channel_id=1, source_target_pairs={{0,4},{4,0},{8,12},{12,8},{1,5},{5,1},{9,13},{13,9},{2,6},{6,2},{1... | collective-permute-start | bytes 196616 | tf_op jit(solution)/shard_map/cond/branch_1_fun/ppermute | solution.py:12
  114.7 3.3 %shard_map.91 = (bf16[1024,128]{1,0:T(8,128)(2,1)S(1)}, bf16[1024,128]{1,0:T(8,128)(2,1)S(1)}) custom-call(s32[16]{0:T(128)S(1)} %get-tuple-element.245.kind, s32[16]{0:T(128)S(1)} %get-tuple-element.234.places, bf16[1024,2048]{1,0:T(8,128)(2,1)} %refs_0_.3, bf16[1024,2048]{1,0:T(8,128)(2,1)} %collective-permute-done.15.refs_1_, ...), custom_call_target="tpu_custom_call" | custom-call | tf_op jit(solution)/shard_map/pallas_call | solution.py:239
  118.0 3.7 %collective-permute-start.31 = (bf16[1024,128]{1,0:T(8,128)(2,1)S(1)}, bf16[1024,128]{1,0:T(8,128)(2,1)S(1)}, u32[]{:S(2)}, u32[]{:S(2)}) collective-permute-start(bf16[1024,128]{1,0:T(8,128)(2,1)S(1)} %get-tuple-element.220), channel_id=1, source_target_pairs={{0,4},{4,0},{8,12},{12,8},{1,5},{5,1},{9,13},{13,9},{2,6},{6,2},{1... | collective-permute-start | bytes 786440 | tf_op jit(solution)/shard_map/ppermute | solution.py:12
  123.0 8.1 %collective-permute-done.29.refs_7_ = bf16[5,2,64,256]{3,2,1,0:T(8,128)(2,1)} collective-permute-done((bf16[5,2,64,256]{3,2,1,0:T(8,128)(2,1)S(1)}, bf16[5,2,64,256]{3,2,1,0:T(8,128)(2,1)}, u32[]{:S(2)}, u32[]{:S(2)}) %collective-permute-start.29) | collective-permute-done | bytes 327712 | tf_op jit(solution)/shard_map/ppermute | solution.py:12
  134.4 5.7 %shard_map.92.refs_0_ = f32[1152,512]{1,0:T(8,128)S(1)} custom-call(bf16[832,2048]{1,0:T(8,128)(2,1)S(1)} %get-tuple-element.228.x, bf16[2048,512]{1,0:T(8,128)(2,1)} %bitcast.43, bf16[832,512]{1,0:T(8,128)(2,1)} %collective-permute-done.32.refs_1_, bf16[832,512]{1,0:T(8,128)(2,1)} %collective-permute-done.25.refs_2_), custom_call_target="tpu_custom_call" | custom-call | tf_op jit(solution)/shard_map/pallas_call | solution.py:193
  140.1 7.1 %collective-permute-done.34.refs_4_ = bf16[1024,128]{1,0:T(8,128)(2,1)} collective-permute-done((bf16[1024,128]{1,0:T(8,128)(2,1)}, bf16[1024,128]{1,0:T(8,128)(2,1)}, u32[]{:S(2)}, u32[]{:S(2)}) %collective-permute-start.34) | collective-permute-done | bytes 262176 | tf_op jit(solution)/shard_map/ppermute | solution.py:12
  147.3 4.9 %shard_map.93 = bf16[1024,2,256]{2,1,0:T(2,128)(2,1)} custom-call(s32[8]{0:T(128)S(1)} %get-tuple-element.250.offsets, s32[8]{0:T(128)S(1)} %copy-done.6, s32[8]{0:T(128)S(1)} %bitcast.40, s32[8]{0:T(128)S(1)} %bitcast.41, f32[1152,512]{1,0:T(8,128)S(1)} %shard_map.92.refs_0_, f32[192,512]{1,0:T(8,128)S(1)} %copy-done.39, bf16[1024,128]{1,0:T(8,128)(2,1)S(1)} %copy-done.1, ...), custom_call_target="tpu_custom_call" | custom-call | tf_op jit(solution)/shard_map/pallas_call | solution.py:333
  (153 shorter events, 35.2 us)
Async XLA Ops:
  0.0 24.9 %collective-permute-start.14 = (bf16[16,2048,128]{2,1,0:T(8,128)(2,1)}, bf16[16,2048,128]{2,1,0:T(8,128)(2,1)}, u32[]{:S(2)}, u32[]{:S(2)}) collective-permute-start(bf16[16,2048,128]{2,1,0:T(8,128)(2,1)} %refs_2_.1), channel_id=1, source_target_pairs={{0,4},{4,0},{8,12},{12,8},{1,5},{5,1},{9,13},{13,9},{2,6},{6,2},{1... | collective-permute-start | bytes 25165832 | tf_op jit(solution)/shard_map/ppermute | solution.py:12
  0.7 24.3 %collective-permute-start.15 = (bf16[1024,2048]{1,0:T(8,128)(2,1)}, bf16[1024,2048]{1,0:T(8,128)(2,1)}, u32[]{:S(2)}, u32[]{:S(2)}) collective-permute-start(bf16[1024,2048]{1,0:T(8,128)(2,1)} %refs_0_.3), channel_id=1, source_target_pairs={{0,4},{4,0},{8,12},{12,8},{1,5},{5,1},{9,13},{13,9},{2,6},{6,2},{1... | collective-permute-start | bytes 12582920 | tf_op jit(solution)/shard_map/ppermute | solution.py:12
  0.7 16.2 %collective-permute-start.10 = (bf16[16,2,64,256]{3,2,1,0:T(8,128)(2,1)}, bf16[16,2,64,256]{3,2,1,0:T(8,128)(2,1)S(1)}, u32[]{:S(2)}, u32[]{:S(2)}) collective-permute-start(bf16[16,2,64,256]{3,2,1,0:T(8,128)(2,1)} %refs_5_.1), channel_id=1, source_target_pairs={{0,4},{4,0},{8,12},{12,8},{1,5},{5,1},{9,13},{13,9},{2,6},{6,2},{1... | collective-permute-start | bytes 3145736 | tf_op jit(solution)/shard_map/ppermute | solution.py:12
  2.4 14.5 %collective-permute-start.9 = (bf16[256,512]{1,0:T(8,128)(2,1)S(1)}, bf16[256,512]{1,0:T(8,128)(2,1)S(1)}, u32[]{:S(2)}, u32[]{:S(2)}) collective-permute-start(bf16[256,512]{1,0:T(8,128)(2,1)S(1)} %bitcast.46), channel_id=1, source_target_pairs={{0,3},{1,2},{2,1},{3,0},{4,7},{5,6},{6,5},{7,4},{8,11},{9,10},{10,... | collective-permute-start | bytes 786440 | tf_op jit(solution)/shard_map/ppermute | solution.py:12
  18.3 26.2 %collective-permute-start.12 = (bf16[512,512]{1,0:T(8,128)(2,1)}, bf16[512,512]{1,0:T(8,128)(2,1)S(1)}, u32[]{:S(2)}, u32[]{:S(2)}) collective-permute-start(bf16[512,512]{1,0:T(8,128)(2,1)} %bitcast.9), channel_id=1, source_target_pairs={{0,2},{1,3},{2,0},{3,1},{4,6},{5,7},{6,4},{7,5},{8,10},{9,11},{10,... | collective-permute-start | bytes 1572872 | tf_op jit(solution)/shard_map/ppermute | solution.py:12
  19.6 24.9 %collective-permute-start.18 = (bf16[512,512]{1,0:T(8,128)(2,1)}, bf16[512,512]{1,0:T(8,128)(2,1)S(1)}, u32[]{:S(2)}, u32[]{:S(2)}) collective-permute-start(bf16[512,512]{1,0:T(8,128)(2,1)} %bitcast.45), channel_id=1, source_target_pairs={{0,1},{1,0},{2,3},{3,2},{4,5},{5,4},{6,7},{7,6},{8,9},{9,8},{10,11... | collective-permute-start | bytes 1572872 | tf_op jit(solution)/shard_map/ppermute | solution.py:12
  24.6 19.9 %collective-permute-start.17 = (bf16[512,512]{1,0:T(8,128)(2,1)S(1)}, bf16[512,512]{1,0:T(8,128)(2,1)S(1)}, u32[]{:S(2)}, u32[]{:S(2)}) collective-permute-start(bf16[512,512]{1,0:T(8,128)(2,1)S(1)} %constant_dynamic-update-slice_fusion.refs_0_), channel_id=1, source_target_pairs={{0,16},{16,0},{1,17},{17,1},{2,18},{18,2},{3,19},{19,3},{4,20},{20... | collective-permute-start | bytes 1572872 | tf_op jit(solution)/shard_map/ppermute | solution.py:12
  28.8 23.4 %collective-permute-start.16 = (bf16[2,2048,128]{2,1,0:T(8,128)(2,1)S(1)}, bf16[2,2048,128]{2,1,0:T(8,128)(2,1)S(1)}, u32[]{:S(2)}, u32[]{:S(2)}) collective-permute-start(bf16[2,2048,128]{2,1,0:T(8,128)(2,1)S(1)} %get-tuple-element.189), channel_id=1, source_target_pairs={{0,8},{4,12},{8,0},{12,4},{1,9},{5,13},{9,1},{13,5},{2,10},{6,14},... | collective-permute-start | bytes 3145736 | tf_op jit(solution)/shard_map/ppermute | solution.py:12
  30.1 16.7 %collective-permute-start.20 = (bf16[512,512]{1,0:T(8,128)(2,1)S(1)}, bf16[512,512]{1,0:T(8,128)(2,1)S(1)}, u32[]{:S(2)}, u32[]{:S(2)}) collective-permute-start(bf16[512,512]{1,0:T(8,128)(2,1)S(1)} %constant_dynamic-update-slice_fusion.refs_0_), channel_id=1, source_target_pairs={{0,4},{4,0},{8,12},{12,8},{1,5},{5,1},{9,13},{13,9},{2,6},{6,2},{1... | collective-permute-start | bytes 1572872 | tf_op jit(solution)/shard_map/ppermute | solution.py:12
  45.4 13.6 %collective-permute-start.13 = (bf16[512,512]{1,0:T(8,128)(2,1)S(1)}, bf16[512,512]{1,0:T(8,128)(2,1)S(1)}, u32[]{:S(2)}, u32[]{:S(2)}) collective-permute-start(bf16[512,512]{1,0:T(8,128)(2,1)S(1)} %collective-permute-done.12.refs_0_), channel_id=1, source_target_pairs={{0,16},{16,0},{1,17},{17,1},{2,18},{18,2},{3,19},{19,3},{4,20},{20... | collective-permute-start | bytes 1572872 | tf_op jit(solution)/shard_map/ppermute | solution.py:12
  45.6 24.6 %collective-permute-start.23 = (bf16[512,512]{1,0:T(8,128)(2,1)S(1)}, bf16[512,512]{1,0:T(8,128)(2,1)S(1)}, u32[]{:S(2)}, u32[]{:S(2)}) collective-permute-start(bf16[512,512]{1,0:T(8,128)(2,1)S(1)} %collective-permute-done.18.refs_0_), channel_id=1, source_target_pairs={{0,16},{16,0},{1,17},{17,1},{2,18},{18,2},{3,19},{19,3},{4,20},{20... | collective-permute-start | bytes 1572872 | tf_op jit(solution)/shard_map/ppermute | solution.py:12
  46.8 24.1 %collective-permute-start.22 = (bf16[512,512]{1,0:T(8,128)(2,1)S(1)}, bf16[512,512]{1,0:T(8,128)(2,1)S(1)}, u32[]{:S(2)}, u32[]{:S(2)}) collective-permute-start(bf16[512,512]{1,0:T(8,128)(2,1)S(1)} %collective-permute-done.12.refs_0_), channel_id=1, source_target_pairs={{0,4},{4,0},{8,12},{12,8},{1,5},{5,1},{9,13},{13,9},{2,6},{6,2},{1... | collective-permute-start | bytes 1572872 | tf_op jit(solution)/shard_map/ppermute | solution.py:12
  49.6 23.9 %collective-permute-start.24 = (bf16[832,512]{1,0:T(8,128)(2,1)S(1)}, bf16[832,512]{1,0:T(8,128)(2,1)S(1)}, u32[]{:S(2)}, u32[]{:S(2)}) collective-permute-start(bf16[832,512]{1,0:T(8,128)(2,1)S(1)} %shard_map.86), channel_id=1, source_target_pairs={{0,1},{1,0},{2,3},{3,2},{4,5},{5,4},{6,7},{7,6},{8,9},{9,8},{10,11... | collective-permute-start | bytes 2555912 | tf_op jit(solution)/shard_map/ppermute | solution.py:12
  53.1 27.4 %collective-permute-start.26 = (bf16[2,2048,128]{2,1,0:T(8,128)(2,1)}, bf16[2,2048,128]{2,1,0:T(8,128)(2,1)}, u32[]{:S(2)}, u32[]{:S(2)}) collective-permute-start(bf16[2,2048,128]{2,1,0:T(8,128)(2,1)} %get-tuple-element.205), channel_id=1, source_target_pairs={{0,8},{4,12},{8,0},{12,4},{1,9},{5,13},{9,1},{13,5},{2,10},{6,14},... | collective-permute-start | bytes 3145736 | tf_op jit(solution)/shard_map/ppermute | solution.py:12
  59.0 12.1 %collective-permute-start.21 = (bf16[512,512]{1,0:T(8,128)(2,1)S(1)}, bf16[512,512]{1,0:T(8,128)(2,1)S(1)}, u32[]{:S(2)}, u32[]{:S(2)}) collective-permute-start(bf16[512,512]{1,0:T(8,128)(2,1)S(1)} %collective-permute-done.13.refs_1_), channel_id=1, source_target_pairs={{0,4},{4,0},{8,12},{12,8},{1,5},{5,1},{9,13},{13,9},{2,6},{6,2},{1... | collective-permute-start | bytes 1572872 | tf_op jit(solution)/shard_map/ppermute | solution.py:12
  71.0 16.0 %collective-permute-start.30 = (bf16[1,2048,128]{2,1,0:T(8,128)(2,1)}, bf16[1,2048,128]{2,1,0:T(8,128)(2,1)}, u32[]{:S(2)}, u32[]{:S(2)}) collective-permute-start(bf16[1,2048,128]{2,1,0:T(8,128)(2,1)} %get-tuple-element.212), channel_id=1, source_target_pairs={{0,8},{4,12},{8,0},{12,4},{1,9},{5,13},{9,1},{13,5},{2,10},{6,14},... | collective-permute-start | bytes 1572872 | tf_op jit(solution)/shard_map/ppermute | solution.py:12
  74.6 57.4 %collective-permute-start.25 = (bf16[832,512]{1,0:T(8,128)(2,1)}, bf16[832,512]{1,0:T(8,128)(2,1)}, u32[]{:S(2)}, u32[]{:S(2)}) collective-permute-start(bf16[832,512]{1,0:T(8,128)(2,1)} %shard_map.88), channel_id=1, source_target_pairs={{0,2},{1,3},{2,0},{3,1},{4,6},{5,7},{6,4},{7,5},{8,10},{9,11},{10,... | collective-permute-start | bytes 2555912 | tf_op jit(solution)/shard_map/ppermute | solution.py:12
  77.6 54.4 %collective-permute-start.32 = (bf16[832,512]{1,0:T(8,128)(2,1)}, bf16[832,512]{1,0:T(8,128)(2,1)}, u32[]{:S(2)}, u32[]{:S(2)}) collective-permute-start(bf16[832,512]{1,0:T(8,128)(2,1)} %shard_map.89), channel_id=1, source_target_pairs={{0,1},{1,0},{2,3},{3,2},{4,5},{5,4},{6,7},{7,6},{8,9},{9,8},{10,11... | collective-permute-start | bytes 2555912 | tf_op jit(solution)/shard_map/ppermute | solution.py:12
  95.4 17.2 %collective-permute-start = (bf16[1,2048,128]{2,1,0:T(8,128)(2,1)S(1)}, bf16[1,2048,128]{2,1,0:T(8,128)(2,1)S(1)}, u32[]{:S(2)}, u32[]{:S(2)}) collective-permute-start(bf16[1,2048,128]{2,1,0:T(8,128)(2,1)S(1)} %get-tuple-element.86), channel_id=1, source_target_pairs={{0,8},{4,12},{8,0},{12,4},{1,9},{5,13},{9,1},{13,5},{2,10},{6,14},... | collective-permute-start | bytes 1572872 | tf_op jit(solution)/shard_map/cond/branch_1_fun/ppermute | solution.py:12
  96.7 10.5 %collective-permute-start.1 = (bf16[1,2,64,256]{3,2,1,0:T(8,128)(2,1)S(1)}, bf16[1,2,64,256]{3,2,1,0:T(8,128)(2,1)}, u32[]{:S(2)}, u32[]{:S(2)}) collective-permute-start(bf16[1,2,64,256]{3,2,1,0:T(8,128)(2,1)S(1)} %get-tuple-element.87), channel_id=1, source_target_pairs={{0,8},{4,12},{8,0},{12,4},{1,9},{5,13},{9,1},{13,5},{2,10},{6,14},... | collective-permute-start | bytes 196616 | tf_op jit(solution)/shard_map/cond/branch_1_fun/ppermute | solution.py:12
  121.7 9.4 %collective-permute-start.29 = (bf16[5,2,64,256]{3,2,1,0:T(8,128)(2,1)S(1)}, bf16[5,2,64,256]{3,2,1,0:T(8,128)(2,1)}, u32[]{:S(2)}, u32[]{:S(2)}) collective-permute-start(bf16[5,2,64,256]{3,2,1,0:T(8,128)(2,1)S(1)} %copy-done.8), channel_id=1, source_target_pairs={{0,8},{4,12},{8,0},{12,4},{1,9},{5,13},{9,1},{13,5},{2,10},{6,14},... | collective-permute-start | bytes 983048 | tf_op jit(solution)/shard_map/ppermute | solution.py:12
  122.9 9.0 %collective-permute-start.33 = (bf16[1024,128]{1,0:T(8,128)(2,1)S(1)}, bf16[1024,128]{1,0:T(8,128)(2,1)S(1)}, u32[]{:S(2)}, u32[]{:S(2)}) collective-permute-start(bf16[1024,128]{1,0:T(8,128)(2,1)S(1)} %add.211.refs_2_), channel_id=1, source_target_pairs={{0,1},{1,0},{2,3},{3,2},{4,5},{5,4},{6,7},{7,6},{8,9},{9,8},{10,11... | collective-permute-start | bytes 786440 | tf_op jit(solution)/shard_map/ppermute | solution.py:12
  131.1 16.2 %collective-permute-start.35 = (bf16[5,2,64,256]{3,2,1,0:T(8,128)(2,1)}, bf16[5,2,64,256]{3,2,1,0:T(8,128)(2,1)}, u32[]{:S(2)}, u32[]{:S(2)}) collective-permute-start(bf16[5,2,64,256]{3,2,1,0:T(8,128)(2,1)} %collective-permute-done.29.refs_7_), channel_id=1, source_target_pairs={{0,4},{4,0},{8,12},{12,8},{1,5},{5,1},{9,13},{13,9},{2,6},{6,2},{1... | collective-permute-start | bytes 983048 | tf_op jit(solution)/shard_map/ppermute | solution.py:12
  133.5 13.7 %collective-permute-start.34 = (bf16[1024,128]{1,0:T(8,128)(2,1)}, bf16[1024,128]{1,0:T(8,128)(2,1)}, u32[]{:S(2)}, u32[]{:S(2)}) collective-permute-start(bf16[1024,128]{1,0:T(8,128)(2,1)} %add_convert_fusion), channel_id=1, source_target_pairs={{0,2},{1,3},{2,0},{3,1},{4,6},{5,7},{6,4},{7,5},{8,10},{9,11},{10,... | collective-permute-start | bytes 786440 | tf_op jit(solution)/shard_map/ppermute | solution.py:12
  (36 other events, 351.4 us)

commit v6 on v5

--- a/solution.py
+++ b/solution.py
@@ -637,10 +637,10 @@
     near_ups = [
         flip(ready(up), "dp", ranks, 2 * (i + 1)) for i, (*_, up) in enumerate(picked)
     ]
-    share_pages(2)
     at = share * plane + jnp.arange(plane, dtype=jnp.int32)
     own = mark(side_by_side(at, ready(key_value_weight), part, 0, plane)[0])
     own = own.reshape(features, columns)
+    share_pages(2)
     pools = [adapter_down_weight] + sum((shared[i] for i in range(3)), []) + more_pools
     shrink, mate_shrink = mark(
         tile_shrink(kind, places, ready(input_rows), mate_rows, pools, tiles)

time: 153 us -> 144 us (0.941)
  waiting for transfers between devices: 61.7 us -> 56.2 us
  starting transfers between devices: 28.2 us -> 23.7 us
    ppermute x30 -> x27, waiting for transfers between devices: 61.7 us -> 56.2 us  [flip(): return lax.ppermute(x, axis, [(i, i ^ mask) for i in range(size)])]
    ppermute x30 -> x27, starting transfers between devices: 28.2 us -> 23.7 us  [flip(): return lax.ppermute(x, axis, [(i, i ^ mask) for i in range(size)])]
    pallas_call x1, Pallas kernels: 3.3 us -> 5.03 us  [tile_shrink(): pl.pallas_call(functools.partial(shrink_kernel, len(pools), tiles), out_s...]
    pallas_call x2 -> x1, Pallas kernels: 5.41 us -> 4.03 us  [pick_pages(): pl.pallas_call(functools.partial(pick_kernel, low, cuts), out_shape=[jax....]
  transfers between devices with their start and end apart: 30 -> 27, of which waited for: 11 -> 11; matrix products, arithmetic and copies ran while one was open for 6% -> 7% of each run, Pallas kernels for 28% -> 30%
where the time goes in v6:
time: 144 us; the launch traced here: 142 us
  waiting for transfers between devices  56.2 us (39%)
  Pallas kernels  47.2 us (33%)
  starting transfers between devices  23.7 us (16%)
  local copies, waits for them, and re-layouts  7.07 us (5%)
  other arithmetic  5.34 us (4%)
  between operations  2.36 us (2%)
    ppermute x27, waiting for transfers between devices, flip(): return lax.ppermute(x, axis, [(i, i ^ mask) for i in range(size)])  56.2 us
    ppermute x27, starting transfers between devices, flip(): return lax.ppermute(x, axis, [(i, i ^ mask) for i in range(size)])  23.7 us
    pallas_call x4, Pallas kernels, multiply(): pl.pallas_call(functools.partial(multiply_kernel, len(weights), len(added...  12.8 us
    pallas_call x3, Pallas kernels, side_by_side(): pl.pallas_call(lambda at, *refs: side_kernel(*refs), out_shape=[jax.Shape...  12.2 us
    pallas_call x1, Pallas kernels, pack(): pl.pallas_call(functools.partial(pack_kernel, first), out_shape=[jax.Shap...  7.24 us
    pallas_call x1, Pallas kernels, tile_shrink(): pl.pallas_call(functools.partial(shrink_kernel, len(pools), tiles), out_s...  5.03 us
    pallas_call x1, Pallas kernels, finish(): pl.pallas_call(functools.partial(finish_kernel, len(pools), len(parts)),...  4.95 us
    pallas_call x1, Pallas kernels, pick_pages(): pl.pallas_call(functools.partial(pick_kernel, low, cuts), out_shape=[jax....  4.03 us
  transfers between devices with their start and end apart: 27, of which 11 were waited for; matrix products, arithmetic and copies ran while one was open for 7% of the time, Pallas kernels for 30%

profile of v6, /device:TPU:3, one launch (start us, length us, event | category | flops | bytes accessed | tf_op | source)
XLA Modules:
  0.0 141.9 jit_solution(16242264874986923375)
XLA Ops:
  2.4 3.4 %collective-permute-start.9 = (bf16[256,512]{1,0:T(8,128)(2,1)S(1)}, bf16[256,512]{1,0:T(8,128)(2,1)S(1)}, u32[]{:S(2)}, u32[]{:S(2)}) collective-permute-start(bf16[256,512]{1,0:T(8,128)(2,1)S(1)} %bitcast.46), channel_id=1, source_target_pairs={{0,3},{1,2},{2,1},{3,0},{4,7},{5,6},{6,5},{7,4},{8,11},{9,10},{10,... | collective-permute-start | bytes 786440 | tf_op jit(solution)/shard_map/ppermute | solution.py:12
  10.6 2.7 %shard_map.82 = bf16[2,256,512]{2,1,0:T(8,128)(2,1)} custom-call(s32[5]{0:T(128)} %xor_add_fusion.at, bf16[8192,2,256]{2,1,0:T(2,128)(2,1)} %refs_0_.2), custom_call_target="tpu_custom_call" | custom-call | tf_op jit(solution)/shard_map/pallas_call | solution.py:78
  13.2 2.8 %shard_map.83 = bf16[2,256,512]{2,1,0:T(8,128)(2,1)} custom-call(s32[5]{0:T(128)} %xor_add_fusion.at, bf16[8192,2,256]{2,1,0:T(2,128)(2,1)} %refs_0_.2), custom_call_target="tpu_custom_call" | custom-call | tf_op jit(solution)/shard_map/pallas_call | solution.py:78
  19.7 4.9 %collective-permute-done.11 = bf16[256,512]{1,0:T(8,128)(2,1)S(1)} collective-permute-done((bf16[256,512]{1,0:T(8,128)(2,1)S(1)}, bf16[256,512]{1,0:T(8,128)(2,1)S(1)}, u32[]{:S(2)}, u32[]{:S(2)}) %collective-permute-start.11) | collective-permute-done | bytes 262176 | tf_op jit(solution)/shard_map/ppermute | solution.py:12
  25.0 4.0 %shard_map.85 = (bf16[2,2048,128]{2,1,0:T(8,128)(2,1)S(1)}, bf16[2,2048,128]{2,1,0:T(8,128)(2,1)}, bf16[1,2048,128]{2,1,0:T(8,128)(2,1)}, bf16[5,2,64,256]{3,2,1,0:T(8,128)(2,1)S(1)}) custom-call(s32[8]{0:T(128)S(1)} %compare_select_fusion.18.own_at, s32[8]{0:T(128)S(1)} %get-tuple-element.237.mate_at, s32[8]{0:T(128)S(1)} %get-tuple-element.238.mine, ...), custom_call_target="tpu_custom_call" | custom-call | tf_op jit(solution)/shard_map/pallas_call | solution.py:48
  30.1 1.6 %collective-permute-start.20 = (bf16[512,512]{1,0:T(8,128)(2,1)S(1)}, bf16[512,512]{1,0:T(8,128)(2,1)S(1)}, u32[]{:S(2)}, u32[]{:S(2)}) collective-permute-start(bf16[512,512]{1,0:T(8,128)(2,1)S(1)} %constant_dynamic-update-slice_fusion.refs_0_), channel_id=1, source_target_pairs={{0,4},{4,0},{8,12},{12,8},{1,5},{5,1},{9,13},{13,9},{2,6},{6,2},{1... | collective-permute-start | bytes 1572872 | tf_op jit(solution)/shard_map/ppermute | solution.py:12
  31.9 7.2 %shard_map.84 = (bf16[832,2048]{1,0:T(8,128)(2,1)S(1)}, bf16[832,2048]{1,0:T(8,128)(2,1)S(1)}) custom-call(s32[8]{0:T(128)S(1)} %iota_xor_fusion.at, s32[1,1024]{1,0:T(1,128)S(1)} %bitcast.38, bf16[1024,2048]{1,0:T(8,128)(2,1)S(1)} %copy-done.9), custom_call_target="tpu_custom_call" | custom-call | tf_op jit(solution)/shard_map/pallas_call | solution.py:108
  39.1 5.4 %collective-permute-done.12.refs_0_ = bf16[512,512]{1,0:T(8,128)(2,1)S(1)} collective-permute-done((bf16[512,512]{1,0:T(8,128)(2,1)}, bf16[512,512]{1,0:T(8,128)(2,1)S(1)}, u32[]{:S(2)}, u32[]{:S(2)}) %collective-permute-start.12) | collective-permute-done | bytes 524320 | tf_op jit(solution)/shard_map/ppermute | solution.py:12
  47.5 2.1 %shard_map.86 = bf16[832,512]{1,0:T(8,128)(2,1)S(1)} custom-call(bf16[832,2048]{1,0:T(8,128)(2,1)S(1)} %get-tuple-element.208.x, bf16[512,512]{1,0:T(8,128)(2,1)S(1)} %constant_dynamic-update-slice_fusion.refs_0_, bf16[512,512]{1,0:T(8,128)(2,1)S(1)} %collective-permute-done.17.refs_1_, bf16[512,512]{1,0:T(8,128)(2,1)S(1)} %collective-permute-done.20.refs_2_, ...), custom_call_target="tpu_custom_call" | custom-call | tf_op jit(solution)/shard_map/pallas_call | solution.py:193
  49.9 2.7 %collective-permute-done.16.refs_3_ = bf16[2,2048,128]{2,1,0:T(8,128)(2,1)S(1)} collective-permute-done((bf16[2,2048,128]{2,1,0:T(8,128)(2,1)S(1)}, bf16[2,2048,128]{2,1,0:T(8,128)(2,1)S(1)}, u32[]{:S(2)}, u32[]{:S(2)}) %collective-permute-start.16) | collective-permute-done | bytes 1048608 | tf_op jit(solution)/shard_map/ppermute | solution.py:12
  54.4 4.5 %collective-permute-done.13.refs_1_ = bf16[512,512]{1,0:T(8,128)(2,1)S(1)} collective-permute-done((bf16[512,512]{1,0:T(8,128)(2,1)S(1)}, bf16[512,512]{1,0:T(8,128)(2,1)S(1)}, u32[]{:S(2)}, u32[]{:S(2)}) %collective-permute-start.13) | collective-permute-done | bytes 524320 | tf_op jit(solution)/shard_map/ppermute | solution.py:12
  60.2 10.0 %collective-permute-done.23.refs_1_ = bf16[512,512]{1,0:T(8,128)(2,1)S(1)} collective-permute-done((bf16[512,512]{1,0:T(8,128)(2,1)S(1)}, bf16[512,512]{1,0:T(8,128)(2,1)S(1)}, u32[]{:S(2)}, u32[]{:S(2)}) %collective-permute-start.23) | collective-permute-done | bytes 524320 | tf_op jit(solution)/shard_map/ppermute | solution.py:12
  71.4 2.1 %shard_map.87.refs_0_ = f32[832,512]{1,0:T(8,128)S(1)} custom-call(bf16[832,2048]{1,0:T(8,128)(2,1)S(1)} %get-tuple-element.208.x, bf16[512,512]{1,0:T(8,128)(2,1)S(1)} %collective-permute-done.12.refs_0_, bf16[512,512]{1,0:T(8,128)(2,1)S(1)} %collective-permute-done.13.refs_1_, bf16[512,512]{1,0:T(8,128)(2,1)S(1)} %collective-permute-done.22.refs_2_, ...), custom_call_target="tpu_custom_call" | custom-call | tf_op jit(solution)/shard_map/pallas_call | solution.py:193
  74.7 2.9 %shard_map.89 = bf16[832,512]{1,0:T(8,128)(2,1)} custom-call(bf16[832,2048]{1,0:T(8,128)(2,1)S(1)} %get-tuple-element.208.x, bf16[512,512]{1,0:T(8,128)(2,1)S(1)} %collective-permute-done.18.refs_0_, bf16[512,512]{1,0:T(8,128)(2,1)S(1)} %collective-permute-done.23.refs_1_, bf16[512,512]{1,0:T(8,128)(2,1)S(1)} %collective-permute-done.28.refs_2_, ...), custom_call_target="tpu_custom_call" | custom-call | tf_op jit(solution)/shard_map/pallas_call | solution.py:193
  80.6 6.7 %shard_map.90 = bf16[8,256,512]{2,1,0:T(8,128)(2,1)} custom-call(s32[8]{0:T(128)} %iota_add_fusion.at, bf16[8192,2,256]{2,1,0:T(2,128)(2,1)} %refs_0_.2), custom_call_target="tpu_custom_call" | custom-call | tf_op jit(solution)/shard_map/pallas_call | solution.py:78
  88.9 5.0 %shard_map.91 = (bf16[1024,128]{1,0:T(8,128)(2,1)S(1)}, bf16[1024,128]{1,0:T(8,128)(2,1)S(1)}) custom-call(s32[16]{0:T(128)S(1)} %get-tuple-element.245.kind, s32[16]{0:T(128)S(1)} %get-tuple-element.234.places, bf16[1024,2048]{1,0:T(8,128)(2,1)} %refs_0_.3, bf16[1024,2048]{1,0:T(8,128)(2,1)} %collective-permute-done.15.refs_1_, ...), custom_call_target="tpu_custom_call" | custom-call | tf_op jit(solution)/shard_map/pallas_call | solution.py:239
  93.9 2.5 %collective-permute-start.31 = (bf16[1024,128]{1,0:T(8,128)(2,1)S(1)}, bf16[1024,128]{1,0:T(8,128)(2,1)S(1)}, u32[]{:S(2)}, u32[]{:S(2)}) collective-permute-start(bf16[1024,128]{1,0:T(8,128)(2,1)S(1)} %get-tuple-element.220), channel_id=1, source_target_pairs={{0,4},{4,0},{8,12},{12,8},{1,5},{5,1},{9,13},{13,9},{2,6},{6,2},{1... | collective-permute-start | bytes 786440 | tf_op jit(solution)/shard_map/ppermute | solution.py:12
  96.4 3.0 %collective-permute-start.29 = (bf16[5,2,64,256]{3,2,1,0:T(8,128)(2,1)S(1)}, bf16[5,2,64,256]{3,2,1,0:T(8,128)(2,1)}, u32[]{:S(2)}, u32[]{:S(2)}) collective-permute-start(bf16[5,2,64,256]{3,2,1,0:T(8,128)(2,1)S(1)} %copy-done.8), channel_id=1, source_target_pairs={{0,8},{4,12},{8,0},{12,4},{1,9},{5,13},{9,1},{13,5},{2,10},{6,14},... | collective-permute-start | bytes 983048 | tf_op jit(solution)/shard_map/ppermute | solution.py:12
  99.6 7.9 %collective-permute-done.29.refs_7_ = bf16[5,2,64,256]{3,2,1,0:T(8,128)(2,1)} collective-permute-done((bf16[5,2,64,256]{3,2,1,0:T(8,128)(2,1)S(1)}, bf16[5,2,64,256]{3,2,1,0:T(8,128)(2,1)}, u32[]{:S(2)}, u32[]{:S(2)}) %collective-permute-start.29) | collective-permute-done | bytes 327712 | tf_op jit(solution)/shard_map/ppermute | solution.py:12
  108.2 6.5 %collective-permute-done.25.refs_2_ = bf16[832,512]{1,0:T(8,128)(2,1)} collective-permute-done((bf16[832,512]{1,0:T(8,128)(2,1)}, bf16[832,512]{1,0:T(8,128)(2,1)}, u32[]{:S(2)}, u32[]{:S(2)}) %collective-permute-start.25) | collective-permute-done | bytes 852000 | tf_op jit(solution)/shard_map/ppermute | solution.py:12
  115.6 5.5 %collective-permute-done.33.refs_3_ = bf16[1024,128]{1,0:T(8,128)(2,1)S(1)} collective-permute-done((bf16[1024,128]{1,0:T(8,128)(2,1)S(1)}, bf16[1024,128]{1,0:T(8,128)(2,1)S(1)}, u32[]{:S(2)}, u32[]{:S(2)}) %collective-permute-start.33) | collective-permute-done | bytes 262176 | tf_op jit(solution)/shard_map/ppermute | solution.py:12
  123.6 5.7 %shard_map.92.refs_0_ = f32[1152,512]{1,0:T(8,128)S(1)} custom-call(bf16[832,2048]{1,0:T(8,128)(2,1)S(1)} %get-tuple-element.228.x, bf16[2048,512]{1,0:T(8,128)(2,1)} %bitcast.43, bf16[832,512]{1,0:T(8,128)(2,1)} %collective-permute-done.32.refs_1_, bf16[832,512]{1,0:T(8,128)(2,1)} %collective-permute-done.25.refs_2_), custom_call_target="tpu_custom_call" | custom-call | tf_op jit(solution)/shard_map/pallas_call | solution.py:193
  129.3 7.4 %collective-permute-done.34.refs_4_ = bf16[1024,128]{1,0:T(8,128)(2,1)} collective-permute-done((bf16[1024,128]{1,0:T(8,128)(2,1)}, bf16[1024,128]{1,0:T(8,128)(2,1)}, u32[]{:S(2)}, u32[]{:S(2)}) %collective-permute-start.34) | collective-permute-done | bytes 262176 | tf_op jit(solution)/shard_map/ppermute | solution.py:12
  136.8 4.9 %shard_map.93 = bf16[1024,2,256]{2,1,0:T(2,128)(2,1)} custom-call(s32[8]{0:T(128)S(1)} %get-tuple-element.250.offsets, s32[8]{0:T(128)S(1)} %copy-done.6, s32[8]{0:T(128)S(1)} %bitcast.40, s32[8]{0:T(128)S(1)} %bitcast.41, f32[1152,512]{1,0:T(8,128)S(1)} %shard_map.92.refs_0_, f32[192,512]{1,0:T(8,128)S(1)} %copy-done.39, bf16[1024,128]{1,0:T(8,128)(2,1)S(1)} %copy-done.1, ...), custom_call_target="tpu_custom_call" | custom-call | tf_op jit(solution)/shard_map/pallas_call | solution.py:333
  (145 shorter events, 27.8 us)
Async XLA Ops:
  0.0 25.0 %collective-permute-start.14 = (bf16[16,2048,128]{2,1,0:T(8,128)(2,1)}, bf16[16,2048,128]{2,1,0:T(8,128)(2,1)}, u32[]{:S(2)}, u32[]{:S(2)}) collective-permute-start(bf16[16,2048,128]{2,1,0:T(8,128)(2,1)} %refs_2_.1), channel_id=1, source_target_pairs={{0,4},{4,0},{8,12},{12,8},{1,5},{5,1},{9,13},{13,9},{2,6},{6,2},{1... | collective-permute-start | bytes 25165832 | tf_op jit(solution)/shard_map/ppermute | solution.py:12
  0.7 24.3 %collective-permute-start.15 = (bf16[1024,2048]{1,0:T(8,128)(2,1)}, bf16[1024,2048]{1,0:T(8,128)(2,1)}, u32[]{:S(2)}, u32[]{:S(2)}) collective-permute-start(bf16[1024,2048]{1,0:T(8,128)(2,1)} %refs_0_.3), channel_id=1, source_target_pairs={{0,4},{4,0},{8,12},{12,8},{1,5},{5,1},{9,13},{13,9},{2,6},{6,2},{1... | collective-permute-start | bytes 12582920 | tf_op jit(solution)/shard_map/ppermute | solution.py:12
  0.7 16.2 %collective-permute-start.10 = (bf16[16,2,64,256]{3,2,1,0:T(8,128)(2,1)}, bf16[16,2,64,256]{3,2,1,0:T(8,128)(2,1)S(1)}, u32[]{:S(2)}, u32[]{:S(2)}) collective-permute-start(bf16[16,2,64,256]{3,2,1,0:T(8,128)(2,1)} %refs_5_.1), channel_id=1, source_target_pairs={{0,4},{4,0},{8,12},{12,8},{1,5},{5,1},{9,13},{13,9},{2,6},{6,2},{1... | collective-permute-start | bytes 3145736 | tf_op jit(solution)/shard_map/ppermute | solution.py:12
  2.4 14.6 %collective-permute-start.9 = (bf16[256,512]{1,0:T(8,128)(2,1)S(1)}, bf16[256,512]{1,0:T(8,128)(2,1)S(1)}, u32[]{:S(2)}, u32[]{:S(2)}) collective-permute-start(bf16[256,512]{1,0:T(8,128)(2,1)S(1)} %bitcast.46), channel_id=1, source_target_pairs={{0,3},{1,2},{2,1},{3,0},{4,7},{5,6},{6,5},{7,4},{8,11},{9,10},{10,... | collective-permute-start | bytes 786440 | tf_op jit(solution)/shard_map/ppermute | solution.py:12
  16.9 7.7 %collective-permute-start.11 = (bf16[256,512]{1,0:T(8,128)(2,1)S(1)}, bf16[256,512]{1,0:T(8,128)(2,1)S(1)}, u32[]{:S(2)}, u32[]{:S(2)}) collective-permute-start(bf16[256,512]{1,0:T(8,128)(2,1)S(1)} %collective-permute-done.9), channel_id=1, source_target_pairs={{0,8},{4,12},{8,0},{12,4},{1,9},{5,13},{9,1},{13,5},{2,10},{6,14},... | collective-permute-start | bytes 786440 | tf_op jit(solution)/shard_map/ppermute | solution.py:12
  18.3 26.2 %collective-permute-start.12 = (bf16[512,512]{1,0:T(8,128)(2,1)}, bf16[512,512]{1,0:T(8,128)(2,1)S(1)}, u32[]{:S(2)}, u32[]{:S(2)}) collective-permute-start(bf16[512,512]{1,0:T(8,128)(2,1)} %bitcast.9), channel_id=1, source_target_pairs={{0,2},{1,3},{2,0},{3,1},{4,6},{5,7},{6,4},{7,5},{8,10},{9,11},{10,... | collective-permute-start | bytes 1572872 | tf_op jit(solution)/shard_map/ppermute | solution.py:12
  19.6 24.9 %collective-permute-start.18 = (bf16[512,512]{1,0:T(8,128)(2,1)}, bf16[512,512]{1,0:T(8,128)(2,1)S(1)}, u32[]{:S(2)}, u32[]{:S(2)}) collective-permute-start(bf16[512,512]{1,0:T(8,128)(2,1)} %bitcast.45), channel_id=1, source_target_pairs={{0,1},{1,0},{2,3},{3,2},{4,5},{5,4},{6,7},{7,6},{8,9},{9,8},{10,11... | collective-permute-start | bytes 1572872 | tf_op jit(solution)/shard_map/ppermute | solution.py:12
  24.6 19.9 %collective-permute-start.17 = (bf16[512,512]{1,0:T(8,128)(2,1)S(1)}, bf16[512,512]{1,0:T(8,128)(2,1)S(1)}, u32[]{:S(2)}, u32[]{:S(2)}) collective-permute-start(bf16[512,512]{1,0:T(8,128)(2,1)S(1)} %constant_dynamic-update-slice_fusion.refs_0_), channel_id=1, source_target_pairs={{0,16},{16,0},{1,17},{17,1},{2,18},{18,2},{3,19},{19,3},{4,20},{20... | collective-permute-start | bytes 1572872 | tf_op jit(solution)/shard_map/ppermute | solution.py:12
  29.0 23.5 %collective-permute-start.16 = (bf16[2,2048,128]{2,1,0:T(8,128)(2,1)S(1)}, bf16[2,2048,128]{2,1,0:T(8,128)(2,1)S(1)}, u32[]{:S(2)}, u32[]{:S(2)}) collective-permute-start(bf16[2,2048,128]{2,1,0:T(8,128)(2,1)S(1)} %get-tuple-element.189), channel_id=1, source_target_pairs={{0,8},{4,12},{8,0},{12,4},{1,9},{5,13},{9,1},{13,5},{2,10},{6,14},... | collective-permute-start | bytes 3145736 | tf_op jit(solution)/shard_map/ppermute | solution.py:12
  30.1 16.7 %collective-permute-start.20 = (bf16[512,512]{1,0:T(8,128)(2,1)S(1)}, bf16[512,512]{1,0:T(8,128)(2,1)S(1)}, u32[]{:S(2)}, u32[]{:S(2)}) collective-permute-start(bf16[512,512]{1,0:T(8,128)(2,1)S(1)} %constant_dynamic-update-slice_fusion.refs_0_), channel_id=1, source_target_pairs={{0,4},{4,0},{8,12},{12,8},{1,5},{5,1},{9,13},{13,9},{2,6},{6,2},{1... | collective-permute-start | bytes 1572872 | tf_op jit(solution)/shard_map/ppermute | solution.py:12
  45.4 13.5 %collective-permute-start.13 = (bf16[512,512]{1,0:T(8,128)(2,1)S(1)}, bf16[512,512]{1,0:T(8,128)(2,1)S(1)}, u32[]{:S(2)}, u32[]{:S(2)}) collective-permute-start(bf16[512,512]{1,0:T(8,128)(2,1)S(1)} %collective-permute-done.12.refs_0_), channel_id=1, source_target_pairs={{0,16},{16,0},{1,17},{17,1},{2,18},{18,2},{3,19},{19,3},{4,20},{20... | collective-permute-start | bytes 1572872 | tf_op jit(solution)/shard_map/ppermute | solution.py:12
  45.6 24.6 %collective-permute-start.23 = (bf16[512,512]{1,0:T(8,128)(2,1)S(1)}, bf16[512,512]{1,0:T(8,128)(2,1)S(1)}, u32[]{:S(2)}, u32[]{:S(2)}) collective-permute-start(bf16[512,512]{1,0:T(8,128)(2,1)S(1)} %collective-permute-done.18.refs_0_), channel_id=1, source_target_pairs={{0,16},{16,0},{1,17},{17,1},{2,18},{18,2},{3,19},{19,3},{4,20},{20... | collective-permute-start | bytes 1572872 | tf_op jit(solution)/shard_map/ppermute | solution.py:12
  46.9 24.1 %collective-permute-start.22 = (bf16[512,512]{1,0:T(8,128)(2,1)S(1)}, bf16[512,512]{1,0:T(8,128)(2,1)S(1)}, u32[]{:S(2)}, u32[]{:S(2)}) collective-permute-start(bf16[512,512]{1,0:T(8,128)(2,1)S(1)} %collective-permute-done.12.refs_0_), channel_id=1, source_target_pairs={{0,4},{4,0},{8,12},{12,8},{1,5},{5,1},{9,13},{13,9},{2,6},{6,2},{1... | collective-permute-start | bytes 1572872 | tf_op jit(solution)/shard_map/ppermute | solution.py:12
  49.6 23.9 %collective-permute-start.24 = (bf16[832,512]{1,0:T(8,128)(2,1)S(1)}, bf16[832,512]{1,0:T(8,128)(2,1)S(1)}, u32[]{:S(2)}, u32[]{:S(2)}) collective-permute-start(bf16[832,512]{1,0:T(8,128)(2,1)S(1)} %shard_map.86), channel_id=1, source_target_pairs={{0,1},{1,0},{2,3},{3,2},{4,5},{5,4},{6,7},{7,6},{8,9},{9,8},{10,11... | collective-permute-start | bytes 2555912 | tf_op jit(solution)/shard_map/ppermute | solution.py:12
  53.5 27.0 %collective-permute-start.26 = (bf16[2,2048,128]{2,1,0:T(8,128)(2,1)}, bf16[2,2048,128]{2,1,0:T(8,128)(2,1)}, u32[]{:S(2)}, u32[]{:S(2)}) collective-permute-start(bf16[2,2048,128]{2,1,0:T(8,128)(2,1)} %get-tuple-element.205), channel_id=1, source_target_pairs={{0,8},{4,12},{8,0},{12,4},{1,9},{5,13},{9,1},{13,5},{2,10},{6,14},... | collective-permute-start | bytes 3145736 | tf_op jit(solution)/shard_map/ppermute | solution.py:12
  58.9 12.2 %collective-permute-start.21 = (bf16[512,512]{1,0:T(8,128)(2,1)S(1)}, bf16[512,512]{1,0:T(8,128)(2,1)S(1)}, u32[]{:S(2)}, u32[]{:S(2)}) collective-permute-start(bf16[512,512]{1,0:T(8,128)(2,1)S(1)} %collective-permute-done.13.refs_1_), channel_id=1, source_target_pairs={{0,4},{4,0},{8,12},{12,8},{1,5},{5,1},{9,13},{13,9},{2,6},{6,2},{1... | collective-permute-start | bytes 1572872 | tf_op jit(solution)/shard_map/ppermute | solution.py:12
  71.0 16.6 %collective-permute-start.30 = (bf16[1,2048,128]{2,1,0:T(8,128)(2,1)}, bf16[1,2048,128]{2,1,0:T(8,128)(2,1)}, u32[]{:S(2)}, u32[]{:S(2)}) collective-permute-start(bf16[1,2048,128]{2,1,0:T(8,128)(2,1)} %get-tuple-element.212), channel_id=1, source_target_pairs={{0,8},{4,12},{8,0},{12,4},{1,9},{5,13},{9,1},{13,5},{2,10},{6,14},... | collective-permute-start | bytes 1572872 | tf_op jit(solution)/shard_map/ppermute | solution.py:12
  74.6 40.2 %collective-permute-start.25 = (bf16[832,512]{1,0:T(8,128)(2,1)}, bf16[832,512]{1,0:T(8,128)(2,1)}, u32[]{:S(2)}, u32[]{:S(2)}) collective-permute-start(bf16[832,512]{1,0:T(8,128)(2,1)} %shard_map.88), channel_id=1, source_target_pairs={{0,2},{1,3},{2,0},{3,1},{4,6},{5,7},{6,4},{7,5},{8,10},{9,11},{10,... | collective-permute-start | bytes 2555912 | tf_op jit(solution)/shard_map/ppermute | solution.py:12
  77.6 38.1 %collective-permute-start.32 = (bf16[832,512]{1,0:T(8,128)(2,1)}, bf16[832,512]{1,0:T(8,128)(2,1)}, u32[]{:S(2)}, u32[]{:S(2)}) collective-permute-start(bf16[832,512]{1,0:T(8,128)(2,1)} %shard_map.89), channel_id=1, source_target_pairs={{0,1},{1,0},{2,3},{3,2},{4,5},{5,4},{6,7},{7,6},{8,9},{9,8},{10,11... | collective-permute-start | bytes 2555912 | tf_op jit(solution)/shard_map/ppermute | solution.py:12
  93.9 5.6 %collective-permute-start.31 = (bf16[1024,128]{1,0:T(8,128)(2,1)S(1)}, bf16[1024,128]{1,0:T(8,128)(2,1)S(1)}, u32[]{:S(2)}, u32[]{:S(2)}) collective-permute-start(bf16[1024,128]{1,0:T(8,128)(2,1)S(1)} %get-tuple-element.220), channel_id=1, source_target_pairs={{0,4},{4,0},{8,12},{12,8},{1,5},{5,1},{9,13},{13,9},{2,6},{6,2},{1... | collective-permute-start | bytes 786440 | tf_op jit(solution)/shard_map/ppermute | solution.py:12
  96.4 11.1 %collective-permute-start.29 = (bf16[5,2,64,256]{3,2,1,0:T(8,128)(2,1)S(1)}, bf16[5,2,64,256]{3,2,1,0:T(8,128)(2,1)}, u32[]{:S(2)}, u32[]{:S(2)}) collective-permute-start(bf16[5,2,64,256]{3,2,1,0:T(8,128)(2,1)S(1)} %copy-done.8), channel_id=1, source_target_pairs={{0,8},{4,12},{8,0},{12,4},{1,9},{5,13},{9,1},{13,5},{2,10},{6,14},... | collective-permute-start | bytes 983048 | tf_op jit(solution)/shard_map/ppermute | solution.py:12
  99.6 21.6 %collective-permute-start.33 = (bf16[1024,128]{1,0:T(8,128)(2,1)S(1)}, bf16[1024,128]{1,0:T(8,128)(2,1)S(1)}, u32[]{:S(2)}, u32[]{:S(2)}) collective-permute-start(bf16[1024,128]{1,0:T(8,128)(2,1)S(1)} %add.211.refs_2_), channel_id=1, source_target_pairs={{0,1},{1,0},{2,3},{3,2},{4,5},{5,4},{6,7},{7,6},{8,9},{9,8},{10,11... | collective-permute-start | bytes 786440 | tf_op jit(solution)/shard_map/ppermute | solution.py:12
  107.6 29.2 %collective-permute-start.35 = (bf16[5,2,64,256]{3,2,1,0:T(8,128)(2,1)}, bf16[5,2,64,256]{3,2,1,0:T(8,128)(2,1)}, u32[]{:S(2)}, u32[]{:S(2)}) collective-permute-start(bf16[5,2,64,256]{3,2,1,0:T(8,128)(2,1)} %collective-permute-done.29.refs_7_), channel_id=1, source_target_pairs={{0,4},{4,0},{8,12},{12,8},{1,5},{5,1},{9,13},{13,9},{2,6},{6,2},{1... | collective-permute-start | bytes 983048 | tf_op jit(solution)/shard_map/ppermute | solution.py:12
  122.7 14.1 %collective-permute-start.34 = (bf16[1024,128]{1,0:T(8,128)(2,1)}, bf16[1024,128]{1,0:T(8,128)(2,1)}, u32[]{:S(2)}, u32[]{:S(2)}) collective-permute-start(bf16[1024,128]{1,0:T(8,128)(2,1)} %add_convert_fusion), channel_id=1, source_target_pairs={{0,2},{1,3},{2,0},{3,1},{4,6},{5,7},{6,4},{7,5},{8,10},{9,11},{10,... | collective-permute-start | bytes 786440 | tf_op jit(solution)/shard_map/ppermute | solution.py:12
  (32 other events, 335.4 us)

commit v7 on v6

--- a/solution.py
+++ b/solution.py
@@ -584,11 +584,11 @@
     go_on(first)
     get_all(first)
     product(first)
-    share_pages(0)
     cross(1)
     cross(2)
     for k in turns[1:-1]:
         go_on(k)
+    share_pages(0)
     go_on(direct)
     for k in turns[1:-1]:
         get_all(k)

time: 144 us -> 144 us (level)
  waiting for transfers between devices: 56.2 us -> 58 us
  starting transfers between devices: 23.7 us -> 22.1 us
    ppermute x27, waiting for transfers between devices: 56.2 us -> 58 us  [flip(): return lax.ppermute(x, axis, [(i, i ^ mask) for i in range(size)])]
    ppermute x27, starting transfers between devices: 23.7 us -> 22.1 us  [flip(): return lax.ppermute(x, axis, [(i, i ^ mask) for i in range(size)])]
where the time goes in v7:
time: 144 us; the launch traced here: 142 us
  waiting for transfers between devices  58 us (40%)
  Pallas kernels  47 us (33%)
  starting transfers between devices  22.1 us (15%)
  local copies, waits for them, and re-layouts  7.06 us (5%)
  other arithmetic  5.34 us (4%)
  between operations  2.34 us (2%)
    ppermute x27, waiting for transfers between devices, flip(): return lax.ppermute(x, axis, [(i, i ^ mask) for i in range(size)])  58 us
    ppermute x27, starting transfers between devices, flip(): return lax.ppermute(x, axis, [(i, i ^ mask) for i in range(size)])  22.1 us
    pallas_call x4, Pallas kernels, multiply(): pl.pallas_call(functools.partial(multiply_kernel, len(weights), len(added...  12.8 us
    pallas_call x3, Pallas kernels, side_by_side(): pl.pallas_call(lambda at, *refs: side_kernel(*refs), out_shape=[jax.Shape...  12.2 us
    pallas_call x1, Pallas kernels, pack(): pl.pallas_call(functools.partial(pack_kernel, first), out_shape=[jax.Shap...  7.25 us
    pallas_call x1, Pallas kernels, finish(): pl.pallas_call(functools.partial(finish_kernel, len(pools), len(parts)),...  4.95 us
    pallas_call x1, Pallas kernels, tile_shrink(): pl.pallas_call(functools.partial(shrink_kernel, len(pools), tiles), out_s...  4.78 us
    pallas_call x1, Pallas kernels, pick_pages(): pl.pallas_call(functools.partial(pick_kernel, low, cuts), out_shape=[jax....  4.03 us
  transfers between devices with their start and end apart: 27, of which 11 were waited for; matrix products, arithmetic and copies ran while one was open for 7% of the time, Pallas kernels for 30%

profile of v7, /device:TPU:3, one launch (start us, length us, event | category | flops | bytes accessed | tf_op | source)
XLA Modules:
  0.0 141.9 jit_solution(12729336804599708382)
XLA Ops:
  2.4 3.4 %collective-permute-start.9 = (bf16[256,512]{1,0:T(8,128)(2,1)S(1)}, bf16[256,512]{1,0:T(8,128)(2,1)S(1)}, u32[]{:S(2)}, u32[]{:S(2)}) collective-permute-start(bf16[256,512]{1,0:T(8,128)(2,1)S(1)} %bitcast.46), channel_id=1, source_target_pairs={{0,3},{1,2},{2,1},{3,0},{4,7},{5,6},{6,5},{7,4},{8,11},{9,10},{10,... | collective-permute-start | bytes 786440 | tf_op jit(solution)/shard_map/ppermute | solution.py:12
  10.5 2.7 %shard_map.82 = bf16[2,256,512]{2,1,0:T(8,128)(2,1)} custom-call(s32[5]{0:T(128)} %xor_add_fusion.at, bf16[8192,2,256]{2,1,0:T(2,128)(2,1)} %refs_0_.2), custom_call_target="tpu_custom_call" | custom-call | tf_op jit(solution)/shard_map/pallas_call | solution.py:78
  13.2 2.8 %shard_map.83 = bf16[2,256,512]{2,1,0:T(8,128)(2,1)} custom-call(s32[5]{0:T(128)} %xor_add_fusion.at, bf16[8192,2,256]{2,1,0:T(2,128)(2,1)} %refs_0_.2), custom_call_target="tpu_custom_call" | custom-call | tf_op jit(solution)/shard_map/pallas_call | solution.py:78
  19.7 4.9 %collective-permute-done.11 = bf16[256,512]{1,0:T(8,128)(2,1)S(1)} collective-permute-done((bf16[256,512]{1,0:T(8,128)(2,1)S(1)}, bf16[256,512]{1,0:T(8,128)(2,1)S(1)}, u32[]{:S(2)}, u32[]{:S(2)}) %collective-permute-start.11) | collective-permute-done | bytes 262176 | tf_op jit(solution)/shard_map/ppermute | solution.py:12
  25.0 4.0 %shard_map.86 = (bf16[2,2048,128]{2,1,0:T(8,128)(2,1)S(1)}, bf16[2,2048,128]{2,1,0:T(8,128)(2,1)}, bf16[1,2048,128]{2,1,0:T(8,128)(2,1)}, bf16[5,2,64,256]{3,2,1,0:T(8,128)(2,1)S(1)}) custom-call(s32[8]{0:T(128)S(1)} %compare_select_fusion.18.own_at, s32[8]{0:T(128)S(1)} %get-tuple-element.237.mate_at, s32[8]{0:T(128)S(1)} %get-tuple-element.238.mine, ...), custom_call_target="tpu_custom_call" | custom-call | tf_op jit(solution)/shard_map/pallas_call | solution.py:48
  31.9 7.2 %shard_map.84 = (bf16[832,2048]{1,0:T(8,128)(2,1)S(1)}, bf16[832,2048]{1,0:T(8,128)(2,1)S(1)}) custom-call(s32[8]{0:T(128)S(1)} %iota_xor_fusion.at, s32[1,1024]{1,0:T(1,128)S(1)} %bitcast.38, bf16[1024,2048]{1,0:T(8,128)(2,1)S(1)} %copy-done.9), custom_call_target="tpu_custom_call" | custom-call | tf_op jit(solution)/shard_map/pallas_call | solution.py:108
  39.1 5.4 %collective-permute-done.12.refs_0_ = bf16[512,512]{1,0:T(8,128)(2,1)S(1)} collective-permute-done((bf16[512,512]{1,0:T(8,128)(2,1)}, bf16[512,512]{1,0:T(8,128)(2,1)S(1)}, u32[]{:S(2)}, u32[]{:S(2)}) %collective-permute-start.12) | collective-permute-done | bytes 524320 | tf_op jit(solution)/shard_map/ppermute | solution.py:12
  47.5 2.1 %shard_map.85 = bf16[832,512]{1,0:T(8,128)(2,1)S(1)} custom-call(bf16[832,2048]{1,0:T(8,128)(2,1)S(1)} %get-tuple-element.208.x, bf16[512,512]{1,0:T(8,128)(2,1)S(1)} %constant_dynamic-update-slice_fusion.refs_0_, bf16[512,512]{1,0:T(8,128)(2,1)S(1)} %collective-permute-done.14.refs_1_, bf16[512,512]{1,0:T(8,128)(2,1)S(1)} %collective-permute-done.17.refs_2_, ...), custom_call_target="tpu_custom_call" | custom-call | tf_op jit(solution)/shard_map/pallas_call | solution.py:193
  49.9 9.0 %collective-permute-done.13.refs_1_ = bf16[512,512]{1,0:T(8,128)(2,1)S(1)} collective-permute-done((bf16[512,512]{1,0:T(8,128)(2,1)S(1)}, bf16[512,512]{1,0:T(8,128)(2,1)S(1)}, u32[]{:S(2)}, u32[]{:S(2)}) %collective-permute-start.13) | collective-permute-done | bytes 524320 | tf_op jit(solution)/shard_map/ppermute | solution.py:12
  61.8 8.4 %collective-permute-done.20.refs_1_ = bf16[512,512]{1,0:T(8,128)(2,1)S(1)} collective-permute-done((bf16[512,512]{1,0:T(8,128)(2,1)S(1)}, bf16[512,512]{1,0:T(8,128)(2,1)S(1)}, u32[]{:S(2)}, u32[]{:S(2)}) %collective-permute-start.20) | collective-permute-done | bytes 524320 | tf_op jit(solution)/shard_map/ppermute | solution.py:12
  71.4 2.1 %shard_map.87.refs_0_ = f32[832,512]{1,0:T(8,128)S(1)} custom-call(bf16[832,2048]{1,0:T(8,128)(2,1)S(1)} %get-tuple-element.208.x, bf16[512,512]{1,0:T(8,128)(2,1)S(1)} %collective-permute-done.12.refs_0_, bf16[512,512]{1,0:T(8,128)(2,1)S(1)} %collective-permute-done.13.refs_1_, bf16[512,512]{1,0:T(8,128)(2,1)S(1)} %collective-permute-done.19.refs_2_, ...), custom_call_target="tpu_custom_call" | custom-call | tf_op jit(solution)/shard_map/pallas_call | solution.py:193
  74.6 2.9 %shard_map.89 = bf16[832,512]{1,0:T(8,128)(2,1)} custom-call(bf16[832,2048]{1,0:T(8,128)(2,1)S(1)} %get-tuple-element.208.x, bf16[512,512]{1,0:T(8,128)(2,1)S(1)} %collective-permute-done.15.refs_0_, bf16[512,512]{1,0:T(8,128)(2,1)S(1)} %collective-permute-done.20.refs_1_, bf16[512,512]{1,0:T(8,128)(2,1)S(1)} %collective-permute-done.28.refs_2_, ...), custom_call_target="tpu_custom_call" | custom-call | tf_op jit(solution)/shard_map/pallas_call | solution.py:193
  80.5 2.0 %collective-permute-done.26.refs_4_ = bf16[2,2048,128]{2,1,0:T(8,128)(2,1)} collective-permute-done((bf16[2,2048,128]{2,1,0:T(8,128)(2,1)}, bf16[2,2048,128]{2,1,0:T(8,128)(2,1)}, u32[]{:S(2)}, u32[]{:S(2)}) %collective-permute-start.26) | collective-permute-done | bytes 1048608 | tf_op jit(solution)/shard_map/ppermute | solution.py:12
  82.5 6.7 %shard_map.90 = bf16[8,256,512]{2,1,0:T(8,128)(2,1)} custom-call(s32[8]{0:T(128)} %iota_add_fusion.at, bf16[8192,2,256]{2,1,0:T(2,128)(2,1)} %refs_0_.2), custom_call_target="tpu_custom_call" | custom-call | tf_op jit(solution)/shard_map/pallas_call | solution.py:78
  89.3 4.5 %collective-permute-done.30.refs_5_ = bf16[1,2048,128]{2,1,0:T(8,128)(2,1)} collective-permute-done((bf16[1,2048,128]{2,1,0:T(8,128)(2,1)}, bf16[1,2048,128]{2,1,0:T(8,128)(2,1)}, u32[]{:S(2)}, u32[]{:S(2)}) %collective-permute-start.30) | collective-permute-done | bytes 524320 | tf_op jit(solution)/shard_map/ppermute | solution.py:12
  95.0 4.8 %shard_map.91 = (bf16[1024,128]{1,0:T(8,128)(2,1)S(1)}, bf16[1024,128]{1,0:T(8,128)(2,1)S(1)}) custom-call(s32[16]{0:T(128)S(1)} %get-tuple-element.245.kind, s32[16]{0:T(128)S(1)} %get-tuple-element.234.places, bf16[1024,2048]{1,0:T(8,128)(2,1)} %refs_0_.3, bf16[1024,2048]{1,0:T(8,128)(2,1)} %collective-permute-done.22.refs_1_, ...), custom_call_target="tpu_custom_call" | custom-call | tf_op jit(solution)/shard_map/pallas_call | solution.py:239
  99.8 2.2 %collective-permute-start.31 = (bf16[1024,128]{1,0:T(8,128)(2,1)S(1)}, bf16[1024,128]{1,0:T(8,128)(2,1)S(1)}, u32[]{:S(2)}, u32[]{:S(2)}) collective-permute-start(bf16[1024,128]{1,0:T(8,128)(2,1)S(1)} %get-tuple-element.220), channel_id=1, source_target_pairs={{0,4},{4,0},{8,12},{12,8},{1,5},{5,1},{9,13},{13,9},{2,6},{6,2},{1... | collective-permute-start | bytes 786440 | tf_op jit(solution)/shard_map/ppermute | solution.py:12
  101.9 2.0 %collective-permute-start.29 = (bf16[5,2,64,256]{3,2,1,0:T(8,128)(2,1)S(1)}, bf16[5,2,64,256]{3,2,1,0:T(8,128)(2,1)}, u32[]{:S(2)}, u32[]{:S(2)}) collective-permute-start(bf16[5,2,64,256]{3,2,1,0:T(8,128)(2,1)S(1)} %copy-done.8), channel_id=1, source_target_pairs={{0,8},{4,12},{8,0},{12,4},{1,9},{5,13},{9,1},{13,5},{2,10},{6,14},... | collective-permute-start | bytes 983048 | tf_op jit(solution)/shard_map/ppermute | solution.py:12
  104.2 7.9 %collective-permute-done.29.refs_7_ = bf16[5,2,64,256]{3,2,1,0:T(8,128)(2,1)} collective-permute-done((bf16[5,2,64,256]{3,2,1,0:T(8,128)(2,1)S(1)}, bf16[5,2,64,256]{3,2,1,0:T(8,128)(2,1)}, u32[]{:S(2)}, u32[]{:S(2)}) %collective-permute-start.29) | collective-permute-done | bytes 327712 | tf_op jit(solution)/shard_map/ppermute | solution.py:12
  112.7 2.0 %collective-permute-done.25.refs_2_ = bf16[832,512]{1,0:T(8,128)(2,1)} collective-permute-done((bf16[832,512]{1,0:T(8,128)(2,1)}, bf16[832,512]{1,0:T(8,128)(2,1)}, u32[]{:S(2)}, u32[]{:S(2)}) %collective-permute-start.25) | collective-permute-done | bytes 852000 | tf_op jit(solution)/shard_map/ppermute | solution.py:12
  115.6 5.5 %collective-permute-done.33.refs_3_ = bf16[1024,128]{1,0:T(8,128)(2,1)S(1)} collective-permute-done((bf16[1024,128]{1,0:T(8,128)(2,1)S(1)}, bf16[1024,128]{1,0:T(8,128)(2,1)S(1)}, u32[]{:S(2)}, u32[]{:S(2)}) %collective-permute-start.33) | collective-permute-done | bytes 262176 | tf_op jit(solution)/shard_map/ppermute | solution.py:12
  123.5 5.7 %shard_map.92.refs_0_ = f32[1152,512]{1,0:T(8,128)S(1)} custom-call(bf16[832,2048]{1,0:T(8,128)(2,1)S(1)} %get-tuple-element.228.x, bf16[2048,512]{1,0:T(8,128)(2,1)} %bitcast.43, bf16[832,512]{1,0:T(8,128)(2,1)} %collective-permute-done.32.refs_1_, bf16[832,512]{1,0:T(8,128)(2,1)} %collective-permute-done.25.refs_2_), custom_call_target="tpu_custom_call" | custom-call | tf_op jit(solution)/shard_map/pallas_call | solution.py:193
  129.2 7.5 %collective-permute-done.34.refs_4_ = bf16[1024,128]{1,0:T(8,128)(2,1)} collective-permute-done((bf16[1024,128]{1,0:T(8,128)(2,1)}, bf16[1024,128]{1,0:T(8,128)(2,1)}, u32[]{:S(2)}, u32[]{:S(2)}) %collective-permute-start.34) | collective-permute-done | bytes 262176 | tf_op jit(solution)/shard_map/ppermute | solution.py:12
  136.8 4.9 %shard_map.93 = bf16[1024,2,256]{2,1,0:T(2,128)(2,1)} custom-call(s32[8]{0:T(128)S(1)} %get-tuple-element.250.offsets, s32[8]{0:T(128)S(1)} %copy-done.6, s32[8]{0:T(128)S(1)} %bitcast.40, s32[8]{0:T(128)S(1)} %bitcast.41, f32[1152,512]{1,0:T(8,128)S(1)} %shard_map.92.refs_0_, f32[192,512]{1,0:T(8,128)S(1)} %copy-done.39, bf16[1024,128]{1,0:T(8,128)(2,1)S(1)} %copy-done.1, ...), custom_call_target="tpu_custom_call" | custom-call | tf_op jit(solution)/shard_map/pallas_call | solution.py:333
  (145 shorter events, 28.9 us)
Async XLA Ops:
  0.0 24.9 %collective-permute-start.21 = (bf16[16,2048,128]{2,1,0:T(8,128)(2,1)}, bf16[16,2048,128]{2,1,0:T(8,128)(2,1)}, u32[]{:S(2)}, u32[]{:S(2)}) collective-permute-start(bf16[16,2048,128]{2,1,0:T(8,128)(2,1)} %refs_2_.1), channel_id=1, source_target_pairs={{0,4},{4,0},{8,12},{12,8},{1,5},{5,1},{9,13},{13,9},{2,6},{6,2},{1... | collective-permute-start | bytes 25165832 | tf_op jit(solution)/shard_map/ppermute | solution.py:12
  0.7 24.3 %collective-permute-start.22 = (bf16[1024,2048]{1,0:T(8,128)(2,1)}, bf16[1024,2048]{1,0:T(8,128)(2,1)}, u32[]{:S(2)}, u32[]{:S(2)}) collective-permute-start(bf16[1024,2048]{1,0:T(8,128)(2,1)} %refs_0_.3), channel_id=1, source_target_pairs={{0,4},{4,0},{8,12},{12,8},{1,5},{5,1},{9,13},{13,9},{2,6},{6,2},{1... | collective-permute-start | bytes 12582920 | tf_op jit(solution)/shard_map/ppermute | solution.py:12
  0.7 16.2 %collective-permute-start.10 = (bf16[16,2,64,256]{3,2,1,0:T(8,128)(2,1)}, bf16[16,2,64,256]{3,2,1,0:T(8,128)(2,1)S(1)}, u32[]{:S(2)}, u32[]{:S(2)}) collective-permute-start(bf16[16,2,64,256]{3,2,1,0:T(8,128)(2,1)} %refs_5_.1), channel_id=1, source_target_pairs={{0,4},{4,0},{8,12},{12,8},{1,5},{5,1},{9,13},{13,9},{2,6},{6,2},{1... | collective-permute-start | bytes 3145736 | tf_op jit(solution)/shard_map/ppermute | solution.py:12
  2.4 14.5 %collective-permute-start.9 = (bf16[256,512]{1,0:T(8,128)(2,1)S(1)}, bf16[256,512]{1,0:T(8,128)(2,1)S(1)}, u32[]{:S(2)}, u32[]{:S(2)}) collective-permute-start(bf16[256,512]{1,0:T(8,128)(2,1)S(1)} %bitcast.46), channel_id=1, source_target_pairs={{0,3},{1,2},{2,1},{3,0},{4,7},{5,6},{6,5},{7,4},{8,11},{9,10},{10,... | collective-permute-start | bytes 786440 | tf_op jit(solution)/shard_map/ppermute | solution.py:12
  16.9 7.7 %collective-permute-start.11 = (bf16[256,512]{1,0:T(8,128)(2,1)S(1)}, bf16[256,512]{1,0:T(8,128)(2,1)S(1)}, u32[]{:S(2)}, u32[]{:S(2)}) collective-permute-start(bf16[256,512]{1,0:T(8,128)(2,1)S(1)} %collective-permute-done.9), channel_id=1, source_target_pairs={{0,8},{4,12},{8,0},{12,4},{1,9},{5,13},{9,1},{13,5},{2,10},{6,14},... | collective-permute-start | bytes 786440 | tf_op jit(solution)/shard_map/ppermute | solution.py:12
  18.3 26.2 %collective-permute-start.12 = (bf16[512,512]{1,0:T(8,128)(2,1)}, bf16[512,512]{1,0:T(8,128)(2,1)S(1)}, u32[]{:S(2)}, u32[]{:S(2)}) collective-permute-start(bf16[512,512]{1,0:T(8,128)(2,1)} %bitcast.9), channel_id=1, source_target_pairs={{0,2},{1,3},{2,0},{3,1},{4,6},{5,7},{6,4},{7,5},{8,10},{9,11},{10,... | collective-permute-start | bytes 1572872 | tf_op jit(solution)/shard_map/ppermute | solution.py:12
  19.6 24.9 %collective-permute-start.15 = (bf16[512,512]{1,0:T(8,128)(2,1)}, bf16[512,512]{1,0:T(8,128)(2,1)S(1)}, u32[]{:S(2)}, u32[]{:S(2)}) collective-permute-start(bf16[512,512]{1,0:T(8,128)(2,1)} %bitcast.45), channel_id=1, source_target_pairs={{0,1},{1,0},{2,3},{3,2},{4,5},{5,4},{6,7},{7,6},{8,9},{9,8},{10,11... | collective-permute-start | bytes 1572872 | tf_op jit(solution)/shard_map/ppermute | solution.py:12
  24.6 19.9 %collective-permute-start.14 = (bf16[512,512]{1,0:T(8,128)(2,1)S(1)}, bf16[512,512]{1,0:T(8,128)(2,1)S(1)}, u32[]{:S(2)}, u32[]{:S(2)}) collective-permute-start(bf16[512,512]{1,0:T(8,128)(2,1)S(1)} %constant_dynamic-update-slice_fusion.refs_0_), channel_id=1, source_target_pairs={{0,16},{16,0},{1,17},{17,1},{2,18},{18,2},{3,19},{19,3},{4,20},{20... | collective-permute-start | bytes 1572872 | tf_op jit(solution)/shard_map/ppermute | solution.py:12
  29.0 30.2 %collective-permute-start.23 = (bf16[2,2048,128]{2,1,0:T(8,128)(2,1)S(1)}, bf16[2,2048,128]{2,1,0:T(8,128)(2,1)S(1)}, u32[]{:S(2)}, u32[]{:S(2)}) collective-permute-start(bf16[2,2048,128]{2,1,0:T(8,128)(2,1)S(1)} %get-tuple-element.196), channel_id=1, source_target_pairs={{0,8},{4,12},{8,0},{12,4},{1,9},{5,13},{9,1},{13,5},{2,10},{6,14},... | collective-permute-start | bytes 3145736 | tf_op jit(solution)/shard_map/ppermute | solution.py:12
  30.3 16.5 %collective-permute-start.17 = (bf16[512,512]{1,0:T(8,128)(2,1)S(1)}, bf16[512,512]{1,0:T(8,128)(2,1)S(1)}, u32[]{:S(2)}, u32[]{:S(2)}) collective-permute-start(bf16[512,512]{1,0:T(8,128)(2,1)S(1)} %constant_dynamic-update-slice_fusion.refs_0_), channel_id=1, source_target_pairs={{0,4},{4,0},{8,12},{12,8},{1,5},{5,1},{9,13},{13,9},{2,6},{6,2},{1... | collective-permute-start | bytes 1572872 | tf_op jit(solution)/shard_map/ppermute | solution.py:12
  45.4 13.5 %collective-permute-start.13 = (bf16[512,512]{1,0:T(8,128)(2,1)S(1)}, bf16[512,512]{1,0:T(8,128)(2,1)S(1)}, u32[]{:S(2)}, u32[]{:S(2)}) collective-permute-start(bf16[512,512]{1,0:T(8,128)(2,1)S(1)} %collective-permute-done.12.refs_0_), channel_id=1, source_target_pairs={{0,16},{16,0},{1,17},{17,1},{2,18},{18,2},{3,19},{19,3},{4,20},{20... | collective-permute-start | bytes 1572872 | tf_op jit(solution)/shard_map/ppermute | solution.py:12
  45.6 24.6 %collective-permute-start.20 = (bf16[512,512]{1,0:T(8,128)(2,1)S(1)}, bf16[512,512]{1,0:T(8,128)(2,1)S(1)}, u32[]{:S(2)}, u32[]{:S(2)}) collective-permute-start(bf16[512,512]{1,0:T(8,128)(2,1)S(1)} %collective-permute-done.15.refs_0_), channel_id=1, source_target_pairs={{0,16},{16,0},{1,17},{17,1},{2,18},{18,2},{3,19},{19,3},{4,20},{20... | collective-permute-start | bytes 1572872 | tf_op jit(solution)/shard_map/ppermute | solution.py:12
  46.8 24.1 %collective-permute-start.19 = (bf16[512,512]{1,0:T(8,128)(2,1)S(1)}, bf16[512,512]{1,0:T(8,128)(2,1)S(1)}, u32[]{:S(2)}, u32[]{:S(2)}) collective-permute-start(bf16[512,512]{1,0:T(8,128)(2,1)S(1)} %collective-permute-done.12.refs_0_), channel_id=1, source_target_pairs={{0,4},{4,0},{8,12},{12,8},{1,5},{5,1},{9,13},{13,9},{2,6},{6,2},{1... | collective-permute-start | bytes 1572872 | tf_op jit(solution)/shard_map/ppermute | solution.py:12
  49.6 23.9 %collective-permute-start.24 = (bf16[832,512]{1,0:T(8,128)(2,1)S(1)}, bf16[832,512]{1,0:T(8,128)(2,1)S(1)}, u32[]{:S(2)}, u32[]{:S(2)}) collective-permute-start(bf16[832,512]{1,0:T(8,128)(2,1)S(1)} %shard_map.85), channel_id=1, source_target_pairs={{0,1},{1,0},{2,3},{3,2},{4,5},{5,4},{6,7},{7,6},{8,9},{9,8},{10,11... | collective-permute-start | bytes 2555912 | tf_op jit(solution)/shard_map/ppermute | solution.py:12
  58.9 23.7 %collective-permute-start.26 = (bf16[2,2048,128]{2,1,0:T(8,128)(2,1)}, bf16[2,2048,128]{2,1,0:T(8,128)(2,1)}, u32[]{:S(2)}, u32[]{:S(2)}) collective-permute-start(bf16[2,2048,128]{2,1,0:T(8,128)(2,1)} %get-tuple-element.205), channel_id=1, source_target_pairs={{0,8},{4,12},{8,0},{12,4},{1,9},{5,13},{9,1},{13,5},{2,10},{6,14},... | collective-permute-start | bytes 3145736 | tf_op jit(solution)/shard_map/ppermute | solution.py:12
  60.2 10.8 %collective-permute-start.18 = (bf16[512,512]{1,0:T(8,128)(2,1)S(1)}, bf16[512,512]{1,0:T(8,128)(2,1)S(1)}, u32[]{:S(2)}, u32[]{:S(2)}) collective-permute-start(bf16[512,512]{1,0:T(8,128)(2,1)S(1)} %collective-permute-done.13.refs_1_), channel_id=1, source_target_pairs={{0,4},{4,0},{8,12},{12,8},{1,5},{5,1},{9,13},{13,9},{2,6},{6,2},{1... | collective-permute-start | bytes 1572872 | tf_op jit(solution)/shard_map/ppermute | solution.py:12
  70.2 4.4 %collective-permute-start.28 = (bf16[512,512]{1,0:T(8,128)(2,1)S(1)}, bf16[512,512]{1,0:T(8,128)(2,1)S(1)}, u32[]{:S(2)}, u32[]{:S(2)}) collective-permute-start(bf16[512,512]{1,0:T(8,128)(2,1)S(1)} %collective-permute-done.15.refs_0_), channel_id=1, source_target_pairs={{0,4},{4,0},{8,12},{12,8},{1,5},{5,1},{9,13},{13,9},{2,6},{6,2},{1... | collective-permute-start | bytes 1572872 | tf_op jit(solution)/shard_map/ppermute | solution.py:12
  71.0 22.7 %collective-permute-start.30 = (bf16[1,2048,128]{2,1,0:T(8,128)(2,1)}, bf16[1,2048,128]{2,1,0:T(8,128)(2,1)}, u32[]{:S(2)}, u32[]{:S(2)}) collective-permute-start(bf16[1,2048,128]{2,1,0:T(8,128)(2,1)} %get-tuple-element.212), channel_id=1, source_target_pairs={{0,8},{4,12},{8,0},{12,4},{1,9},{5,13},{9,1},{13,5},{2,10},{6,14},... | collective-permute-start | bytes 1572872 | tf_op jit(solution)/shard_map/ppermute | solution.py:12
  74.6 40.2 %collective-permute-start.25 = (bf16[832,512]{1,0:T(8,128)(2,1)}, bf16[832,512]{1,0:T(8,128)(2,1)}, u32[]{:S(2)}, u32[]{:S(2)}) collective-permute-start(bf16[832,512]{1,0:T(8,128)(2,1)} %shard_map.88), channel_id=1, source_target_pairs={{0,2},{1,3},{2,0},{3,1},{4,6},{5,7},{6,4},{7,5},{8,10},{9,11},{10,... | collective-permute-start | bytes 2555912 | tf_op jit(solution)/shard_map/ppermute | solution.py:12
  77.5 38.0 %collective-permute-start.32 = (bf16[832,512]{1,0:T(8,128)(2,1)}, bf16[832,512]{1,0:T(8,128)(2,1)}, u32[]{:S(2)}, u32[]{:S(2)}) collective-permute-start(bf16[832,512]{1,0:T(8,128)(2,1)} %shard_map.89), channel_id=1, source_target_pairs={{0,1},{1,0},{2,3},{3,2},{4,5},{5,4},{6,7},{7,6},{8,9},{9,8},{10,11... | collective-permute-start | bytes 2555912 | tf_op jit(solution)/shard_map/ppermute | solution.py:12
  101.9 10.1 %collective-permute-start.29 = (bf16[5,2,64,256]{3,2,1,0:T(8,128)(2,1)S(1)}, bf16[5,2,64,256]{3,2,1,0:T(8,128)(2,1)}, u32[]{:S(2)}, u32[]{:S(2)}) collective-permute-start(bf16[5,2,64,256]{3,2,1,0:T(8,128)(2,1)S(1)} %copy-done.8), channel_id=1, source_target_pairs={{0,8},{4,12},{8,0},{12,4},{1,9},{5,13},{9,1},{13,5},{2,10},{6,14},... | collective-permute-start | bytes 983048 | tf_op jit(solution)/shard_map/ppermute | solution.py:12
  104.1 17.0 %collective-permute-start.33 = (bf16[1024,128]{1,0:T(8,128)(2,1)S(1)}, bf16[1024,128]{1,0:T(8,128)(2,1)S(1)}, u32[]{:S(2)}, u32[]{:S(2)}) collective-permute-start(bf16[1024,128]{1,0:T(8,128)(2,1)S(1)} %add.211.refs_2_), channel_id=1, source_target_pairs={{0,1},{1,0},{2,3},{3,2},{4,5},{5,4},{6,7},{7,6},{8,9},{9,8},{10,11... | collective-permute-start | bytes 786440 | tf_op jit(solution)/shard_map/ppermute | solution.py:12
  112.1 24.6 %collective-permute-start.35 = (bf16[5,2,64,256]{3,2,1,0:T(8,128)(2,1)}, bf16[5,2,64,256]{3,2,1,0:T(8,128)(2,1)}, u32[]{:S(2)}, u32[]{:S(2)}) collective-permute-start(bf16[5,2,64,256]{3,2,1,0:T(8,128)(2,1)} %collective-permute-done.29.refs_7_), channel_id=1, source_target_pairs={{0,4},{4,0},{8,12},{12,8},{1,5},{5,1},{9,13},{13,9},{2,6},{6,2},{1... | collective-permute-start | bytes 983048 | tf_op jit(solution)/shard_map/ppermute | solution.py:12
  122.6 14.1 %collective-permute-start.34 = (bf16[1024,128]{1,0:T(8,128)(2,1)}, bf16[1024,128]{1,0:T(8,128)(2,1)}, u32[]{:S(2)}, u32[]{:S(2)}) collective-permute-start(bf16[1024,128]{1,0:T(8,128)(2,1)} %add_convert_fusion), channel_id=1, source_target_pairs={{0,2},{1,3},{2,0},{3,1},{4,6},{5,7},{6,4},{7,5},{8,10},{9,11},{10,... | collective-permute-start | bytes 786440 | tf_op jit(solution)/shard_map/ppermute | solution.py:12
  (32 other events, 343.1 us)
